TPU v7x, 32 devices: a whole 2x2x4 slice. The times are simulated.
32 devices in a mesh: parts: 2 (over x), store: 16 (over z, y, core).
Axes of the slice: x: 2, y: 2, z: 4, core: 2. Of those that a mesh axis runs over, the one named last changes fastest.
Arguments:
- rows_in: bfloat16 [128, 40, 8192], P(('parts', 'store')), parts along dimension 0, may hold values from -6 to 6
- norm_gain: bfloat16 [8192], replicated, may hold values from 0.099609375 to 1.8984375
- kv_weight: bfloat16 [8192, 1024], P('store'), may hold values from -0.0625 to 0.0625
- queries: bfloat16 [128, 40, 4096], P(('parts', 'store')), parts along dimension 0, may hold values from -8 to 8
- store_pages: bfloat16 [128, 16, 2, 512], P(('parts', 'store')), parts along dimension 0, may hold values from -8 to 8
- passage_home: int32 [128], P('parts'), parts along dimension 0, may hold values from 0 to 63, as said below
- passage_ids: int32 [128, 20], P('parts'), parts along dimension 0, may hold values from 0 to 63, as said below
- passage_count: int32 [128], P(('parts', 'store')), parts along dimension 0, may hold values from 6 to 20
- recompute_rows: int32 [128, 20, 2], P('parts'), parts along dimension 0, may hold values from 0 to 15, as said below
Outputs:
- attended: bfloat16 [128, 40, 4096], P(('parts', 'store')), parts along dimension 0
There are 2 independent parts, one for each index of `parts`. A program takes and returns all parts, laid end to end along the dimension named above; an argument that names none is the same for every part. Nothing has to cross between parts.
Inputs may be any that keep to these rules, and one draw needn't show every extreme that they name: `passage_home`: A permutation. `passage_ids`: over all slots of the 4 requests of one device, at most 5 name passages held in the rows of one device's block of store_pages; some device pair reaches 5. Unused slots name passages too. `recompute_rows`: the 2 rows of one passage slot differ.
All inputs are finite; a program needn't handle non-finite values.
Results may differ from a plain program's by a relative error of at most 0.0055.
Values may be sent and summed in bfloat16 or wider, within the bound.
No kernel may reach another device: no remote copies, remote signals or barrier semaphores. Data moves between devices by JAX's collectives and lax.ppermute only.
A program may use at most 128 MiB of HBM per device.

v0:
```python
import math

import jax
import jax.numpy as jnp
from jax import lax
from jax.sharding import PartitionSpec as P

QUERY_HEADS = 32
KEY_VALUE_HEADS = 4
HEAD_SIZE = 128


def per_device(
    rows_in,
    norm_gain,
    kv_weight,
    queries,
    store_pages,
    passage_home,
    passage_ids,
    passage_count,
    recompute_rows,
):
    shards = lax.axis_size("store")
    me = lax.axis_index("store")
    owned_tokens, selected_rows, width = rows_in.shape
    maxp = passage_ids.shape[1]
    per_pass = recompute_rows.shape[2]
    local_count = store_pages.shape[0]
    plen = store_pages.shape[1]
    kvw = store_pages.shape[3]
    context_length = maxp * plen
    query_group = QUERY_HEADS // KEY_VALUE_HEADS
    scale = 1.0 / math.sqrt(HEAD_SIZE)
    wide = rows_in.astype(jnp.float32)
    normed = (
        wide
        * lax.rsqrt(jnp.mean(wide * wide, axis=-1, keepdims=True) + 1e-05)
        * norm_gain.astype(jnp.float32)
    ).astype(jnp.bfloat16)
    flat = normed.reshape(owned_tokens * selected_rows, width)
    fresh = jnp.dot(
        flat,
        lax.all_gather(kv_weight, "store", axis=0, tiled=True),
        preferred_element_type=jnp.float32,
    ).astype(jnp.bfloat16)
    my_rows = lax.dynamic_slice_in_dim(recompute_rows, me * owned_tokens, owned_tokens, 0)
    onehot = my_rows[..., None] == jnp.arange(plen, dtype=jnp.int32)
    touched = jnp.any(onehot, axis=2)
    slots = passage_home[passage_ids]
    positions = owned_tokens * maxp
    slots_cap = (positions + shards - 1) // shards
    home_shard = (slots // local_count).reshape(shards, positions)
    local_slot = (slots % local_count).reshape(shards, positions)
    earlier = jnp.tril(jnp.ones((positions, positions), jnp.bool_), -1)
    same = home_shard[:, :, None] == home_shard[:, None, :]
    rank = jnp.sum(same & earlier[None], axis=2)
    ladder = jnp.arange(slots_cap, dtype=jnp.int32)
    hit = (home_shard[:, :, None] == me) & (rank[:, :, None] == ladder[None, None, :])
    pick = jnp.sum(jnp.where(hit, local_slot[:, :, None], 0), axis=1)
    outgoing = store_pages[pick.reshape(shards * slots_cap)]
    my_shard = lax.dynamic_slice_in_dim(home_shard, me, 1, 0)[0]
    my_rank = lax.dynamic_slice_in_dim(rank, me, 1, 0)[0]
    arrived = lax.all_to_all(outgoing, "store", split_axis=0, concat_axis=0, tiled=True)
    gathered = arrived[my_shard * slots_cap + my_rank]
    cached = gathered.reshape(owned_tokens, maxp, plen, 2, kvw)
    fresh_rows = fresh.reshape(owned_tokens, maxp, per_pass, 2, kvw)
    placed = jnp.einsum(
        "omij,omick->omjck",
        onehot.astype(jnp.bfloat16),
        fresh_rows,
        preferred_element_type=jnp.float32,
    )
    patched_cache = jnp.where(
        touched[..., None, None], placed.astype(jnp.bfloat16), cached
    ).reshape(owned_tokens, context_length, 2, kvw)
    key_matrix = (
        patched_cache[:, :, 0]
        .reshape(owned_tokens, context_length, KEY_VALUE_HEADS, HEAD_SIZE)
        .transpose(0, 2, 1, 3)
    )
    value_matrix = (
        patched_cache[:, :, 1]
        .reshape(owned_tokens, context_length, KEY_VALUE_HEADS, HEAD_SIZE)
        .transpose(0, 2, 1, 3)
    )
    head_count = queries.reshape(
        owned_tokens, selected_rows, KEY_VALUE_HEADS, query_group, HEAD_SIZE
    ).transpose(0, 2, 1, 3, 4)
    key_pos = jnp.arange(context_length, dtype=jnp.int32)
    key_slot = key_pos // plen
    query_slot = jnp.arange(selected_rows, dtype=jnp.int32) // per_pass

    def attend(items):
        head_rows, key_rows, value_rows, rows, count = items
        query_pos = query_slot * plen + rows.reshape(selected_rows)
        visible = (key_slot[None, :] < count) & (key_pos[None, :] <= query_pos[:, None])

        def one_head(group_items):
            group_rows, group_keys, group_values = group_items
            scores = (
                jnp.einsum(
                    "qgd,kd->gqk", group_rows, group_keys, preferred_element_type=jnp.float32
                )
                * scale
            )
            scores = jnp.where(visible[None], scores, -1e30)
            top = jnp.max(scores, axis=-1, keepdims=True)
            expd = jnp.exp(scores - top)
            weights = (expd / jnp.sum(expd, axis=-1, keepdims=True)).astype(jnp.bfloat16)
            return jnp.einsum(
                "gqk,kd->qgd", weights, group_values, preferred_element_type=jnp.float32
            )

        result = lax.map(one_head, (head_rows, key_rows, value_rows))
        result = result.transpose(1, 0, 2, 3).reshape(selected_rows, QUERY_HEADS * HEAD_SIZE)
        live = query_slot < count
        return jnp.where(live[:, None], result, 0.0).astype(jnp.bfloat16)

    return lax.map(attend, (head_count, key_matrix, value_matrix, my_rows, passage_count))


def solution(mesh):
    in_specs = (
        P(("parts", "store"), None, None),
        P(),
        P("store", None),
        P(("parts", "store"), None, None),
        P(("parts", "store"), None, None, None),
        P("parts"),
        P("parts", None),
        P(("parts", "store")),
        P("parts", None, None),
    )
    out_specs = P(("parts", "store"), None, None)
    return jax.shard_map(
        per_device, mesh=mesh, in_specs=in_specs, out_specs=out_specs, check_vma=False
    )
```

profile of v0, /device:TPU:0, one launch (start us, length us, event | category | flops | bytes accessed | tf_op | source)
XLA Modules:
  0.0 252.8 jit_solution(687904685290852283)
XLA Ops:
  8.2 7.6 %gather_fusion = s32[1280]{0:T(1024)S(1)} fusion(s32[64]{0:T(128)S(1)} %copy-done.1, s32[2048]{0:T(1024)S(1)} %pad_clamp_fusion), kind=kCustom, calls=%fused_computation | custom fusion | bytes 15360 | tf_op jit(solution)/shard_map/gather | solution.py:50
  17.0 9.1 %gather_fusion.1 = bf16[80,16,2,512]{3,2,1,0:T(2,128)(2,1)} fusion(bf16[4,16,2,512]{3,2,1,0:T(2,128)(2,1)S(1)} %copy-done, s32[1024]{0:T(1024)S(1)} %pad_clamp_fusion.2), kind=kCustom, calls=%fused_computation.1 | custom fusion | bytes 5243200 | tf_op jit(solution)/shard_map/gather | solution.py:61
  26.1 7.6 %all-to-all-start = ((bf16[80,16,2,512]{3,2,1,0:T(2,128)(2,1)}), bf16[80,16,2,512]{3,2,1,0:T(2,128)(2,1)}, u32[]{:S(2)}, u32[]{:S(2)}) async-start(bf16[80,16,2,512]{3,2,1,0:T(2,128)(2,1)} %gather_fusion.1), calls=%async_computation | async-start | bytes 5242880 | tf_op jit(solution)/shard_map/all_to_all | solution.py:64
  34.1 3.0 %copy.38 = bf16[20,8,32,128]{3,2,1,0:T(8,128)(2,1)} copy(bf16[20,8,32,128]{3,1,2,0:T(8,128)(2,1)} %bitcast.135) | data formatting | bytes 2621440
  37.9 2.2 fusion.59
  40.1 65.5 %all-to-all-done = bf16[80,16,2,512]{3,2,1,0:T(2,128)(2,1)} async-done(((bf16[80,16,2,512]{3,2,1,0:T(2,128)(2,1)}), bf16[80,16,2,512]{3,2,1,0:T(2,128)(2,1)}, u32[]{:S(2)}, u32[]{:S(2)}) %all-to-all-start) | async-done | bytes 2621472 | tf_op jit(solution)/shard_map/all_to_all | solution.py:64
  105.7 10.8 %gather_fusion.2 = bf16[80,16,2,512]{3,2,1,0:T(2,128)(2,1)S(1)} fusion(bf16[80,16,2,512]{3,2,1,0:T(2,128)(2,1)} %all-to-all-done, s32[1024]{0:T(1024)S(1)} %pad_clamp_fusion.1), kind=kCustom, calls=%fused_computation.2 | custom fusion | bytes 5243200 | tf_op jit(solution)/shard_map/gather | solution.py:65
  116.5 2.2 copy.28
  118.7 66.5 %all-gather.2.cloned.1.call-done = bf16[8192,1024]{1,0:T(8,128)(2,1)} async-done(((bf16[512,1024]{1,0:T(8,128)(2,1)}), bf16[8192,1024]{1,0:T(8,128)(2,1)}) %all-gather.2.cloned.1.call-update) | async-done | bytes 16777232 | tf_op jit(solution)/shard_map/all_gather | solution.py:44
  185.2 9.6 %convolution_convert_fusion = bf16[160,1024]{1,0:T(8,128)(2,1)S(1)} fusion(bf16[160,8192]{1,0:T(8,128)(2,1)} %bitcast.133, bf16[8192,1024]{1,0:T(8,128)(2,1)} %all-gather.2.cloned.1.call-done), kind=kOutput, calls=%fused_computation.62 | convolution fusion | flops 2684518400 | bytes 19726336 | tf_op jit(solution)/shard_map/dot_general | solution.py:42
  195.0 2.7 %convert_select_fusion = bf16[4,20,16,2,512]{4,2,3,1,0:T(8,128)(2,1)S(1)} fusion(bf16[4,20,16,2,512]{4,2,3,1,0:T(8,128)(2,1)S(1)} %bitcast.134, pred[4,20,16]{2,1,0:T(8,128)(4,1)S(1)} %fusion.62, bf16[4,20,2,2,512]{4,3,2,1,0:T(2,128)(2,1)S(1)} %reshape.255, s32[4,20,2]{2,1,0:T(8,128)S(1)} %copy.37), kind=kOutput, calls=%fused_computation.61 | convolution fusion | flops 7866880 | bytes 5572480 | tf_op jit(solution)/shard_map/omij,omick->omjck/dot_general | solution.py:68
  198.0 1.2 fusion.77
  199.2 2.7 %reshape_squeeze.7 = bf16[4,320,4,128]{3,2,1,0:T(4,128)(2,1)S(1)} reshape(bf16[4,320,1,512]{3,1,2,0:T(8,128)(2,1)} %get-tuple-element.206) | data formatting | bytes 2621440 | tf_op jit(solution)/shard_map/reshape;squeeze | solution.py:84
  201.9 1.2 reshape_squeeze.6
  203.2 42.8 %while.26 = (s32[]{:T(128)}, bf16[4,40,4096]{2,1,0:T(8,128)(2,1)}, s32[4]{0:T(128)S(1)}, bf16[4,4,40,8,128]{4,3,1,2,0:T(8,128)(2,1)}, bf16[4,4,320,128]{3,1,2,0:...) while((s32[]{:T(128)}, bf16[4,40,4096]{2,1,0:T(8,128)(2,1)}, ...), condition=%wide.region_9.10_spmd.clone.clone, body=%wide.region_4.9_spmd.clone.clone.sunk | while | flops 79758840 | bytes 6528866 | solution.py:120
  203.2 1.2 constant_dynamic-slice_fusion.10
  205.7 1.0 constant_dynamic-slice_fusion.11
  207.0 5.1 %while.27 = (s32[]{:T(128)}, bf16[4,40,8,128]{3,1,2,0:T(8,128)(2,1)S(1)}, bf16[4,320,128]{2,1,0:T(8,128)(2,1)S(1)}, bf16[4,320,128]{2,1,0:T(8,128)(2,1)S(1)}, bf...) while((s32[]{:T(128)}, ...), condition=%wide.region_8.8_spmd.clone, body=%wide.region_5.7_spmd.clone.sunk | while | flops 79591360 | bytes 627261 | solution.py:115
  210.1 0.7 fusion.99
  213.0 0.9 fusion.92
  213.9 1.2 constant_dynamic-slice_fusion.10
  216.4 1.0 constant_dynamic-slice_fusion.11
  217.7 5.1 %while.27 = (s32[]{:T(128)}, bf16[4,40,8,128]{3,1,2,0:T(8,128)(2,1)S(1)}, bf16[4,320,128]{2,1,0:T(8,128)(2,1)S(1)}, bf16[4,320,128]{2,1,0:T(8,128)(2,1)S(1)}, bf...) while((s32[]{:T(128)}, ...), condition=%wide.region_8.8_spmd.clone, body=%wide.region_5.7_spmd.clone.sunk | while | flops 79591360 | bytes 627261 | solution.py:115
  223.7 0.9 fusion.92
  224.6 1.2 constant_dynamic-slice_fusion.10
  227.1 1.0 constant_dynamic-slice_fusion.11
  228.4 5.1 %while.27 = (s32[]{:T(128)}, bf16[4,40,8,128]{3,1,2,0:T(8,128)(2,1)S(1)}, bf16[4,320,128]{2,1,0:T(8,128)(2,1)S(1)}, bf16[4,320,128]{2,1,0:T(8,128)(2,1)S(1)}, bf...) while((s32[]{:T(128)}, ...), condition=%wide.region_8.8_spmd.clone, body=%wide.region_5.7_spmd.clone.sunk | while | flops 79591360 | bytes 627261 | solution.py:115
  234.4 0.9 fusion.92
  235.3 1.2 constant_dynamic-slice_fusion.10
  237.8 1.0 constant_dynamic-slice_fusion.11
  239.1 5.1 %while.27 = (s32[]{:T(128)}, bf16[4,40,8,128]{3,1,2,0:T(8,128)(2,1)S(1)}, bf16[4,320,128]{2,1,0:T(8,128)(2,1)S(1)}, bf16[4,320,128]{2,1,0:T(8,128)(2,1)S(1)}, bf...) while((s32[]{:T(128)}, ...), condition=%wide.region_8.8_spmd.clone, body=%wide.region_5.7_spmd.clone.sunk | while | flops 79591360 | bytes 627261 | solution.py:115
  245.1 0.9 fusion.92
  (141 shorter events, 33.5 us)
Async XLA Ops:
  6.5 10.4 %copy-start = (bf16[4,16,2,512]{3,2,1,0:T(2,128)(2,1)S(1)}, bf16[4,16,2,512]{3,2,1,0:T(2,128)(2,1)}, u32[]{:S(2)}) copy-start(bf16[4,16,2,512]{3,2,1,0:T(2,128)(2,1)} %param.17) | copy-start | bytes 393220
  6.5 1.7 copy-start.1
  6.5 178.6 %all-gather.2.cloned.1.call-start = ((), (), s32[]{:S(2)}) async-start(), calls=%async_computation.1 | async-start | bytes 17825792 | tf_op jit(solution)/shard_map/all_gather | solution.py:44
  26.1 7.6 %copy-start.4 = (s32[64,20,2]{0,2,1:T(2,128)S(1)}, s32[64,20,2]{0,2,1:T(2,128)}, u32[]{:S(2)}) copy-start(s32[64,20,2]{0,2,1:T(2,128)} %param.21) | copy-start | bytes 30724
  26.1 8.0 %copy-start.5 = (bf16[8192]{0:T(1024)(128)(2,1)S(1)}, bf16[8192]{0:T(1024)(128)(2,1)}, u32[]{:S(2)}) copy-start(bf16[8192]{0:T(1024)(128)(2,1)} %param.14) | copy-start | bytes 49156
  26.1 79.6 %all-to-all-start = ((bf16[80,16,2,512]{3,2,1,0:T(2,128)(2,1)}), bf16[80,16,2,512]{3,2,1,0:T(2,128)(2,1)}, u32[]{:S(2)}, u32[]{:S(2)}) async-start(bf16[80,16,2,512]{3,2,1,0:T(2,128)(2,1)} %gather_fusion.1), calls=%async_computation | async-start | bytes 5242880 | tf_op jit(solution)/shard_map/all_to_all | solution.py:64
  33.7 3.6 %copy-start.2 = (bf16[4,40,8192]{2,1,0:T(8,128)(2,1)S(1)}, bf16[4,40,8192]{2,1,0:T(8,128)(2,1)}, u32[]{:S(2)}) copy-start(bf16[4,40,8192]{2,1,0:T(8,128)(2,1)} %param.13) | copy-start | bytes 7864324
  185.2 9.8 %copy-start.3 = (bf16[80,16,2,512]{3,1,2,0:T(8,128)(2,1)S(1)}, bf16[80,16,2,512]{3,1,2,0:T(8,128)(2,1)}, u32[]{:S(2)}) copy-start(bf16[80,16,2,512]{3,1,2,0:T(8,128)(2,1)} %copy.28) | copy-start | bytes 7864324
  199.2 3.9 %copy-start.6 = (s32[4]{0:T(128)S(1)}, s32[4]{0:T(128)}, u32[]{:S(2)}) copy-start(s32[4]{0:T(128)} %param.20) | copy-start | bytes 52
Sparse Core Ops, SparseCore 0:
  9.5 175.6 all-gather.1
where the time goes:
time: 254 us; the launch traced here: 253 us
  waiting for transfers between devices  133 us (52%)
  local copies, waits for them, and re-layouts  52.6 us (21%)
  matrix products  31.1 us (12%)
  other arithmetic  14.5 us (6%)
  between operations  13.6 us (5%)
  starting transfers between devices  7.57 us (3%)
    all_gather x1, waiting for transfers between devices, per_device(): lax.all_gather(kv_weight, 'store', axis=0, tiled=True)  66.5 us
    all_to_all x1, waiting for transfers between devices, per_device(): lax.all_to_all(outgoing, 'store', split_axis=0, concat_axis=0, tiled=True)  65.5 us
    gather x2, local copies, waits for them, and re-layouts, per_device(): gathered = arrived[my_shard * slots_cap + my_rank]  13 us
    dynamic_slice x28, local copies, waits for them, and re-layouts, per_device(): lax.map(attend, (head_count, key_matrix, value_matrix, my_rows, passage_c...  12.2 us
    dot_general x16, matrix products, one_head(): jnp.einsum('gqk,kd->qgd', weights, group_values, preferred_element_type=j...  11.8 us
    dot_general x1, matrix products, per_device(): jnp.dot(flat, lax.all_gather(kv_weight, 'store', axis=0, tiled=True), pre...  9.58 us
    gather x1, local copies, waits for them, and re-layouts, per_device(): outgoing = store_pages[pick.reshape(shards * slots_cap)]  9.1 us
    gather x2, local copies, waits for them, and re-layouts, per_device(): slots = passage_home[passage_ids]  7.7 us
  transfers between devices with their start and end apart: 2, of which 2 were waited for; matrix products, arithmetic and copies ran while one was open for 15% of the time, Pallas kernels for 0%

commit v1 on v0

v1 whole, which is shorter than its diff:
```python
import functools
import math

import jax
import jax.numpy as jnp
from jax import lax
from jax.experimental import pallas as pl
from jax.experimental.pallas import tpu as pltpu
from jax.sharding import PartitionSpec as P

QUERY_HEADS = 32
KEY_VALUE_HEADS = 4
HEAD_SIZE = 128
HEAD_GROUP = QUERY_HEADS // KEY_VALUE_HEADS
GROUP = 4
HIDDEN = -1e30
EXP2_SCALE = math.log2(math.e) / math.sqrt(HEAD_SIZE)
VMEM_LIMIT = 48 * 2**20


def params(**more):
    return pltpu.CompilerParams(vmem_limit_bytes=VMEM_LIMIT, **more)


def whole():
    return pl.BlockSpec(memory_space=pltpu.VMEM)


def smem():
    return pl.BlockSpec(memory_space=pltpu.SMEM)


def send(x, steps):
    shards = lax.axis_size("store")
    pairs = [(i, (i + steps * GROUP) % shards) for i in range(shards)]
    return lax.ppermute(x, "store", pairs)


def flip(x, bits):
    pairs = [(i, i ^ bits) for i in range(lax.axis_size("store"))]
    return lax.ppermute(x, "store", pairs)


def swap(x):
    return lax.ppermute(x, "parts", [(0, 1), (1, 0)])


def norm_kernel(chunk, chunks, offs_ref, rows_ref, gain_ref, o0, o1, o2, o3, held):
    wide = rows_ref[...].astype(jnp.float32)
    inv = lax.rsqrt(jnp.mean(wide * wide, axis=-1, keepdims=True) + 1e-05)
    held[...] = (wide * inv * gain_ref[...].astype(jnp.float32)).astype(jnp.bfloat16)
    for j, out in enumerate((o0, o1, o2, o3)):
        for k in range(chunks):
            at = pl.multiple_of(offs_ref[j * chunks + k] * 128, 128)
            out[:, k * chunk : (k + 1) * chunk] = held[:, pl.ds(at, chunk)]


def norm_rows(rows, gain, offs, chunk):
    count, width = rows.shape
    chunks = width // GROUP // chunk
    block = 32
    out = jax.ShapeDtypeStruct((count, width // GROUP), jnp.bfloat16)
    return pl.pallas_call(
        functools.partial(norm_kernel, chunk, chunks),
        out_shape=[out] * GROUP,
        grid=(count // block,),
        in_specs=[
            smem(),
            pl.BlockSpec((block, width), lambda i: (i, 0)),
            pl.BlockSpec((1, width), lambda i: (0, 0)),
        ],
        out_specs=[pl.BlockSpec((block, width // GROUP), lambda i: (i, 0))] * GROUP,
        scratch_shapes=[pltpu.VMEM((block, width), jnp.bfloat16)],
        compiler_params=params(),
        cost_estimate=pl.CostEstimate(
            flops=6 * count * width, bytes_accessed=4 * count * width, transcendentals=0
        ),
        name="norm",
    )(offs, rows, gain.reshape(1, width))


def dot(a, b):
    return jnp.dot(a, b, preferred_element_type=jnp.float32)


def first_kernel(a0, a1, a2, a3, w0, w1, w2, w3, w4, acc):
    rows = a0.shape[0]
    for j, a in enumerate((a0, a1, a2, a3)):
        total = None
        at = 0
        for w in (w0, w1, w2, w3, w4):
            depth = w.shape[0]
            term = dot(a[:, at : at + depth], w[...])
            total = term if total is None else total + term
            at += depth
        acc[j * rows : (j + 1) * rows, :] = total


def first_part(acts, weights):
    rows, depth = acts[0].shape
    features = weights[0].shape[1]
    block = 256
    used = sum(w.shape[0] for w in weights)
    return pl.pallas_call(
        first_kernel,
        out_shape=jax.ShapeDtypeStruct((GROUP * rows, features), jnp.float32),
        grid=(features // block,),
        in_specs=[pl.BlockSpec((rows, used), lambda i: (0, 0))] * GROUP
        + [pl.BlockSpec((w.shape[0], block), lambda i: (0, i)) for w in weights],
        out_specs=pl.BlockSpec((GROUP * rows, block), lambda i: (0, i)),
        compiler_params=params(),
        cost_estimate=pl.CostEstimate(
            flops=2 * GROUP * rows * used * features,
            bytes_accessed=2 * used * (GROUP * rows + features) + 4 * GROUP * rows * features,
            transcendentals=0,
        ),
        name="first_part",
    )(*acts, *weights)


def second_kernel(a0, a1, a2, a3, w0, w1, w2, w3, acc, keep, send):
    rows = a0.shape[0]
    for j, a in enumerate((a0, a1, a2, a3)):
        total = acc[j * rows : (j + 1) * rows, :]
        at = 0
        for w in (w0, w1, w2, w3):
            depth = w.shape[0]
            total = total + dot(a[:, at : at + depth], w[...])
            at += depth
        place = slice((j // 2) * rows, (j // 2 + 1) * rows)
        if j % 2:
            send[place, :] = total.astype(jnp.bfloat16)
        else:
            keep[place, :] = total


def second_part(acts, weights, acc):
    rows, depth = acts[0].shape
    features = weights[0].shape[1]
    block = 256
    used = sum(w.shape[0] for w in weights)
    last = depth // used - 1
    return pl.pallas_call(
        second_kernel,
        out_shape=[
            jax.ShapeDtypeStruct((2 * rows, features), jnp.float32),
            jax.ShapeDtypeStruct((2 * rows, features), jnp.bfloat16),
        ],
        grid=(features // block,),
        in_specs=[pl.BlockSpec((rows, used), lambda i: (0, last))] * GROUP
        + [pl.BlockSpec((w.shape[0], block), lambda i: (0, i)) for w in weights]
        + [pl.BlockSpec((GROUP * rows, block), lambda i: (0, i))],
        out_specs=[pl.BlockSpec((2 * rows, block), lambda i: (0, i))] * 2,
        compiler_params=params(),
        cost_estimate=pl.CostEstimate(
            flops=2 * GROUP * rows * used * features,
            bytes_accessed=2 * used * (GROUP * rows + features) + 7 * GROUP * rows * features,
            transcendentals=0,
        ),
        name="second_part",
    )(*acts, *weights, acc)


def stacked_queries(q_ref, head):
    parts = []
    for i in range(HEAD_GROUP):
        at = (head * HEAD_GROUP + i) * HEAD_SIZE
        parts.append(q_ref[0, :, at : at + HEAD_SIZE].astype(jnp.float32))
    return jnp.concatenate(parts, axis=0).astype(jnp.bfloat16)


def scores_of(q, keys, bias):
    s = lax.dot_general(q, keys, (((1,), (1,)), ((), ())), preferred_element_type=jnp.float32)
    rows, cols = bias.shape
    s = (s * EXP2_SCALE).reshape(HEAD_GROUP, rows, cols) + bias[None]
    return s.reshape(HEAD_GROUP * rows, cols)


def cached_kernel(
    per_dev, place_ref, home_ref, ids_ref, q_ref, near_ref, far_ref, bias_ref,
    out_ref, stat_ref, pages, context, sems,
):
    r = pl.program_id(0)
    rows = near_ref.shape[0]
    plen = context.shape[0] // ids_ref.shape[1]

    @pl.when(r == 0)
    def _():
        one = pltpu.make_async_copy(near_ref, pages.at[pl.ds(0, rows)], sems.at[0])
        two = pltpu.make_async_copy(far_ref, pages.at[pl.ds(rows, rows)], sems.at[1])
        one.start()
        two.start()
        one.wait()
        two.wait()

    for m in range(ids_ref.shape[1]):
        slot = home_ref[ids_ref[r, m]]
        position = place_ref[slot // per_dev] * per_dev + slot % per_dev
        at = pl.multiple_of(position * plen, plen)
        context[m * plen : (m + 1) * plen, :] = pages[pl.ds(at, plen), :]
    bias = bias_ref[0]
    kvw = KEY_VALUE_HEADS * HEAD_SIZE
    lane = lax.broadcasted_iota(jnp.int32, (HEAD_GROUP * bias.shape[0], HEAD_SIZE), 1)
    for g in range(KEY_VALUE_HEADS):
        q = stacked_queries(q_ref, g)
        keys = context[:, g * HEAD_SIZE : (g + 1) * HEAD_SIZE]
        values = context[:, kvw + g * HEAD_SIZE : kvw + (g + 1) * HEAD_SIZE]
        s = scores_of(q, keys, bias)
        top = jnp.max(s, axis=-1, keepdims=True)
        e = jnp.exp2(s - top)
        total = jnp.sum(e, axis=-1, keepdims=True)
        out_ref[0, g] = dot(e.astype(jnp.bfloat16), values)
        stat_ref[0, g] = jnp.where(lane < HEAD_SIZE // 2, top, total)


def cached_attention(per_dev, place, home, ids, near, far, queries, bias):
    owned, rows, width = queries.shape
    context = bias.shape[2]
    stacked = HEAD_GROUP * rows
    state = jax.ShapeDtypeStruct((owned, KEY_VALUE_HEADS, stacked, HEAD_SIZE), jnp.float32)
    state_spec = pl.BlockSpec((1, KEY_VALUE_HEADS, stacked, HEAD_SIZE), lambda r: (r, 0, 0, 0))
    return pl.pallas_call(
        functools.partial(cached_kernel, per_dev),
        out_shape=[state, state],
        grid=(owned,),
        in_specs=[
            smem(),
            smem(),
            smem(),
            pl.BlockSpec((1, rows, width), lambda r: (r, 0, 0)),
            pl.BlockSpec(memory_space=pl.ANY),
            pl.BlockSpec(memory_space=pl.ANY),
            pl.BlockSpec((1, rows, context), lambda r: (r, 0, 0)),
        ],
        out_specs=[state_spec, state_spec],
        scratch_shapes=[
            pltpu.VMEM((2 * near.shape[0], near.shape[1]), jnp.bfloat16),
            pltpu.VMEM((context, near.shape[1]), jnp.bfloat16),
            pltpu.SemaphoreType.DMA((2,)),
        ],
        compiler_params=params(),
        cost_estimate=pl.CostEstimate(
            flops=4 * owned * rows * width * context,
            bytes_accessed=4 * near.size + 2 * queries.size + 8 * owned * stacked * 4 * HEAD_SIZE,
            transcendentals=owned * rows * QUERY_HEADS * context,
        ),
        name="cached_attention",
    )(place, home, ids, queries, near, far, bias)


def fresh_kernel(maxp, count_ref, q_ref, own_ref, core_ref, y_ref, bias_ref, part_ref, stat_ref, out_ref):
    r = pl.program_id(0)
    fresh = (
        own_ref[0] + core_ref[0].astype(jnp.float32) + y_ref[0].astype(jnp.float32)
    ).astype(jnp.bfloat16)
    bias = bias_ref[0]
    rows = bias.shape[0]
    kvw = KEY_VALUE_HEADS * HEAD_SIZE
    per_pass = rows // maxp
    slot = lax.broadcasted_iota(jnp.int32, (rows, HEAD_SIZE), 0) // per_pass
    live = slot < count_ref[r]
    for g in range(KEY_VALUE_HEADS):
        q = stacked_queries(q_ref, g)
        keys = fresh[:, g * HEAD_SIZE : (g + 1) * HEAD_SIZE]
        values = fresh[:, kvw + g * HEAD_SIZE : kvw + (g + 1) * HEAD_SIZE]
        s = scores_of(q, keys, bias)
        top1 = stat_ref[0, g, :, 0:1]
        sum1 = stat_ref[0, g, :, HEAD_SIZE // 2 : HEAD_SIZE // 2 + 1]
        top = jnp.maximum(top1, jnp.max(s, axis=-1, keepdims=True))
        e = jnp.exp2(s - top)
        keep = jnp.exp2(top1 - top)
        inv = 1.0 / (sum1 * keep + jnp.sum(e, axis=-1, keepdims=True))
        result = (part_ref[0, g] * keep + dot(e.astype(jnp.bfloat16), values)) * inv
        for i in range(HEAD_GROUP):
            at = (g * HEAD_GROUP + i) * HEAD_SIZE
            one = result[i * rows : (i + 1) * rows]
            out_ref[0, :, at : at + HEAD_SIZE] = jnp.where(live, one, 0.0).astype(jnp.bfloat16)


def fresh_attention(maxp, count, queries, own, core, y, bias, part, stat):
    owned, rows, width = queries.shape
    features = own.shape[-1]
    stacked = HEAD_GROUP * rows
    state_spec = pl.BlockSpec((1, KEY_VALUE_HEADS, stacked, HEAD_SIZE), lambda r: (r, 0, 0, 0))
    row_spec = pl.BlockSpec((1, rows, features), lambda r: (r, 0, 0))
    query_spec = pl.BlockSpec((1, rows, width), lambda r: (r, 0, 0))
    return pl.pallas_call(
        functools.partial(fresh_kernel, maxp),
        out_shape=jax.ShapeDtypeStruct(queries.shape, jnp.bfloat16),
        grid=(owned,),
        in_specs=[
            smem(),
            query_spec,
            row_spec,
            row_spec,
            row_spec,
            pl.BlockSpec((1, rows, rows), lambda r: (r, 0, 0)),
            state_spec,
            state_spec,
        ],
        out_specs=query_spec,
        compiler_params=params(),
        cost_estimate=pl.CostEstimate(
            flops=4 * owned * rows * width * rows,
            bytes_accessed=4 * queries.size + 8 * part.size,
            transcendentals=owned * rows * QUERY_HEADS * rows,
        ),
        name="fresh_attention",
    )(count, queries, own, core, y, bias, part, stat)


def masks(rows, count, plen):
    owned, maxp, per_pass = rows.shape
    selected = maxp * per_pass
    touched = jnp.any(rows[..., None] == jnp.arange(plen, dtype=jnp.int32), axis=2)
    touched = touched.reshape(owned, 1, maxp * plen)
    key_pos = jnp.arange(maxp * plen, dtype=jnp.int32)
    slot = jnp.arange(selected, dtype=jnp.int32) // per_pass
    query_pos = slot * plen + rows.reshape(owned, selected)
    seen = (key_pos // plen < count[:, None, None]) & (key_pos <= query_pos[:, :, None])
    cached_bias = jnp.where(seen & ~touched, 0.0, HIDDEN).astype(jnp.float32)
    seen = (slot < count[:, None, None]) & (query_pos[:, None, :] <= query_pos[:, :, None])
    fresh_bias = jnp.where(seen, 0.0, HIDDEN).astype(jnp.float32)
    return cached_bias, fresh_bias


def ring_projection(rows_in, norm_gain, kv_weight):
    shards = lax.axis_size("store")
    me = lax.axis_index("store")
    side = lax.axis_index("parts")
    ring = shards // GROUP
    z, member = me // GROUP, me % GROUP
    owned, selected, width = rows_in.shape
    depth, features = kv_weight.shape
    half = depth // 2

    mine = lax.dynamic_slice_in_dim(kv_weight, side * half, half, 0)
    below = send(mine, 1)
    above = send(mine, -1)
    low = send(below[: half // 2], 1)
    high = send(above[half // 2 :], -1)

    steps = jnp.array([0, 0, -1, -1, 1, 1, 2, 2], jnp.int32)
    blocks = (z + steps) % ring
    halves = jnp.array([0, 1, 0, 1, 0, 1, 0, 1], jnp.int32)
    halves = jnp.where(steps == 0, halves, halves ^ side)
    targets = member ^ jnp.arange(GROUP, dtype=jnp.int32)
    offs = (blocks[None] * GROUP + targets[:, None]) * depth + halves[None] * half
    offs = (offs // 128).reshape(-1)
    flat = rows_in.reshape(owned * selected, width)
    acts = norm_rows(flat, norm_gain, offs, half)
    acts = [acts[0]] + [flip(acts[j], j) for j in (1, 2, 3)]

    acc = first_part(acts, [kv_weight, below, swap(below), above, swap(above)])
    keep, out = second_part(acts, [low, high, swap(low), swap(high)], acc)
    count = owned * selected
    back = flip(out, 1)
    y_out = (keep[count:] + back[count:].astype(jnp.float32)).astype(jnp.bfloat16)
    return keep[:count], back[:count], flip(y_out, 2)


def gathered_projection(rows_in, norm_gain, kv_weight):
    owned, selected, width = rows_in.shape
    wide = rows_in.reshape(owned * selected, width).astype(jnp.float32)
    inv = lax.rsqrt(jnp.mean(wide * wide, axis=-1, keepdims=True) + 1e-05)
    normed = (wide * inv * norm_gain.astype(jnp.float32)).astype(jnp.bfloat16)
    fresh = dot(normed, lax.all_gather(kv_weight, "store", axis=0, tiled=True))
    none = jnp.zeros(fresh.shape, jnp.bfloat16)
    return fresh, none, none


def ring_pages(store_pages, passage_home, passage_ids):
    shards = lax.axis_size("store")
    me = lax.axis_index("store")
    ring = shards // GROUP
    z, member = me // GROUP, me % GROUP
    local, plen, _, kvw = store_pages.shape
    own = store_pages.reshape(local * plen, 2 * kvw)
    mid = local * plen // 2
    below = send(own, 1)
    above = send(own, -1)
    low = send(below[:mid], 1)
    high = send(above[mid:], -1)
    column = jnp.concatenate([own, below, above, low, high], axis=0)
    near = jnp.concatenate([column, flip(column, 2)], axis=0)
    far = flip(near, 1)
    owned = passage_ids.shape[0] // shards
    ids = lax.dynamic_slice_in_dim(passage_ids, me * owned, owned, 0)
    device = jnp.arange(shards, dtype=jnp.int32)
    apart = (device // GROUP - z) % ring
    rank = jnp.where(apart == 0, 0, jnp.where(apart == ring - 1, 1, apart + 1))
    rel = (device % GROUP) ^ member
    place = ((rel % 2) * 2 + rel // 2) * ring + rank
    return place, passage_home, ids, near, far


def sent_pages(store_pages, passage_home, passage_ids):
    shards = lax.axis_size("store")
    me = lax.axis_index("store")
    local, plen, _, kvw = store_pages.shape
    owned = passage_ids.shape[0] // shards
    positions = owned * passage_ids.shape[1]
    cap = (positions + shards - 1) // shards
    slots = passage_home[passage_ids]
    home_shard = (slots // local).reshape(shards, positions)
    local_slot = (slots % local).reshape(shards, positions)
    earlier = jnp.tril(jnp.ones((positions, positions), jnp.bool_), -1)
    same = home_shard[:, :, None] == home_shard[:, None, :]
    rank = jnp.sum(same & earlier[None], axis=2)
    ladder = jnp.arange(cap, dtype=jnp.int32)
    hit = (home_shard[:, :, None] == me) & (rank[:, :, None] == ladder[None, None, :])
    pick = jnp.sum(jnp.where(hit, local_slot[:, :, None], 0), axis=1)
    outgoing = store_pages[pick.reshape(shards * cap)]
    my_shard = lax.dynamic_slice_in_dim(home_shard, me, 1, 0)[0]
    my_rank = lax.dynamic_slice_in_dim(rank, me, 1, 0)[0]
    arrived = lax.all_to_all(outgoing, "store", split_axis=0, concat_axis=0, tiled=True)
    arrived = arrived.reshape(shards * cap * plen, 2 * kvw)
    middle = arrived.shape[0] // 2
    place = jnp.arange(shards * cap, dtype=jnp.int32)
    home = (my_shard * cap + my_rank).astype(jnp.int32)
    ids = jnp.arange(positions, dtype=jnp.int32).reshape(owned, passage_ids.shape[1])
    return place, home, ids, arrived[:middle], arrived[middle:]


def per_device(
    rows_in,
    norm_gain,
    kv_weight,
    queries,
    store_pages,
    passage_home,
    passage_ids,
    passage_count,
    recompute_rows,
):
    shards = lax.axis_size("store")
    me = lax.axis_index("store")
    owned, selected, _ = rows_in.shape
    local, plen = store_pages.shape[:2]
    ringed = shards == 4 * GROUP and lax.axis_size("parts") == 2 and kv_weight.shape[0] % 512 == 0
    if ringed and local % 2 == 0:
        pages = ring_pages(store_pages, passage_home, passage_ids)
        per_dev = local
    else:
        pages = sent_pages(store_pages, passage_home, passage_ids)
        per_dev = 1
    rows = lax.dynamic_slice_in_dim(recompute_rows, me * owned, owned, 0)
    cached_bias, fresh_bias = masks(rows, passage_count, plen)
    part, stat = cached_attention(per_dev, *pages, queries, cached_bias)
    project = ring_projection if ringed else gathered_projection
    terms = project(rows_in, norm_gain, kv_weight)
    terms = [t.reshape(owned, selected, t.shape[1]) for t in terms]
    return fresh_attention(passage_ids.shape[1], passage_count, queries, *terms, fresh_bias, part, stat)


def solution(mesh):
    in_specs = (
        P(("parts", "store"), None, None),
        P(),
        P("store", None),
        P(("parts", "store"), None, None),
        P(("parts", "store"), None, None, None),
        P("parts"),
        P("parts", None),
        P(("parts", "store")),
        P("parts", None, None),
    )
    out_specs = P(("parts", "store"), None, None)
    return jax.shard_map(
        per_device, mesh=mesh, in_specs=in_specs, out_specs=out_specs, check_vma=False
    )
```

time: 254 us -> 116 us (0.46)
  waiting for transfers between devices: 133 us -> 38.6 us
  local copies, waits for them, and re-layouts: 52.6 us -> 19.5 us
  Pallas kernels: 0 us -> 31.8 us
  matrix products: 31.1 us -> 0 us
  starting transfers between devices: 7.57 us -> 22.8 us
  between operations: 13.6 us -> 0.21 us
  other arithmetic: 14.5 us -> 2.2 us
    all_gather x1 -> x0, waiting for transfers between devices: 66.5 us -> none  [per_device(): lax.all_gather(kv_weight, 'store', axis=0, tiled=True)]
    all_to_all x1 -> x0, waiting for transfers between devices: 65.5 us -> none  [per_device(): lax.all_to_all(outgoing, 'store', split_axis=0, concat_axis=0, tiled=True)]
    ppermute x0 -> x19, waiting for transfers between devices: none -> 38.6 us  [the longest x8 21.8 us: send(): return lax.ppermute(x, 'store', pairs)]
    pallas_call x0 -> x5, Pallas kernels: none -> 31.8 us  [the longest x1 9.34 us: cached_attention(): pl.pallas_call(functools.partial(cached_kernel, per_dev), out_shape=[stat...]
    gather x5 -> x0, local copies, waits for them, and re-layouts: 29.8 us -> none  [the longest x2 13 us: per_device(): gathered = arrived[my_shard * slots_cap + my_rank]]
    dot_general x18 -> x0, matrix products: 24 us -> none  [the longest x16 11.8 us: one_head(): jnp.einsum('gqk,kd->qgd', weights, group_values, preferred_element_type=j...]
    ppermute x0 -> x19, starting transfers between devices: none -> 22.8 us  [the longest x8 13.2 us: send(): return lax.ppermute(x, 'store', pairs)]
    dynamic_slice x29 -> x4, local copies, waits for them, and re-layouts: 12.3 us -> 2.15 us  [the longest x1 1.9 us: ring_projection(): mine = lax.dynamic_slice_in_dim(kv_weight, side * half, half, 0)]
  transfers between devices with their start and end apart: 2 -> 19, of which waited for: 2 -> 9; matrix products, arithmetic and copies ran while one was open for 15% -> 12% of each run, Pallas kernels for 0% -> 20%
where the time goes in v1:
time: 116 us; the launch traced here: 115 us
  waiting for transfers between devices  38.6 us (33%)
  Pallas kernels  31.8 us (27%)
  starting transfers between devices  22.8 us (20%)
  local copies, waits for them, and re-layouts  19.5 us (17%)
  other arithmetic  2.2 us (2%)
    ppermute x8, waiting for transfers between devices, send(): return lax.ppermute(x, 'store', pairs)  21.8 us
    ppermute x8, starting transfers between devices, send(): return lax.ppermute(x, 'store', pairs)  13.2 us
    unnamed x28, local copies, waits for them, and re-layouts  10.3 us
    pallas_call x1, Pallas kernels, cached_attention(): pl.pallas_call(functools.partial(cached_kernel, per_dev), out_shape=[stat...  9.34 us
    pallas_call x1, Pallas kernels, fresh_attention(): pl.pallas_call(functools.partial(fresh_kernel, maxp), out_shape=jax.Shape...  9.03 us
    ppermute x7, waiting for transfers between devices, flip(): return lax.ppermute(x, 'store', pairs)  8.64 us
    ppermute x4, waiting for transfers between devices, swap(): return lax.ppermute(x, 'parts', [(0, 1), (1, 0)])  8.17 us
    pallas_call x1, Pallas kernels, first_part(): pl.pallas_call(first_kernel, out_shape=jax.ShapeDtypeStruct((GROUP * rows...  5.43 us
  transfers between devices with their start and end apart: 19, of which 9 were waited for; matrix products, arithmetic and copies ran while one was open for 12% of the time, Pallas kernels for 20%

profile of v1, /device:TPU:0, one launch (start us, length us, event | category | flops | bytes accessed | tf_op | source)
XLA Modules:
  0.0 115.2 jit_solution(5775059594683197649)
XLA Ops:
  0.0 1.9 %constant_dynamic-slice_fusion.2 = bf16[256,1024]{1,0:T(8,128)(2,1)} fusion(bf16[512,1024]{1,0:T(8,128)(2,1)} %w0.1, s32[]{:T(128)S(6)} %select_n.103), kind=kLoop, calls=%fused_computation.57 | loop fusion | bytes 1048580 | tf_op jit(solution)/shard_map/dynamic_slice | solution.py:337
  1.9 3.0 %collective-permute-start.3 = (bf16[256,1024]{1,0:T(8,128)(2,1)}, bf16[256,1024]{1,0:T(8,128)(2,1)S(1)}, u32[]{:S(2)}, u32[]{:S(2)}) collective-permute-start(bf16[256,1024]{1,0:T(8,128)(2,1)} %constant_dynamic-slice_fusion.2), channel_id=1, source_target_pairs={{0,4},{1,5},{2,6},{3,7},{4,8},{5,9},{6,10},{7,11},{8,12},{9,13},{1... | collective-permute-start | bytes 1572872 | tf_op jit(solution)/shard_map/ppermute | solution.py:36
  4.9 2.0 %collective-permute-start.5 = (bf16[256,1024]{1,0:T(8,128)(2,1)}, bf16[256,1024]{1,0:T(8,128)(2,1)}, u32[]{:S(2)}, u32[]{:S(2)}) collective-permute-start(bf16[256,1024]{1,0:T(8,128)(2,1)} %constant_dynamic-slice_fusion.2), channel_id=1, source_target_pairs={{0,12},{1,13},{2,14},{3,15},{4,0},{5,1},{6,2},{7,3},{8,4},{9,5},{1... | collective-permute-start | bytes 1572872 | tf_op jit(solution)/shard_map/ppermute | solution.py:36
  7.0 0.9 copy.30
  7.9 3.8 %collective-permute-start.14 = (bf16[64,1024]{1,0:T(8,128)(2,1)S(1)}, bf16[64,1024]{1,0:T(8,128)(2,1)S(1)}, u32[]{:S(2)}, u32[]{:S(2)}) collective-permute-start(bf16[64,1024]{1,0:T(8,128)(2,1)S(1)} %bitcast.13), channel_id=1, source_target_pairs={{0,12},{1,13},{2,14},{3,15},{4,0},{5,1},{6,2},{7,3},{8,4},{9,5},{1... | collective-permute-start | bytes 393224 | tf_op jit(solution)/shard_map/ppermute | solution.py:36
  13.4 1.7 %copy-done.3 = bf16[4,40,8192]{2,1,0:T(8,128)(2,1)S(1)} copy-done((bf16[4,40,8192]{2,1,0:T(8,128)(2,1)S(1)}, bf16[4,40,8192]{2,1,0:T(8,128)(2,1)}, u32[]{:S(2)}) %copy-start.3) | copy-done | bytes 2621464
  15.1 4.0 %norm.1 = (bf16[160,2048]{1,0:T(8,128)(2,1)S(1)}, bf16[160,2048]{1,0:T(8,128)(2,1)}, bf16[160,2048]{1,0:T(8,128)(2,1)}, bf16[160,2048]{1,0:T(8,128)(2,1)S(1)}) custom-call(s32[32]{0:T(128)S(1)} %and_select_fusion.7.offs_ref, bf16[160,8192]{1,0:T(8,128)(2,1)S(1)} %bitcast.9, bf16[1,8192]{1,0:T(2,128)(2,1)S(1)} %reshape.178.gain_ref), custom_call_target="tpu_custom_call" | custom-call | flops 7864320 | bytes 5242880 | tf_op jit(solution)/shard_map/norm/pallas_call | solution.py:63
  20.9 13.2 %collective-permute-done.13 = bf16[64,1024]{1,0:T(8,128)(2,1)S(1)} collective-permute-done((bf16[64,1024]{1,0:T(8,128)(2,1)S(1)}, bf16[64,1024]{1,0:T(8,128)(2,1)S(1)}, u32[]{:S(2)}, u32[]{:S(2)}) %collective-permute-start.13) | collective-permute-done | bytes 131104 | tf_op jit(solution)/shard_map/ppermute | solution.py:36
  34.1 1.2 %collective-permute-done.14 = bf16[64,1024]{1,0:T(8,128)(2,1)S(1)} collective-permute-done((bf16[64,1024]{1,0:T(8,128)(2,1)S(1)}, bf16[64,1024]{1,0:T(8,128)(2,1)S(1)}, u32[]{:S(2)}, u32[]{:S(2)}) %collective-permute-start.14) | collective-permute-done | bytes 131104 | tf_op jit(solution)/shard_map/ppermute | solution.py:36
  35.4 1.5 %collective-permute-start.1 = (bf16[160,2048]{1,0:T(8,128)(2,1)}, bf16[160,2048]{1,0:T(8,128)(2,1)S(1)}, u32[]{:S(2)}, u32[]{:S(2)}) collective-permute-start(bf16[160,2048]{1,0:T(8,128)(2,1)} %get-tuple-element.15), channel_id=1, source_target_pairs={{0,2},{1,3},{2,0},{3,1},{4,6},{5,7},{6,4},{7,5},{8,10},{9,11},{10,... | collective-permute-start | bytes 1966088 | tf_op jit(solution)/shard_map/ppermute | solution.py:41
  36.9 3.8 %collective-permute-done.15 = bf16[32,1024]{1,0:T(8,128)(2,1)S(1)} collective-permute-done((bf16[32,1024]{1,0:T(8,128)(2,1)S(1)}, bf16[32,1024]{1,0:T(8,128)(2,1)S(1)}, u32[]{:S(2)}, u32[]{:S(2)}) %collective-permute-start.15) | collective-permute-done | bytes 65568 | tf_op jit(solution)/shard_map/ppermute | solution.py:36
  40.8 1.2 %collective-permute-start.16 = (bf16[32,1024]{1,0:T(8,128)(2,1)S(1)}, bf16[32,1024]{1,0:T(8,128)(2,1)S(1)}, u32[]{:S(2)}, u32[]{:S(2)}) collective-permute-start(bf16[32,1024]{1,0:T(8,128)(2,1)S(1)} %slice.37), channel_id=1, source_target_pairs={{0,12},{1,13},{2,14},{3,15},{4,0},{5,1},{6,2},{7,3},{8,4},{9,5},{1... | collective-permute-start | bytes 196616 | tf_op jit(solution)/shard_map/ppermute | solution.py:36
  42.0 3.0 %collective-permute-done.16 = bf16[32,1024]{1,0:T(8,128)(2,1)S(1)} collective-permute-done((bf16[32,1024]{1,0:T(8,128)(2,1)S(1)}, bf16[32,1024]{1,0:T(8,128)(2,1)S(1)}, u32[]{:S(2)}, u32[]{:S(2)}) %collective-permute-start.16) | collective-permute-done | bytes 65568 | tf_op jit(solution)/shard_map/ppermute | solution.py:36
  45.0 1.6 %constant_dynamic-update-slice_fusion.3 = (bf16[256,1024]{1,0:T(8,128)(2,1)}, bf16[512,1024]{1,0:T(8,128)(2,1)}) fusion(bf16[256,1024]{1,0:T(8,128)(2,1)} %get-tuple-element.27, bf16[64,1024]{1,0:T(8,128)(2,1)} %copy-done.9, bf16[512,1024]{1,0:T(8,128)(2,1)} %get-tuple-element.28), kind=kLoop, calls=%fused_computation.11 | loop fusion | bytes 393216
  47.4 1.5 %collective-permute-start.9 = (bf16[256,1024]{1,0:T(8,128)(2,1)S(1)}, bf16[256,1024]{1,0:T(8,128)(2,1)}, u32[]{:S(2)}, u32[]{:S(2)}) collective-permute-start(bf16[256,1024]{1,0:T(8,128)(2,1)S(1)} %collective-permute-done.3.w1), channel_id=1, source_target_pairs={{0,16},{16,0},{1,17},{17,1},{2,18},{18,2},{3,19},{19,3},{4,20},{20... | collective-permute-start | bytes 1572872 | tf_op jit(solution)/shard_map/ppermute | solution.py:45
  50.8 1.7 %slice.33 = bf16[128,1024]{1,0:T(8,128)(2,1)} slice(bf16[256,1024]{1,0:T(8,128)(2,1)} %collective-permute-done.5.w3), slice={[128:256], [0:1024]} | slice | bytes 524288 | tf_op jit(solution)/shard_map/slice | solution.py:341
  53.3 3.0 %collective-permute-start.6 = (bf16[128,1024]{1,0:T(8,128)(2,1)}, bf16[128,1024]{1,0:T(8,128)(2,1)}, u32[]{:S(2)}, u32[]{:S(2)}) collective-permute-start(bf16[128,1024]{1,0:T(8,128)(2,1)} %slice.33), channel_id=1, source_target_pairs={{0,12},{1,13},{2,14},{3,15},{4,0},{5,1},{6,2},{7,3},{8,4},{9,5},{1... | collective-permute-start | bytes 786440 | tf_op jit(solution)/shard_map/ppermute | solution.py:36
  57.0 7.8 %collective-permute-done.2.a3 = bf16[160,2048]{1,0:T(8,128)(2,1)S(1)} collective-permute-done((bf16[160,2048]{1,0:T(8,128)(2,1)}, bf16[160,2048]{1,0:T(8,128)(2,1)S(1)}, u32[]{:S(2)}, u32[]{:S(2)}) %collective-permute-start.2) | collective-permute-done | bytes 655392 | tf_op jit(solution)/shard_map/ppermute | solution.py:41
  65.7 1.5 %collective-permute-start.7 = (bf16[128,1024]{1,0:T(8,128)(2,1)S(1)}, bf16[128,1024]{1,0:T(8,128)(2,1)S(1)}, u32[]{:S(2)}, u32[]{:S(2)}) collective-permute-start(bf16[128,1024]{1,0:T(8,128)(2,1)S(1)} %collective-permute-done.4.w0), channel_id=1, source_target_pairs={{0,16},{16,0},{1,17},{17,1},{2,18},{18,2},{3,19},{19,3},{4,20},{20... | collective-permute-start | bytes 786440 | tf_op jit(solution)/shard_map/ppermute | solution.py:45
  67.7 1.5 %collective-permute-start.8 = (bf16[128,1024]{1,0:T(8,128)(2,1)}, bf16[128,1024]{1,0:T(8,128)(2,1)S(1)}, u32[]{:S(2)}, u32[]{:S(2)}) collective-permute-start(bf16[128,1024]{1,0:T(8,128)(2,1)} %collective-permute-done.6.w1), channel_id=1, source_target_pairs={{0,16},{16,0},{1,17},{17,1},{2,18},{18,2},{3,19},{19,3},{4,20},{20... | collective-permute-start | bytes 786440 | tf_op jit(solution)/shard_map/ppermute | solution.py:45
  69.3 3.7 %collective-permute-done.10.w4 = bf16[256,1024]{1,0:T(8,128)(2,1)} collective-permute-done((bf16[256,1024]{1,0:T(8,128)(2,1)}, bf16[256,1024]{1,0:T(8,128)(2,1)}, u32[]{:S(2)}, u32[]{:S(2)}) %collective-permute-start.10) | collective-permute-done | bytes 524320 | tf_op jit(solution)/shard_map/ppermute | solution.py:45
  72.9 1.2 %copy-done.4 = bf16[512,1024]{1,0:T(8,128)(2,1)S(1)} copy-done((bf16[512,1024]{1,0:T(8,128)(2,1)S(1)}, bf16[512,1024]{1,0:T(8,128)(2,1)}, u32[]{:S(2)}) %copy-start.4) | copy-done | bytes 1048600
  74.2 5.4 %first_part.1.acc = f32[640,1024]{1,0:T(8,128)} custom-call(bf16[160,2048]{1,0:T(8,128)(2,1)S(1)} %get-tuple-element.13.a0, bf16[160,2048]{1,0:T(8,128)(2,1)S(1)} %collective-permute-done.a1, bf16[160,2048]{1,0:T(8,128)(2,1)S(1)} %collective-permute-done.1.a2, bf16[160,2048]{1,0:T(8,128)(2,1)S(1)} %collective-permute-done.2.a3, ...), custom_call_target="tpu_custom_call" | custom-call | flops 2013265920 | bytes 7733248 | tf_op jit(solution)/shard_map/first_part/pallas_call | solution.py:104
  79.6 4.5 %collective-permute-done.8.w3 = bf16[128,1024]{1,0:T(8,128)(2,1)S(1)} collective-permute-done((bf16[128,1024]{1,0:T(8,128)(2,1)}, bf16[128,1024]{1,0:T(8,128)(2,1)S(1)}, u32[]{:S(2)}, u32[]{:S(2)}) %collective-permute-start.8) | collective-permute-done | bytes 262176 | tf_op jit(solution)/shard_map/ppermute | solution.py:45
  84.1 4.0 %second_part.1 = (f32[320,1024]{1,0:T(8,128)S(1)}, bf16[320,1024]{1,0:T(8,128)(2,1)S(1)}) custom-call(bf16[160,2048]{1,0:T(8,128)(2,1)S(1)} %get-tuple-element.13.a0, bf16[160,2048]{1,0:T(8,128)(2,1)S(1)} %collective-permute-done.a1, bf16[160,2048]{1,0:T(8,128)(2,1)S(1)} %collective-permute-done.1.a2, bf16[160,2048]{1,0:T(8,128)(2,1)S(1)} %collective-permute-done.2.a3, ...), custom_call_target="tpu_custom_call" | custom-call | flops 671088640 | bytes 6291456 | tf_op jit(solution)/shard_map/second_part/pallas_call | solution.py:143
  88.6 1.9 %constant_dynamic-update-slice_fusion.5.near_ref = bf16[512,1024]{1,0:T(8,128)(2,1)} fusion(bf16[512,1024]{1,0:T(8,128)(2,1)} %get-tuple-element.30, bf16[256,1024]{1,0:T(8,128)(2,1)} %collective-permute-done.17), kind=kLoop, calls=%fused_computation.13 | loop fusion | bytes 1048576 | tf_op jit(solution)/shard_map/concatenate | solution.py:385
  90.9 1.0 add_convert_fusion
  92.0 1.6 %collective-permute-start.12 = (bf16[160,1024]{1,0:T(8,128)(2,1)}, bf16[160,1024]{1,0:T(8,128)(2,1)S(1)}, u32[]{:S(2)}, u32[]{:S(2)}) collective-permute-start(bf16[160,1024]{1,0:T(8,128)(2,1)} %get-tuple-element.21), channel_id=1, source_target_pairs={{0,2},{1,3},{2,0},{3,1},{4,6},{5,7},{6,4},{7,5},{8,10},{9,11},{10,... | collective-permute-start | bytes 983048 | tf_op jit(solution)/shard_map/ppermute | solution.py:41
  94.0 1.0 slice.34
  95.1 9.3 %cached_attention.1 = (f32[4,4,320,128]{3,2,1,0:T(8,128)}, f32[4,4,320,128]{3,2,1,0:T(8,128)}) custom-call(s32[16]{0:T(128)S(1)} %fusion.13.place_ref, s32[64]{0:T(128)S(1)} %copy-done.6, s32[4,20]{1,0:T(4,128)S(1)} %copy.29.ids_ref, bf16[4,40,4096]{2,1,0:T(8,128)(2,1)S(1)} %copy-done.1, bf16[512,1024]{1,0:T(8,128)(2,1)} %constant_dynamic-update-slice_fusion.5.near_ref, ...), custom_call_target="tpu_custom_call" | custom-call | flops 838860800 | bytes 8650752 | tf_op jit(solution)/shard_map/cached_attention/pallas_call | solution.py:222
  104.4 1.7 %copy-done.2 = f32[4,4,320,128]{3,2,1,0:T(8,128)S(1)} copy-done((f32[4,4,320,128]{3,2,1,0:T(8,128)S(1)}, f32[4,4,320,128]{3,2,1,0:T(8,128)}, u32[]{:S(2)}) %copy-start.2) | copy-done | bytes 2621464
  106.2 9.0 %fresh_attention.1 = bf16[4,40,4096]{2,1,0:T(8,128)(2,1)} custom-call(s32[4]{0:T(128)S(1)} %copy-done.5, bf16[4,40,4096]{2,1,0:T(8,128)(2,1)S(1)} %copy-done.1, f32[4,40,1024]{2,1,0:T(8,128)S(1)} %bitcast.8, bf16[4,40,1024]{2,1,0:T(8,128)(2,1)S(1)} %bitcast.10, bf16[4,40,1024]{2,1,0:T(8,128)(2,1)S(1)} %bitcast.11, f32[4,40,40]{2,1,0:T(8,128)S(1)} %and_select_fusion.bias_ref, ...), custom_call_target="tpu_custom_call" | custom-call | flops 104857600 | bytes 7864320 | tf_op jit(solution)/shard_map/fresh_attention/pallas_call | solution.py:287
  (70 shorter events, 10.4 us)
Async XLA Ops:
  0.0 20.7 %copy-start = (s32[64,20,2]{0,2,1:T(2,128)S(1)}, s32[64,20,2]{0,2,1:T(2,128)}, u32[]{:S(2)}) copy-start(s32[64,20,2]{0,2,1:T(2,128)} %param.19) | copy-start | bytes 30724
  1.9 45.5 %collective-permute-start.3 = (bf16[256,1024]{1,0:T(8,128)(2,1)}, bf16[256,1024]{1,0:T(8,128)(2,1)S(1)}, u32[]{:S(2)}, u32[]{:S(2)}) collective-permute-start(bf16[256,1024]{1,0:T(8,128)(2,1)} %constant_dynamic-slice_fusion.2), channel_id=1, source_target_pairs={{0,4},{1,5},{2,6},{3,7},{4,8},{5,9},{6,10},{7,11},{8,12},{9,13},{1... | collective-permute-start | bytes 1572872 | tf_op jit(solution)/shard_map/ppermute | solution.py:36
  4.9 44.0 %collective-permute-start.5 = (bf16[256,1024]{1,0:T(8,128)(2,1)}, bf16[256,1024]{1,0:T(8,128)(2,1)}, u32[]{:S(2)}, u32[]{:S(2)}) collective-permute-start(bf16[256,1024]{1,0:T(8,128)(2,1)} %constant_dynamic-slice_fusion.2), channel_id=1, source_target_pairs={{0,12},{1,13},{2,14},{3,15},{4,0},{5,1},{6,2},{7,3},{8,4},{9,5},{1... | collective-permute-start | bytes 1572872 | tf_op jit(solution)/shard_map/ppermute | solution.py:36
  7.9 26.2 %collective-permute-start.13 = (bf16[64,1024]{1,0:T(8,128)(2,1)S(1)}, bf16[64,1024]{1,0:T(8,128)(2,1)S(1)}, u32[]{:S(2)}, u32[]{:S(2)}) collective-permute-start(bf16[64,1024]{1,0:T(8,128)(2,1)S(1)} %bitcast.12), channel_id=1, source_target_pairs={{0,4},{1,5},{2,6},{3,7},{4,8},{5,9},{6,10},{7,11},{8,12},{9,13},{1... | collective-permute-start | bytes 393224 | tf_op jit(solution)/shard_map/ppermute | solution.py:36
  7.9 27.4 %collective-permute-start.14 = (bf16[64,1024]{1,0:T(8,128)(2,1)S(1)}, bf16[64,1024]{1,0:T(8,128)(2,1)S(1)}, u32[]{:S(2)}, u32[]{:S(2)}) collective-permute-start(bf16[64,1024]{1,0:T(8,128)(2,1)S(1)} %bitcast.13), channel_id=1, source_target_pairs={{0,12},{1,13},{2,14},{3,15},{4,0},{5,1},{6,2},{7,3},{8,4},{9,5},{1... | collective-permute-start | bytes 393224 | tf_op jit(solution)/shard_map/ppermute | solution.py:36
  13.4 1.7 %copy-start.3 = (bf16[4,40,8192]{2,1,0:T(8,128)(2,1)S(1)}, bf16[4,40,8192]{2,1,0:T(8,128)(2,1)}, u32[]{:S(2)}) copy-start(bf16[4,40,8192]{2,1,0:T(8,128)(2,1)} %param.11) | copy-start | bytes 7864324
  15.1 50.4 %copy-start.5 = (s32[4]{0:T(128)S(1)}, s32[4]{0:T(128)}, u32[]{:S(2)}) copy-start(s32[4]{0:T(128)} %count_ref.1) | copy-start | bytes 52
  19.1 0.9 copy-start.7
  20.0 32.5 %collective-permute-start = (bf16[160,2048]{1,0:T(8,128)(2,1)}, bf16[160,2048]{1,0:T(8,128)(2,1)S(1)}, u32[]{:S(2)}, u32[]{:S(2)}) collective-permute-start(bf16[160,2048]{1,0:T(8,128)(2,1)} %get-tuple-element.14), channel_id=1, source_target_pairs={{0,1},{1,0},{2,3},{3,2},{4,5},{5,4},{6,7},{7,6},{8,9},{9,8},{10,11... | collective-permute-start | bytes 1966088 | tf_op jit(solution)/shard_map/ppermute | solution.py:41
  34.0 1.3 %copy-start.9 = (bf16[64,1024]{1,0:T(8,128)(2,1)}, bf16[64,1024]{1,0:T(8,128)(2,1)S(1)}, u32[]{:S(2)}) copy-start(bf16[64,1024]{1,0:T(8,128)(2,1)S(1)} %collective-permute-done.13) | copy-start | bytes 393220
  34.1 6.7 %collective-permute-start.15 = (bf16[32,1024]{1,0:T(8,128)(2,1)S(1)}, bf16[32,1024]{1,0:T(8,128)(2,1)S(1)}, u32[]{:S(2)}, u32[]{:S(2)}) collective-permute-start(bf16[32,1024]{1,0:T(8,128)(2,1)S(1)} %slice.36), channel_id=1, source_target_pairs={{0,4},{1,5},{2,6},{3,7},{4,8},{5,9},{6,10},{7,11},{8,12},{9,13},{1... | collective-permute-start | bytes 196616 | tf_op jit(solution)/shard_map/ppermute | solution.py:36
  35.4 17.9 %collective-permute-start.1 = (bf16[160,2048]{1,0:T(8,128)(2,1)}, bf16[160,2048]{1,0:T(8,128)(2,1)S(1)}, u32[]{:S(2)}, u32[]{:S(2)}) collective-permute-start(bf16[160,2048]{1,0:T(8,128)(2,1)} %get-tuple-element.15), channel_id=1, source_target_pairs={{0,2},{1,3},{2,0},{3,1},{4,6},{5,7},{6,4},{7,5},{8,10},{9,11},{10,... | collective-permute-start | bytes 1966088 | tf_op jit(solution)/shard_map/ppermute | solution.py:41
  40.8 4.3 %collective-permute-start.16 = (bf16[32,1024]{1,0:T(8,128)(2,1)S(1)}, bf16[32,1024]{1,0:T(8,128)(2,1)S(1)}, u32[]{:S(2)}, u32[]{:S(2)}) collective-permute-start(bf16[32,1024]{1,0:T(8,128)(2,1)S(1)} %slice.37), channel_id=1, source_target_pairs={{0,12},{1,13},{2,14},{3,15},{4,0},{5,1},{6,2},{7,3},{8,4},{9,5},{1... | collective-permute-start | bytes 196616 | tf_op jit(solution)/shard_map/ppermute | solution.py:36
  45.0 19.8 %collective-permute-start.2 = (bf16[160,2048]{1,0:T(8,128)(2,1)}, bf16[160,2048]{1,0:T(8,128)(2,1)S(1)}, u32[]{:S(2)}, u32[]{:S(2)}) collective-permute-start(bf16[160,2048]{1,0:T(8,128)(2,1)} %copy-done.7), channel_id=1, source_target_pairs={{0,3},{1,2},{2,1},{3,0},{4,7},{5,6},{6,5},{7,4},{8,11},{9,10},{10,... | collective-permute-start | bytes 1966088 | tf_op jit(solution)/shard_map/ppermute | solution.py:41
  47.4 21.9 %collective-permute-start.9 = (bf16[256,1024]{1,0:T(8,128)(2,1)S(1)}, bf16[256,1024]{1,0:T(8,128)(2,1)}, u32[]{:S(2)}, u32[]{:S(2)}) collective-permute-start(bf16[256,1024]{1,0:T(8,128)(2,1)S(1)} %collective-permute-done.3.w1), channel_id=1, source_target_pairs={{0,16},{16,0},{1,17},{17,1},{2,18},{18,2},{3,19},{19,3},{4,20},{20... | collective-permute-start | bytes 1572872 | tf_op jit(solution)/shard_map/ppermute | solution.py:45
  48.9 24.1 %collective-permute-start.10 = (bf16[256,1024]{1,0:T(8,128)(2,1)}, bf16[256,1024]{1,0:T(8,128)(2,1)}, u32[]{:S(2)}, u32[]{:S(2)}) collective-permute-start(bf16[256,1024]{1,0:T(8,128)(2,1)} %collective-permute-done.5.w3), channel_id=1, source_target_pairs={{0,16},{16,0},{1,17},{17,1},{2,18},{18,2},{3,19},{19,3},{4,20},{20... | collective-permute-start | bytes 1572872 | tf_op jit(solution)/shard_map/ppermute | solution.py:45
  52.5 13.2 %collective-permute-start.4 = (bf16[128,1024]{1,0:T(8,128)(2,1)}, bf16[128,1024]{1,0:T(8,128)(2,1)S(1)}, u32[]{:S(2)}, u32[]{:S(2)}) collective-permute-start(bf16[128,1024]{1,0:T(8,128)(2,1)} %slice.32), channel_id=1, source_target_pairs={{0,4},{1,5},{2,6},{3,7},{4,8},{5,9},{6,10},{7,11},{8,12},{9,13},{1... | collective-permute-start | bytes 786440 | tf_op jit(solution)/shard_map/ppermute | solution.py:36
  53.3 14.5 %collective-permute-start.6 = (bf16[128,1024]{1,0:T(8,128)(2,1)}, bf16[128,1024]{1,0:T(8,128)(2,1)}, u32[]{:S(2)}, u32[]{:S(2)}) collective-permute-start(bf16[128,1024]{1,0:T(8,128)(2,1)} %slice.33), channel_id=1, source_target_pairs={{0,12},{1,13},{2,14},{3,15},{4,0},{5,1},{6,2},{7,3},{8,4},{9,5},{1... | collective-permute-start | bytes 786440 | tf_op jit(solution)/shard_map/ppermute | solution.py:36
  64.8 23.8 %collective-permute-start.17 = (bf16[256,1024]{1,0:T(8,128)(2,1)}, bf16[256,1024]{1,0:T(8,128)(2,1)}, u32[]{:S(2)}, u32[]{:S(2)}) collective-permute-start(bf16[256,1024]{1,0:T(8,128)(2,1)} %get-tuple-element.29), channel_id=1, source_target_pairs={{0,2},{1,3},{2,0},{3,1},{4,6},{5,7},{6,4},{7,5},{8,10},{9,11},{10,... | collective-permute-start | bytes 1572872 | tf_op jit(solution)/shard_map/ppermute | solution.py:41
  65.7 13.9 %collective-permute-start.7 = (bf16[128,1024]{1,0:T(8,128)(2,1)S(1)}, bf16[128,1024]{1,0:T(8,128)(2,1)S(1)}, u32[]{:S(2)}, u32[]{:S(2)}) collective-permute-start(bf16[128,1024]{1,0:T(8,128)(2,1)S(1)} %collective-permute-done.4.w0), channel_id=1, source_target_pairs={{0,16},{16,0},{1,17},{17,1},{2,18},{18,2},{3,19},{19,3},{4,20},{20... | collective-permute-start | bytes 786440 | tf_op jit(solution)/shard_map/ppermute | solution.py:45
  67.7 16.3 %collective-permute-start.8 = (bf16[128,1024]{1,0:T(8,128)(2,1)}, bf16[128,1024]{1,0:T(8,128)(2,1)S(1)}, u32[]{:S(2)}, u32[]{:S(2)}) collective-permute-start(bf16[128,1024]{1,0:T(8,128)(2,1)} %collective-permute-done.6.w1), channel_id=1, source_target_pairs={{0,16},{16,0},{1,17},{17,1},{2,18},{18,2},{3,19},{19,3},{4,20},{20... | collective-permute-start | bytes 786440 | tf_op jit(solution)/shard_map/ppermute | solution.py:45
  72.9 1.2 %copy-start.4 = (bf16[512,1024]{1,0:T(8,128)(2,1)S(1)}, bf16[512,1024]{1,0:T(8,128)(2,1)}, u32[]{:S(2)}) copy-start(bf16[512,1024]{1,0:T(8,128)(2,1)} %w0.1) | copy-start | bytes 3145732
  79.6 9.0 %copy-start.10 = (s32[64,20]{0,1:T(8,128)S(1)}, s32[64,20]{0,1:T(8,128)}, u32[]{:S(2)}) copy-start(s32[64,20]{0,1:T(8,128)} %param.17) | copy-start | bytes 15364
  88.1 7.0 %copy-start.1 = (bf16[4,40,4096]{2,1,0:T(8,128)(2,1)S(1)}, bf16[4,40,4096]{2,1,0:T(8,128)(2,1)}, u32[]{:S(2)}) copy-start(bf16[4,40,4096]{2,1,0:T(8,128)(2,1)} %q_ref.3) | copy-start | bytes 3932164
  88.1 7.0 %copy-start.6 = (s32[64]{0:T(128)S(1)}, s32[64]{0:T(128)}, u32[]{:S(2)}) copy-start(s32[64]{0:T(128)} %home_ref.1) | copy-start | bytes 772
  88.1 2.8 %collective-permute-start.11 = (bf16[320,1024]{1,0:T(8,128)(2,1)S(1)}, bf16[320,1024]{1,0:T(8,128)(2,1)S(1)}, u32[]{:S(2)}, u32[]{:S(2)}) collective-permute-start(bf16[320,1024]{1,0:T(8,128)(2,1)S(1)} %get-tuple-element.18), channel_id=1, source_target_pairs={{0,1},{1,0},{2,3},{3,2},{4,5},{5,4},{6,7},{7,6},{8,9},{9,8},{10,11... | collective-permute-start | bytes 1966088 | tf_op jit(solution)/shard_map/ppermute | solution.py:41
  90.5 4.5 %collective-permute-start.18 = (bf16[512,1024]{1,0:T(8,128)(2,1)}, bf16[512,1024]{1,0:T(8,128)(2,1)S(1)}, u32[]{:S(2)}, u32[]{:S(2)}) collective-permute-start(bf16[512,1024]{1,0:T(8,128)(2,1)} %constant_dynamic-update-slice_fusion.5.near_ref), channel_id=1, source_target_pairs={{0,1},{1,0},{2,3},{3,2},{4,5},{5,4},{6,7},{7,6},{8,9},{9,8},{10,11... | collective-permute-start | bytes 3145736 | tf_op jit(solution)/shard_map/ppermute | solution.py:41
  90.9 2.6 %copy-start.8 = (bf16[320,1024]{1,0:T(8,128)(2,1)}, bf16[320,1024]{1,0:T(8,128)(2,1)S(1)}, u32[]{:S(2)}) copy-start(bf16[320,1024]{1,0:T(8,128)(2,1)S(1)} %collective-permute-done.11) | copy-start | bytes 1966084
  92.0 12.5 %collective-permute-start.12 = (bf16[160,1024]{1,0:T(8,128)(2,1)}, bf16[160,1024]{1,0:T(8,128)(2,1)S(1)}, u32[]{:S(2)}, u32[]{:S(2)}) collective-permute-start(bf16[160,1024]{1,0:T(8,128)(2,1)} %get-tuple-element.21), channel_id=1, source_target_pairs={{0,2},{1,3},{2,0},{3,1},{4,6},{5,7},{6,4},{7,5},{8,10},{9,11},{10,... | collective-permute-start | bytes 983048 | tf_op jit(solution)/shard_map/ppermute | solution.py:41
  104.4 1.7 %copy-start.2 = (f32[4,4,320,128]{3,2,1,0:T(8,128)S(1)}, f32[4,4,320,128]{3,2,1,0:T(8,128)}, u32[]{:S(2)}) copy-start(f32[4,4,320,128]{3,2,1,0:T(8,128)} %get-tuple-element.19.part_ref) | copy-start | bytes 7864324

commit v2 on v1

v2 whole, which is shorter than its diff:
```python
import functools
import math

import jax
import jax.numpy as jnp
from jax import lax
from jax.experimental import pallas as pl
from jax.experimental.pallas import tpu as pltpu
from jax.sharding import PartitionSpec as P

QUERY_HEADS = 32
KEY_VALUE_HEADS = 4
HEAD_SIZE = 128
HEAD_GROUP = QUERY_HEADS // KEY_VALUE_HEADS
GROUP = 4
HIDDEN = -1e30
EXP2_SCALE = math.log2(math.e) / math.sqrt(HEAD_SIZE)
VMEM_LIMIT = 48 * 2**20


def params(**more):
    return pltpu.CompilerParams(vmem_limit_bytes=VMEM_LIMIT, **more)


def whole():
    return pl.BlockSpec(memory_space=pltpu.VMEM)


def smem():
    return pl.BlockSpec(memory_space=pltpu.SMEM)


def send(x, steps):
    shards = lax.axis_size("store")
    pairs = [(i, (i + steps * GROUP) % shards) for i in range(shards)]
    return lax.ppermute(x, "store", pairs)


def flip(x, bits):
    pairs = [(i, i ^ bits) for i in range(lax.axis_size("store"))]
    return lax.ppermute(x, "store", pairs)


def swap(x):
    return lax.ppermute(x, "parts", [(0, 1), (1, 0)])


def norm_kernel(chunk, chunks, offs_ref, rows_ref, gain_ref, own_ref, y_ref, core_ref, held):
    wide = rows_ref[...].astype(jnp.float32)
    inv = lax.rsqrt(jnp.mean(wide * wide, axis=-1, keepdims=True) + 1e-05)
    held[...] = (wide * inv * gain_ref[...].astype(jnp.float32)).astype(jnp.bfloat16)
    for j in range(GROUP):
        for k in range(chunks):
            at = pl.multiple_of(offs_ref[j * chunks + k] * 128, 128)
            piece = held[:, pl.ds(at, chunk)]
            if j < 2:
                out = (own_ref, core_ref)[j]
                out[:, k * chunk : (k + 1) * chunk] = piece
            else:
                y_ref[j - 2, :, k * chunk : (k + 1) * chunk] = piece


def norm_rows(rows, gain, offs, chunk):
    count, width = rows.shape
    chunks = width // GROUP // chunk
    block = 32
    depth = width // GROUP
    one = jax.ShapeDtypeStruct((count, depth), jnp.bfloat16)
    two = jax.ShapeDtypeStruct((2, count, depth), jnp.bfloat16)
    one_spec = pl.BlockSpec((block, depth), lambda i: (i, 0))
    own, y, core = pl.pallas_call(
        functools.partial(norm_kernel, chunk, chunks),
        out_shape=[one, two, one],
        grid=(count // block,),
        in_specs=[
            smem(),
            pl.BlockSpec((block, width), lambda i: (i, 0)),
            pl.BlockSpec((1, width), lambda i: (0, 0)),
        ],
        out_specs=[one_spec, pl.BlockSpec((2, block, depth), lambda i: (0, i, 0)), one_spec],
        scratch_shapes=[pltpu.VMEM((block, width), jnp.bfloat16)],
        compiler_params=params(),
        cost_estimate=pl.CostEstimate(
            flops=6 * count * width, bytes_accessed=4 * count * width, transcendentals=0
        ),
        name="norm",
    )(offs, rows, gain.reshape(1, width))
    return own, y.reshape(2 * count, depth), core


def dot(a, b):
    return jnp.dot(a, b, preferred_element_type=jnp.float32)


def project_kernel(a0, a1, a2, a3, *refs):
    weights, (keep, send) = refs[:-2], refs[-2:]
    rows = a0.shape[0]
    for j, a in enumerate((a0, a1, a2, a3)):
        total = None
        at = 0
        for w in weights:
            depth = w.shape[0]
            term = dot(a[:, at : at + depth], w[...])
            total = term if total is None else total + term
            at += depth
        place = slice((j // 2) * rows, (j // 2 + 1) * rows)
        if j % 2:
            send[place, :] = total.astype(jnp.bfloat16)
        else:
            keep[place, :] = total


def project(acts, own, first, weights, half):
    rows, depth = acts[0].shape
    features = weights[0].shape[1]
    block = 256
    shift = first * features // block
    return pl.pallas_call(
        project_kernel,
        out_shape=[
            jax.ShapeDtypeStruct((2 * rows, features), jnp.float32),
            jax.ShapeDtypeStruct((2 * rows, features), jnp.bfloat16),
        ],
        grid=(features // block,),
        in_specs=[pl.BlockSpec((rows, depth), lambda i: (0, 0))] * GROUP
        + [pl.BlockSpec((own.shape[0], block), lambda i: (0, i + shift))]
        + [pl.BlockSpec((half, block), lambda i: (0, i)) for w in weights],
        out_specs=[pl.BlockSpec((2 * rows, block), lambda i: (0, i))] * 2,
        compiler_params=params(),
        cost_estimate=pl.CostEstimate(
            flops=2 * GROUP * rows * depth * features,
            bytes_accessed=2 * depth * (GROUP * rows + features) + 6 * GROUP * rows * features,
            transcendentals=0,
        ),
        name="project",
    )(*acts, own, *weights)


def stacked_queries(q_ref, head):
    parts = []
    for i in range(HEAD_GROUP):
        at = (head * HEAD_GROUP + i) * HEAD_SIZE
        parts.append(q_ref[0, :, at : at + HEAD_SIZE].astype(jnp.float32))
    return jnp.concatenate(parts, axis=0).astype(jnp.bfloat16)


def scores_of(q, keys, bias):
    s = lax.dot_general(q, keys, (((1,), (1,)), ((), ())), preferred_element_type=jnp.float32)
    rows, cols = bias.shape
    s = (s * EXP2_SCALE).reshape(HEAD_GROUP, rows, cols) + bias[None]
    return s.reshape(HEAD_GROUP * rows, cols)


def cached_kernel(per_dev, place_ref, home_ref, ids_ref, q_ref, *refs):
    sources, (bias_ref, out_ref, stat_ref, pages, context, sems) = refs[:-6], refs[-6:]
    r = pl.program_id(0)
    maxp = ids_ref.shape[1]
    plen = context.shape[1] // maxp

    @pl.when(r == 0)
    def _():
        copies = []
        at = 0
        for n, source in enumerate(sources):
            rows = source.shape[0]
            copies.append(pltpu.make_async_copy(source, pages.at[pl.ds(at, rows)], sems.at[n]))
            at += rows
        for copy in copies:
            copy.start()
        for copy in copies:
            copy.wait()

    for m in range(maxp):
        slot = home_ref[ids_ref[r, m]]
        block = place_ref[slot // per_dev] * (2 * per_dev) + slot % per_dev
        for c in range(2):
            at = pl.multiple_of((block + c * per_dev) * plen, plen)
            context[c, m * plen : (m + 1) * plen, :] = pages[pl.ds(at, plen), :]
    bias = bias_ref[0]
    lane = lax.broadcasted_iota(jnp.int32, (HEAD_GROUP * bias.shape[0], HEAD_SIZE), 1)
    for g in range(KEY_VALUE_HEADS):
        q = stacked_queries(q_ref, g)
        keys = context[0, :, g * HEAD_SIZE : (g + 1) * HEAD_SIZE]
        values = context[1, :, g * HEAD_SIZE : (g + 1) * HEAD_SIZE]
        s = scores_of(q, keys, bias)
        top = jnp.max(s, axis=-1, keepdims=True)
        e = jnp.exp2(s - top)
        total = jnp.sum(e, axis=-1, keepdims=True)
        out_ref[0, g] = dot(e.astype(jnp.bfloat16), values)
        stat_ref[0, g] = jnp.where(lane < HEAD_SIZE // 2, top, total)


def cached_attention(per_dev, place, home, ids, sources, queries, bias):
    owned, rows, width = queries.shape
    context = bias.shape[2]
    features = sources[0].shape[1]
    stacked = HEAD_GROUP * rows
    state = jax.ShapeDtypeStruct((owned, KEY_VALUE_HEADS, stacked, HEAD_SIZE), jnp.float32)
    state_spec = pl.BlockSpec((1, KEY_VALUE_HEADS, stacked, HEAD_SIZE), lambda r: (r, 0, 0, 0))
    return pl.pallas_call(
        functools.partial(cached_kernel, per_dev),
        out_shape=[state, state],
        grid=(owned,),
        in_specs=[
            smem(),
            smem(),
            smem(),
            pl.BlockSpec((1, rows, width), lambda r: (r, 0, 0)),
            *[pl.BlockSpec(memory_space=pl.ANY)] * len(sources),
            pl.BlockSpec((1, rows, context), lambda r: (r, 0, 0)),
        ],
        out_specs=[state_spec, state_spec],
        scratch_shapes=[
            pltpu.VMEM((sum(x.shape[0] for x in sources), features), jnp.bfloat16),
            pltpu.VMEM((2, context, features), jnp.bfloat16),
            pltpu.SemaphoreType.DMA((len(sources),)),
        ],
        compiler_params=params(),
        cost_estimate=pl.CostEstimate(
            flops=4 * owned * rows * width * context,
            bytes_accessed=8 * sources[0].size + 2 * queries.size + 8 * owned * stacked * 4 * HEAD_SIZE,
            transcendentals=owned * rows * QUERY_HEADS * context,
        ),
        name="cached_attention",
    )(place, home, ids, queries, *sources, bias)


def added(own_ref, core_ref, y_ref):
    total = own_ref[0] + core_ref[0].astype(jnp.float32) + y_ref[0].astype(jnp.float32)
    return total.astype(jnp.bfloat16)


def fresh_kernel(
    maxp, count_ref, q_ref, ko_ref, kc_ref, ky_ref, vo_ref, vc_ref, vy_ref, bias_ref, part_ref,
    stat_ref, out_ref,
):
    r = pl.program_id(0)
    fresh_keys = added(ko_ref, kc_ref, ky_ref)
    fresh_values = added(vo_ref, vc_ref, vy_ref)
    bias = bias_ref[0]
    rows = bias.shape[0]
    per_pass = rows // maxp
    slot = lax.broadcasted_iota(jnp.int32, (rows, HEAD_SIZE), 0) // per_pass
    live = slot < count_ref[r]
    for g in range(KEY_VALUE_HEADS):
        q = stacked_queries(q_ref, g)
        keys = fresh_keys[:, g * HEAD_SIZE : (g + 1) * HEAD_SIZE]
        values = fresh_values[:, g * HEAD_SIZE : (g + 1) * HEAD_SIZE]
        s = scores_of(q, keys, bias)
        top1 = stat_ref[0, g, :, 0:1]
        sum1 = stat_ref[0, g, :, HEAD_SIZE // 2 : HEAD_SIZE // 2 + 1]
        top = jnp.maximum(top1, jnp.max(s, axis=-1, keepdims=True))
        e = jnp.exp2(s - top)
        keep = jnp.exp2(top1 - top)
        inv = 1.0 / (sum1 * keep + jnp.sum(e, axis=-1, keepdims=True))
        result = (part_ref[0, g] * keep + dot(e.astype(jnp.bfloat16), values)) * inv
        for i in range(HEAD_GROUP):
            at = (g * HEAD_GROUP + i) * HEAD_SIZE
            one = result[i * rows : (i + 1) * rows]
            out_ref[0, :, at : at + HEAD_SIZE] = jnp.where(live, one, 0.0).astype(jnp.bfloat16)


def fresh_attention(maxp, count, queries, terms, bias, part, stat):
    owned, rows, width = queries.shape
    features = terms[0].shape[-1]
    stacked = HEAD_GROUP * rows
    state_spec = pl.BlockSpec((1, KEY_VALUE_HEADS, stacked, HEAD_SIZE), lambda r: (r, 0, 0, 0))
    row_spec = pl.BlockSpec((1, rows, features), lambda r: (r, 0, 0))
    query_spec = pl.BlockSpec((1, rows, width), lambda r: (r, 0, 0))
    return pl.pallas_call(
        functools.partial(fresh_kernel, maxp),
        out_shape=jax.ShapeDtypeStruct(queries.shape, jnp.bfloat16),
        grid=(owned,),
        in_specs=[
            smem(),
            query_spec,
            *[row_spec] * 6,
            pl.BlockSpec((1, rows, rows), lambda r: (r, 0, 0)),
            state_spec,
            state_spec,
        ],
        out_specs=query_spec,
        compiler_params=params(),
        cost_estimate=pl.CostEstimate(
            flops=4 * owned * rows * width * rows,
            bytes_accessed=4 * queries.size + 8 * part.size,
            transcendentals=owned * rows * QUERY_HEADS * rows,
        ),
        name="fresh_attention",
    )(count, queries, *terms, bias, part, stat)


def masks(rows, count, plen):
    owned, maxp, per_pass = rows.shape
    selected = maxp * per_pass
    touched = jnp.any(rows[..., None] == jnp.arange(plen, dtype=jnp.int32), axis=2)
    touched = touched.reshape(owned, 1, maxp * plen)
    key_pos = jnp.arange(maxp * plen, dtype=jnp.int32)
    slot = jnp.arange(selected, dtype=jnp.int32) // per_pass
    query_pos = slot * plen + rows.reshape(owned, selected)
    seen = (key_pos // plen < count[:, None, None]) & (key_pos <= query_pos[:, :, None])
    cached_bias = jnp.where(seen & ~touched, 0.0, HIDDEN).astype(jnp.float32)
    seen = (slot < count[:, None, None]) & (query_pos[:, None, :] <= query_pos[:, :, None])
    fresh_bias = jnp.where(seen, 0.0, HIDDEN).astype(jnp.float32)
    return cached_bias, fresh_bias


def after(x, *earlier):
    return lax.optimization_barrier((x, *earlier))[0]


def ring_plan(rows_in, norm_gain, kv_weight, store_pages):
    shards = lax.axis_size("store")
    me = lax.axis_index("store")
    side = lax.axis_index("parts")
    ring = shards // GROUP
    z, member = me // GROUP, me % GROUP
    owned, selected, width = rows_in.shape
    depth, features = kv_weight.shape
    local, plen, _, kvw = store_pages.shape
    half = depth // 2
    columns = features // 2

    pages = store_pages.reshape(local * plen, 2, kvw)
    mine = [
        lax.dynamic_slice(kv_weight, (side * half, n * columns), (half, columns)) for n in range(2)
    ]
    own = jnp.concatenate([pages[:, 0], pages[:, 1]], axis=0)
    a0 = jnp.concatenate([mine[0], own], axis=0)
    a1, b1 = send(a0, 1), send(mine[1], 1)
    gate = a0

    steps = jnp.arange(2 * ring, dtype=jnp.int32) // 2
    blocks = (z - steps) % ring
    halves = jnp.arange(2 * ring, dtype=jnp.int32) % 2
    halves = jnp.where(steps == 0, halves, halves ^ side)
    targets = member ^ jnp.arange(GROUP, dtype=jnp.int32)
    offs = (blocks[None] * GROUP + targets[:, None]) * depth + halves[None] * half
    offs = (offs // 128).reshape(-1)
    flat = rows_in.reshape(owned * selected, width)
    acts = norm_rows(flat, norm_gain, after(offs, gate), half)
    y_acts = flip(acts[1], 2)
    near_act = flip(acts[2], 1)

    a2 = send(after(a1, near_act), 1)
    xa1 = swap(after(a1[:half], near_act))
    b2 = send(after(b1, near_act), 1)
    xb1 = swap(b1)
    a3 = send(after(a2, xa1), 1)
    xa2 = swap(after(a2[:half], xa1))
    b3 = send(after(b2, xb1), 1)
    xb2 = swap(after(b2, xb1))
    xa3 = swap(after(a3[:half], xa2))
    column = jnp.concatenate([own, a1[half:], a2[half:], a3[half:]], axis=0)
    column = after(column, y_acts)
    y_column = flip(column, 2)
    y_far = flip(y_acts[acts[0].shape[0] :], 1)
    xb3 = swap(after(b3, xb2))
    far = flip(column, 1)
    y_column_far = flip(y_column, 1)
    acts = [acts[0], near_act, y_acts, y_far]
    chunks = [[a1, xa1, a2, xa2, a3, xa3], [b1, xb1, b2, xb2, b3, xb3]]

    count = owned * selected
    terms = []
    for n in range(2):
        keep, out = project(acts, kv_weight, n, chunks[n], half)
        back = flip(out, 1)
        y_out = (keep[count:] + back[count:].astype(jnp.float32)).astype(jnp.bfloat16)
        terms.append((keep[:count], back[:count], flip(y_out, 2)))

    device = jnp.arange(shards, dtype=jnp.int32)
    rank = (z - device // GROUP) % ring
    rel = (device % GROUP) ^ member
    place = ((rel % 2) * 2 + rel // 2) * ring + rank
    return (place, [column, y_column, far, y_column_far]), terms


def gathered_projection(rows_in, norm_gain, kv_weight):
    owned, selected, width = rows_in.shape
    wide = rows_in.reshape(owned * selected, width).astype(jnp.float32)
    inv = lax.rsqrt(jnp.mean(wide * wide, axis=-1, keepdims=True) + 1e-05)
    normed = (wide * inv * norm_gain.astype(jnp.float32)).astype(jnp.bfloat16)
    fresh = dot(normed, lax.all_gather(kv_weight, "store", axis=0, tiled=True))
    none = jnp.zeros((fresh.shape[0], fresh.shape[1] // 2), jnp.bfloat16)
    return [(part, none, none) for part in jnp.split(fresh, 2, axis=1)]


def sent_pages(store_pages, passage_home, passage_ids):
    shards = lax.axis_size("store")
    me = lax.axis_index("store")
    local, plen, _, kvw = store_pages.shape
    owned = passage_ids.shape[0] // shards
    positions = owned * passage_ids.shape[1]
    cap = (positions + shards - 1) // shards
    slots = passage_home[passage_ids]
    home_shard = (slots // local).reshape(shards, positions)
    local_slot = (slots % local).reshape(shards, positions)
    earlier = jnp.tril(jnp.ones((positions, positions), jnp.bool_), -1)
    same = home_shard[:, :, None] == home_shard[:, None, :]
    rank = jnp.sum(same & earlier[None], axis=2)
    ladder = jnp.arange(cap, dtype=jnp.int32)
    hit = (home_shard[:, :, None] == me) & (rank[:, :, None] == ladder[None, None, :])
    pick = jnp.sum(jnp.where(hit, local_slot[:, :, None], 0), axis=1)
    outgoing = store_pages[pick.reshape(shards * cap)]
    my_shard = lax.dynamic_slice_in_dim(home_shard, me, 1, 0)[0]
    my_rank = lax.dynamic_slice_in_dim(rank, me, 1, 0)[0]
    arrived = lax.all_to_all(outgoing, "store", split_axis=0, concat_axis=0, tiled=True)
    arrived = arrived.transpose(0, 2, 1, 3).reshape(shards * cap * 2 * plen, kvw)
    place = jnp.arange(shards * cap, dtype=jnp.int32)
    home = (my_shard * cap + my_rank).astype(jnp.int32)
    ids = jnp.arange(positions, dtype=jnp.int32).reshape(owned, passage_ids.shape[1])
    return place, home, ids, [arrived]


def per_device(
    rows_in,
    norm_gain,
    kv_weight,
    queries,
    store_pages,
    passage_home,
    passage_ids,
    passage_count,
    recompute_rows,
):
    shards = lax.axis_size("store")
    me = lax.axis_index("store")
    owned, selected, _ = rows_in.shape
    local, plen = store_pages.shape[:2]
    ringed = shards == 4 * GROUP and lax.axis_size("parts") == 2 and kv_weight.shape[0] % 512 == 0
    if ringed:
        (place, sources), terms = ring_plan(rows_in, norm_gain, kv_weight, store_pages)
        ids = lax.dynamic_slice_in_dim(passage_ids, me * owned, owned, 0)
        pages = (place, passage_home, ids, sources)
        per_dev = local
    else:
        terms = gathered_projection(rows_in, norm_gain, kv_weight)
        pages = sent_pages(store_pages, passage_home, passage_ids)
        per_dev = 1
    rows = lax.dynamic_slice_in_dim(recompute_rows, me * owned, owned, 0)
    cached_bias, fresh_bias = masks(rows, passage_count, plen)
    part, stat = cached_attention(per_dev, *pages, queries, cached_bias)
    terms = [t.reshape(owned, selected, t.shape[1]) for chunk in terms for t in chunk]
    return fresh_attention(passage_ids.shape[1], passage_count, queries, terms, fresh_bias, part, stat)


def solution(mesh):
    in_specs = (
        P(("parts", "store"), None, None),
        P(),
        P("store", None),
        P(("parts", "store"), None, None),
        P(("parts", "store"), None, None, None),
        P("parts"),
        P("parts", None),
        P(("parts", "store")),
        P("parts", None, None),
    )
    out_specs = P(("parts", "store"), None, None)
    return jax.shard_map(
        per_device, mesh=mesh, in_specs=in_specs, out_specs=out_specs, check_vma=False
    )
```

time: 116 us -> 92.6 us (0.80)
  local copies, waits for them, and re-layouts: 19.5 us -> 10.9 us
  waiting for transfers between devices: 38.6 us -> 30.6 us
  starting transfers between devices: 22.8 us -> 18.2 us
  Pallas kernels: 31.8 us -> 29.5 us
    ppermute x8 -> x6, starting transfers between devices: 13.2 us -> 4.93 us  [send(): return lax.ppermute(x, 'store', pairs)]
    ppermute x4 -> x6, waiting for transfers between devices: 8.17 us -> 2.68 us  [swap(): return lax.ppermute(x, 'parts', [(0, 1), (1, 0)])]
    unnamed x28, local copies, waits for them, and re-layouts: 10.3 us -> 5.4 us
    ppermute x7 -> x10, waiting for transfers between devices: 8.64 us -> 3.76 us  [flip(): return lax.ppermute(x, 'store', pairs)]
    ppermute x4 -> x6, starting transfers between devices: 5.01 us -> 8.47 us  [swap(): return lax.ppermute(x, 'parts', [(0, 1), (1, 0)])]
    concatenate x2 -> x1, local copies, waits for them, and re-layouts: 2.53 us -> 0.01 us  [ring_plan(): column = jnp.concatenate([own, a1[half:], a2[half:], a3[half:]], axis=0)]
    ppermute x8 -> x6, waiting for transfers between devices: 21.8 us -> 24.2 us  [send(): return lax.ppermute(x, 'store', pairs)]
    pallas_call x2, Pallas kernels: 9.42 us -> 7.37 us  [project(): pl.pallas_call(project_kernel, out_shape=[jax.ShapeDtypeStruct((2 * rows,...]
  transfers between devices with their start and end apart: 19 -> 22, of which waited for: 9 -> 10; matrix products, arithmetic and copies ran while one was open for 12% -> 7% of each run, Pallas kernels for 20% -> 22%
where the time goes in v2:
time: 92.6 us; the launch traced here: 92.1 us
  waiting for transfers between devices  30.6 us (33%)
  Pallas kernels  29.5 us (32%)
  starting transfers between devices  18.2 us (20%)
  local copies, waits for them, and re-layouts  10.9 us (12%)
  other arithmetic  2.52 us (3%)
    ppermute x6, waiting for transfers between devices, send(): return lax.ppermute(x, 'store', pairs)  24.2 us
    pallas_call x1, Pallas kernels, cached_attention(): pl.pallas_call(functools.partial(cached_kernel, per_dev), out_shape=[stat...  9.12 us
    pallas_call x1, Pallas kernels, fresh_attention(): pl.pallas_call(functools.partial(fresh_kernel, maxp), out_shape=jax.Shape...  9.04 us
    ppermute x6, starting transfers between devices, swap(): return lax.ppermute(x, 'parts', [(0, 1), (1, 0)])  8.47 us
    pallas_call x2, Pallas kernels, project(): pl.pallas_call(project_kernel, out_shape=[jax.ShapeDtypeStruct((2 * rows,...  7.37 us
    unnamed x28, local copies, waits for them, and re-layouts  5.4 us
    ppermute x6, starting transfers between devices, send(): return lax.ppermute(x, 'store', pairs)  4.93 us
    ppermute x10, starting transfers between devices, flip(): return lax.ppermute(x, 'store', pairs)  4.83 us
  transfers between devices with their start and end apart: 22, of which 10 were waited for; matrix products, arithmetic and copies ran while one was open for 7% of the time, Pallas kernels for 22%

profile of v2, /device:TPU:0, one launch (start us, length us, event | category | flops | bytes accessed | tf_op | source)
XLA Modules:
  0.0 92.1 jit_solution(13780567410802839497)
XLA Ops:
  0.0 0.9 %copy.26 = bf16[4,16,2,512]{3,1,0,2:T(8,128)(2,1)S(1)} copy(bf16[4,16,2,512]{3,2,1,0:T(2,128)(2,1)} %param.13) | data formatting | bytes 262144 | tf_op args[4]
  1.0 1.8 %constant_dynamic-slice_fusion.3 = (bf16[256,512]{1,0:T(8,128)(2,1)}, bf16[256,512]{1,0:T(8,128)(2,1)S(1)}) fusion(bf16[512,1024]{1,0:T(8,128)(2,1)} %refs_0_.3, s32[]{:T(128)S(6)} %select_n.127), kind=kLoop, calls=%fused_computation.71 | loop fusion | bytes 1048580 | tf_op jit(solution)/shard_map/dynamic_slice | solution.py:326
  2.8 3.1 %collective-permute-start.3 = (bf16[384,512]{1,0:T(8,128)(2,1)S(1)}, bf16[384,512]{1,0:T(8,128)(2,1)S(1)}, u32[]{:S(2)}, u32[]{:S(2)}) collective-permute-start(bf16[384,512]{1,0:T(8,128)(2,1)S(1)} %pad_maximum_fusion), channel_id=1, source_target_pairs={{0,4},{1,5},{2,6},{3,7},{4,8},{5,9},{6,10},{7,11},{8,12},{9,13},{1... | collective-permute-start | bytes 1179656 | tf_op jit(solution)/shard_map/ppermute | solution.py:36
  6.1 1.7 %copy-done.4 = bf16[4,40,8192]{2,1,0:T(8,128)(2,1)S(1)} copy-done((bf16[4,40,8192]{2,1,0:T(8,128)(2,1)S(1)}, bf16[4,40,8192]{2,1,0:T(8,128)(2,1)}, u32[]{:S(2)}) %copy-start.4) | copy-done | bytes 2621464
  7.8 4.0 %norm.1 = (bf16[160,2048]{1,0:T(8,128)(2,1)S(1)}, bf16[2,160,2048]{2,1,0:T(8,128)(2,1)}, bf16[160,2048]{1,0:T(8,128)(2,1)S(1)}) custom-call(s32[32]{0:T(128)S(1)} %and_select_fusion.7.offs_ref, bf16[160,8192]{1,0:T(8,128)(2,1)S(1)} %bitcast.18, bf16[1,8192]{1,0:T(2,128)(2,1)S(1)} %reshape.230.gain_ref), custom_call_target="tpu_custom_call" | custom-call | flops 7864320 | bytes 5242880 | tf_op jit(solution)/shard_map/norm/pallas_call | solution.py:71
  11.8 1.5 %collective-permute-start.1 = (bf16[320,2048]{1,0:T(8,128)(2,1)}, bf16[320,2048]{1,0:T(8,128)(2,1)}, u32[]{:S(2)}, u32[]{:S(2)}) collective-permute-start(bf16[320,2048]{1,0:T(8,128)(2,1)} %bitcast.4), channel_id=1, source_target_pairs={{0,2},{1,3},{2,0},{3,1},{4,6},{5,7},{6,4},{7,5},{8,10},{9,11},{10,... | collective-permute-start | bytes 3932168 | tf_op jit(solution)/shard_map/ppermute | solution.py:41
  13.3 1.6 %collective-permute-start.11 = (bf16[256,512]{1,0:T(8,128)(2,1)}, bf16[256,512]{1,0:T(8,128)(2,1)S(1)}, u32[]{:S(2)}, u32[]{:S(2)}) collective-permute-start(bf16[256,512]{1,0:T(8,128)(2,1)} %get-tuple-element.43), channel_id=1, source_target_pairs={{0,4},{1,5},{2,6},{3,7},{4,8},{5,9},{6,10},{7,11},{8,12},{9,13},{1... | collective-permute-start | bytes 786440 | tf_op jit(solution)/shard_map/ppermute | solution.py:36
  15.7 1.3 %collective-permute-done.3.refs_1_ = bf16[384,512]{1,0:T(8,128)(2,1)S(1)} collective-permute-done((bf16[384,512]{1,0:T(8,128)(2,1)S(1)}, bf16[384,512]{1,0:T(8,128)(2,1)S(1)}, u32[]{:S(2)}, u32[]{:S(2)}) %collective-permute-start.3) | collective-permute-done | bytes 393248 | tf_op jit(solution)/shard_map/ppermute | solution.py:36
  17.0 1.6 %collective-permute-start.4 = (bf16[256,512]{1,0:T(8,128)(2,1)S(1)}, bf16[256,512]{1,0:T(8,128)(2,1)S(1)}, u32[]{:S(2)}, u32[]{:S(2)}) collective-permute-start(bf16[256,512]{1,0:T(8,128)(2,1)S(1)} %slice.71), channel_id=1, source_target_pairs={{0,16},{16,0},{1,17},{17,1},{2,18},{18,2},{3,19},{19,3},{4,20},{20... | collective-permute-start | bytes 786440 | tf_op jit(solution)/shard_map/ppermute | solution.py:45
  18.9 5.6 %collective-permute-done.11.refs_1_ = bf16[256,512]{1,0:T(8,128)(2,1)S(1)} collective-permute-done((bf16[256,512]{1,0:T(8,128)(2,1)}, bf16[256,512]{1,0:T(8,128)(2,1)S(1)}, u32[]{:S(2)}, u32[]{:S(2)}) %collective-permute-start.11) | collective-permute-done | bytes 262176 | tf_op jit(solution)/shard_map/ppermute | solution.py:36
  24.5 1.5 %collective-permute-start.12 = (bf16[256,512]{1,0:T(8,128)(2,1)S(1)}, bf16[256,512]{1,0:T(8,128)(2,1)S(1)}, u32[]{:S(2)}, u32[]{:S(2)}) collective-permute-start(bf16[256,512]{1,0:T(8,128)(2,1)S(1)} %collective-permute-done.11.refs_1_), channel_id=1, source_target_pairs={{0,16},{16,0},{1,17},{17,1},{2,18},{18,2},{3,19},{19,3},{4,20},{20... | collective-permute-start | bytes 786440 | tf_op jit(solution)/shard_map/ppermute | solution.py:45
  26.0 6.9 %collective-permute-done.5.refs_3_ = bf16[384,512]{1,0:T(8,128)(2,1)S(1)} collective-permute-done((bf16[384,512]{1,0:T(8,128)(2,1)S(1)}, bf16[384,512]{1,0:T(8,128)(2,1)S(1)}, u32[]{:S(2)}, u32[]{:S(2)}) %collective-permute-start.5) | collective-permute-done | bytes 393248 | tf_op jit(solution)/shard_map/ppermute | solution.py:36
  32.9 1.6 %collective-permute-start.6 = (bf16[256,512]{1,0:T(8,128)(2,1)S(1)}, bf16[256,512]{1,0:T(8,128)(2,1)S(1)}, u32[]{:S(2)}, u32[]{:S(2)}) collective-permute-start(bf16[256,512]{1,0:T(8,128)(2,1)S(1)} %slice.72), channel_id=1, source_target_pairs={{0,16},{16,0},{1,17},{17,1},{2,18},{18,2},{3,19},{19,3},{4,20},{20... | collective-permute-start | bytes 786440 | tf_op jit(solution)/shard_map/ppermute | solution.py:45
  34.6 3.7 %collective-permute-done.13.refs_3_ = bf16[256,512]{1,0:T(8,128)(2,1)S(1)} collective-permute-done((bf16[256,512]{1,0:T(8,128)(2,1)S(1)}, bf16[256,512]{1,0:T(8,128)(2,1)S(1)}, u32[]{:S(2)}, u32[]{:S(2)}) %collective-permute-start.13) | collective-permute-done | bytes 262176 | tf_op jit(solution)/shard_map/ppermute | solution.py:36
  38.3 1.8 %collective-permute-start.14 = (bf16[256,512]{1,0:T(8,128)(2,1)S(1)}, bf16[256,512]{1,0:T(8,128)(2,1)S(1)}, u32[]{:S(2)}, u32[]{:S(2)}) collective-permute-start(bf16[256,512]{1,0:T(8,128)(2,1)S(1)} %collective-permute-done.13.refs_3_), channel_id=1, source_target_pairs={{0,16},{16,0},{1,17},{17,1},{2,18},{18,2},{3,19},{19,3},{4,20},{20... | collective-permute-start | bytes 786440 | tf_op jit(solution)/shard_map/ppermute | solution.py:45
  40.0 3.3 %collective-permute-done.1.a2 = bf16[320,2048]{1,0:T(8,128)(2,1)} collective-permute-done((bf16[320,2048]{1,0:T(8,128)(2,1)}, bf16[320,2048]{1,0:T(8,128)(2,1)}, u32[]{:S(2)}, u32[]{:S(2)}) %collective-permute-start.1) | collective-permute-done | bytes 1310752 | tf_op jit(solution)/shard_map/ppermute | solution.py:41
  43.3 1.1 %slice.70 = bf16[160,2048]{1,0:T(8,128)(2,1)S(1)} slice(bf16[320,2048]{1,0:T(8,128)(2,1)} %collective-permute-done.1.a2), slice={[160:320], [0:2048]} | slice | bytes 1310720 | tf_op jit(solution)/shard_map/slice | solution.py:357
  44.5 3.8 %collective-permute-done.7.refs_5_ = bf16[384,512]{1,0:T(8,128)(2,1)S(1)} collective-permute-done((bf16[384,512]{1,0:T(8,128)(2,1)S(1)}, bf16[384,512]{1,0:T(8,128)(2,1)S(1)}, u32[]{:S(2)}, u32[]{:S(2)}) %collective-permute-start.7) | collective-permute-done | bytes 393248 | tf_op jit(solution)/shard_map/ppermute | solution.py:36
  49.0 2.9 %collective-permute-done.15.refs_5_ = bf16[256,512]{1,0:T(8,128)(2,1)S(1)} collective-permute-done((bf16[256,512]{1,0:T(8,128)(2,1)S(1)}, bf16[256,512]{1,0:T(8,128)(2,1)S(1)}, u32[]{:S(2)}, u32[]{:S(2)}) %collective-permute-start.15) | collective-permute-done | bytes 262176 | tf_op jit(solution)/shard_map/ppermute | solution.py:36
  51.9 1.5 %collective-permute-start.16 = (bf16[256,512]{1,0:T(8,128)(2,1)S(1)}, bf16[256,512]{1,0:T(8,128)(2,1)S(1)}, u32[]{:S(2)}, u32[]{:S(2)}) collective-permute-start(bf16[256,512]{1,0:T(8,128)(2,1)S(1)} %collective-permute-done.15.refs_5_), channel_id=1, source_target_pairs={{0,16},{16,0},{1,17},{17,1},{2,18},{18,2},{3,19},{19,3},{4,20},{20... | collective-permute-start | bytes 786440 | tf_op jit(solution)/shard_map/ppermute | solution.py:45
  53.9 2.5 %collective-permute-done.8.refs_6_ = bf16[256,512]{1,0:T(8,128)(2,1)S(1)} collective-permute-done((bf16[256,512]{1,0:T(8,128)(2,1)S(1)}, bf16[256,512]{1,0:T(8,128)(2,1)S(1)}, u32[]{:S(2)}, u32[]{:S(2)}) %collective-permute-start.8) | collective-permute-done | bytes 262176 | tf_op jit(solution)/shard_map/ppermute | solution.py:45
  56.4 3.7 %project.2 = (f32[320,512]{1,0:T(8,128)S(1)}, bf16[320,512]{1,0:T(8,128)(2,1)}) custom-call(bf16[160,2048]{1,0:T(8,128)(2,1)S(1)} %get-tuple-element.25.a0, bf16[160,2048]{1,0:T(8,128)(2,1)S(1)} %collective-permute-done.a1, bf16[320,2048]{1,0:T(8,128)(2,1)} %collective-permute-done.1.a2, bf16[160,2048]{1,0:T(8,128)(2,1)S(1)} %collective-permute-done.2.a3, ...), custom_call_target="tpu_custom_call" | custom-call | flops 1342177280 | bytes 6684672 | tf_op jit(solution)/shard_map/project/pallas_call | solution.py:118
  60.4 3.7 %project.3 = (f32[320,512]{1,0:T(8,128)S(1)}, bf16[320,512]{1,0:T(8,128)(2,1)}) custom-call(bf16[160,2048]{1,0:T(8,128)(2,1)S(1)} %get-tuple-element.25.a0, bf16[160,2048]{1,0:T(8,128)(2,1)S(1)} %collective-permute-done.a1, bf16[320,2048]{1,0:T(8,128)(2,1)} %collective-permute-done.1.a2, bf16[160,2048]{1,0:T(8,128)(2,1)S(1)} %collective-permute-done.2.a3, ...), custom_call_target="tpu_custom_call" | custom-call | flops 1342177280 | bytes 6684672 | tf_op jit(solution)/shard_map/project/pallas_call | solution.py:118
  66.1 1.0 %add_convert_fusion.1 = (bf16[160,512]{1,0:T(8,128)(2,1)S(1)}, f32[160,512]{1,0:T(8,128)S(1)}) fusion(f32[320,512]{1,0:T(8,128)S(1)} %get-tuple-element.33, bf16[320,512]{1,0:T(8,128)(2,1)} %collective-permute-done.9), kind=kLoop, calls=%fused_computation.2 | loop fusion | flops 245760 | bytes 1310720 | tf_op jit(solution)/shard_map/convert_element_type | solution.py:369
  67.1 1.1 %collective-permute-start.10 = (bf16[160,512]{1,0:T(8,128)(2,1)S(1)}, bf16[160,512]{1,0:T(8,128)(2,1)S(1)}, u32[]{:S(2)}, u32[]{:S(2)}) collective-permute-start(bf16[160,512]{1,0:T(8,128)(2,1)S(1)} %get-tuple-element.47), channel_id=1, source_target_pairs={{0,2},{1,3},{2,0},{3,1},{4,6},{5,7},{6,4},{7,5},{8,10},{9,11},{10,... | collective-permute-start | bytes 491528 | tf_op jit(solution)/shard_map/ppermute | solution.py:41
  68.2 1.0 %add_convert_fusion = (bf16[160,512]{1,0:T(8,128)(2,1)S(1)}, f32[160,512]{1,0:T(8,128)S(1)}) fusion(f32[320,512]{1,0:T(8,128)S(1)} %copy-done.6, bf16[320,512]{1,0:T(8,128)(2,1)} %collective-permute-done.17), kind=kLoop, calls=%fused_computation.1 | loop fusion | flops 245760 | bytes 1310720 | tf_op jit(solution)/shard_map/convert_element_type | solution.py:369
  69.2 1.0 %collective-permute-start.18 = (bf16[160,512]{1,0:T(8,128)(2,1)S(1)}, bf16[160,512]{1,0:T(8,128)(2,1)S(1)}, u32[]{:S(2)}, u32[]{:S(2)}) collective-permute-start(bf16[160,512]{1,0:T(8,128)(2,1)S(1)} %get-tuple-element.45), channel_id=1, source_target_pairs={{0,2},{1,3},{2,0},{3,1},{4,6},{5,7},{6,4},{7,5},{8,10},{9,11},{10,... | collective-permute-start | bytes 491528 | tf_op jit(solution)/shard_map/ppermute | solution.py:41
  70.3 0.9 %slice.74 = bf16[160,512]{1,0:T(8,128)(2,1)S(1)} slice(bf16[320,512]{1,0:T(8,128)(2,1)} %collective-permute-done.9), slice={[0:160], [0:512]} | slice | bytes 327680 | tf_op jit(solution)/shard_map/slice | solution.py:370
  71.2 0.9 %slice.76 = bf16[160,512]{1,0:T(8,128)(2,1)S(1)} slice(bf16[320,512]{1,0:T(8,128)(2,1)} %collective-permute-done.17), slice={[0:160], [0:512]} | slice | bytes 327680 | tf_op jit(solution)/shard_map/slice | solution.py:370
  72.2 9.1 %cached_attention.1 = (f32[4,4,320,128]{3,2,1,0:T(8,128)}, f32[4,4,320,128]{3,2,1,0:T(8,128)}) custom-call(s32[16]{0:T(128)S(1)} %fusion.7.place_ref, s32[64]{0:T(128)S(1)} %copy-done.8, s32[4,20]{1,0:T(4,128)S(1)} %copy.31.ids_ref, bf16[4,40,4096]{2,1,0:T(8,128)(2,1)S(1)} %copy-done.2, bf16[512,512]{1,0:T(8,128)(2,1)S(1)} %slice_dynamic-update-slice_fusion.refs_0_, ...), custom_call_target="tpu_custom_call" | custom-call | flops 838860800 | bytes 8650752 | tf_op jit(solution)/shard_map/cached_attention/pallas_call | solution.py:200
  81.3 1.7 %copy-done.3 = f32[4,4,320,128]{3,2,1,0:T(8,128)S(1)} copy-done((f32[4,4,320,128]{3,2,1,0:T(8,128)S(1)}, f32[4,4,320,128]{3,2,1,0:T(8,128)}, u32[]{:S(2)}) %copy-start.3) | copy-done | bytes 2621464
  83.1 9.0 %fresh_attention.1 = bf16[4,40,4096]{2,1,0:T(8,128)(2,1)} custom-call(s32[4]{0:T(128)S(1)} %copy-done.7, bf16[4,40,4096]{2,1,0:T(8,128)(2,1)S(1)} %copy-done.2, f32[4,40,512]{2,1,0:T(8,128)S(1)} %bitcast.19, bf16[4,40,512]{2,1,0:T(8,128)(2,1)S(1)} %bitcast.21, bf16[4,40,512]{2,1,0:T(8,128)(2,1)S(1)} %bitcast.23, f32[4,40,512]{2,1,0:T(8,128)S(1)} %bitcast.20, ...), custom_call_target="tpu_custom_call" | custom-call | flops 104857600 | bytes 7864320 | tf_op jit(solution)/shard_map/fresh_attention/pallas_call | solution.py:270
  (79 shorter events, 5.0 us)
Async XLA Ops:
  0.0 14.9 %copy-start = (s32[64,20,2]{0,2,1:T(2,128)S(1)}, s32[64,20,2]{0,2,1:T(2,128)}, u32[]{:S(2)}) copy-start(s32[64,20,2]{0,2,1:T(2,128)} %param.17) | copy-start | bytes 30724
  0.0 6.1 %copy-start.9 = (bf16[8192]{0:T(1024)(128)(2,1)S(1)}, bf16[8192]{0:T(1024)(128)(2,1)}, u32[]{:S(2)}) copy-start(bf16[8192]{0:T(1024)(128)(2,1)} %param.10) | copy-start | bytes 49156
  2.8 14.2 %collective-permute-start.3 = (bf16[384,512]{1,0:T(8,128)(2,1)S(1)}, bf16[384,512]{1,0:T(8,128)(2,1)S(1)}, u32[]{:S(2)}, u32[]{:S(2)}) collective-permute-start(bf16[384,512]{1,0:T(8,128)(2,1)S(1)} %pad_maximum_fusion), channel_id=1, source_target_pairs={{0,4},{1,5},{2,6},{3,7},{4,8},{5,9},{6,10},{7,11},{8,12},{9,13},{1... | collective-permute-start | bytes 1179656 | tf_op jit(solution)/shard_map/ppermute | solution.py:36
  6.1 1.7 %copy-start.4 = (bf16[4,40,8192]{2,1,0:T(8,128)(2,1)S(1)}, bf16[4,40,8192]{2,1,0:T(8,128)(2,1)}, u32[]{:S(2)}) copy-start(bf16[4,40,8192]{2,1,0:T(8,128)(2,1)} %param.9) | copy-start | bytes 7864324
  7.8 7.6 %copy-start.7 = (s32[4]{0:T(128)S(1)}, s32[4]{0:T(128)}, u32[]{:S(2)}) copy-start(s32[4]{0:T(128)} %count_ref.1) | copy-start | bytes 52
  11.8 5.2 %collective-permute-start = (bf16[160,2048]{1,0:T(8,128)(2,1)S(1)}, bf16[160,2048]{1,0:T(8,128)(2,1)S(1)}, u32[]{:S(2)}, u32[]{:S(2)}) collective-permute-start(bf16[160,2048]{1,0:T(8,128)(2,1)S(1)} %get-tuple-element.26), channel_id=1, source_target_pairs={{0,1},{1,0},{2,3},{3,2},{4,5},{5,4},{6,7},{7,6},{8,9},{9,8},{10,11... | collective-permute-start | bytes 1966088 | tf_op jit(solution)/shard_map/ppermute | solution.py:41
  11.8 31.5 %collective-permute-start.1 = (bf16[320,2048]{1,0:T(8,128)(2,1)}, bf16[320,2048]{1,0:T(8,128)(2,1)}, u32[]{:S(2)}, u32[]{:S(2)}) collective-permute-start(bf16[320,2048]{1,0:T(8,128)(2,1)} %bitcast.4), channel_id=1, source_target_pairs={{0,2},{1,3},{2,0},{3,1},{4,6},{5,7},{6,4},{7,5},{8,10},{9,11},{10,... | collective-permute-start | bytes 3932168 | tf_op jit(solution)/shard_map/ppermute | solution.py:41
  13.3 11.1 %collective-permute-start.11 = (bf16[256,512]{1,0:T(8,128)(2,1)}, bf16[256,512]{1,0:T(8,128)(2,1)S(1)}, u32[]{:S(2)}, u32[]{:S(2)}) collective-permute-start(bf16[256,512]{1,0:T(8,128)(2,1)} %get-tuple-element.43), channel_id=1, source_target_pairs={{0,4},{1,5},{2,6},{3,7},{4,8},{5,9},{6,10},{7,11},{8,12},{9,13},{1... | collective-permute-start | bytes 786440 | tf_op jit(solution)/shard_map/ppermute | solution.py:36
  17.0 15.9 %collective-permute-start.4 = (bf16[256,512]{1,0:T(8,128)(2,1)S(1)}, bf16[256,512]{1,0:T(8,128)(2,1)S(1)}, u32[]{:S(2)}, u32[]{:S(2)}) collective-permute-start(bf16[256,512]{1,0:T(8,128)(2,1)S(1)} %slice.71), channel_id=1, source_target_pairs={{0,16},{16,0},{1,17},{17,1},{2,18},{18,2},{3,19},{19,3},{4,20},{20... | collective-permute-start | bytes 786440 | tf_op jit(solution)/shard_map/ppermute | solution.py:45
  18.6 14.3 %collective-permute-start.5 = (bf16[384,512]{1,0:T(8,128)(2,1)S(1)}, bf16[384,512]{1,0:T(8,128)(2,1)S(1)}, u32[]{:S(2)}, u32[]{:S(2)}) collective-permute-start(bf16[384,512]{1,0:T(8,128)(2,1)S(1)} %collective-permute-done.3.refs_1_), channel_id=1, source_target_pairs={{0,4},{1,5},{2,6},{3,7},{4,8},{5,9},{6,10},{7,11},{8,12},{9,13},{1... | collective-permute-start | bytes 1179656 | tf_op jit(solution)/shard_map/ppermute | solution.py:36
  24.5 10.1 %collective-permute-start.12 = (bf16[256,512]{1,0:T(8,128)(2,1)S(1)}, bf16[256,512]{1,0:T(8,128)(2,1)S(1)}, u32[]{:S(2)}, u32[]{:S(2)}) collective-permute-start(bf16[256,512]{1,0:T(8,128)(2,1)S(1)} %collective-permute-done.11.refs_1_), channel_id=1, source_target_pairs={{0,16},{16,0},{1,17},{17,1},{2,18},{18,2},{3,19},{19,3},{4,20},{20... | collective-permute-start | bytes 786440 | tf_op jit(solution)/shard_map/ppermute | solution.py:45
  26.0 12.3 %collective-permute-start.13 = (bf16[256,512]{1,0:T(8,128)(2,1)S(1)}, bf16[256,512]{1,0:T(8,128)(2,1)S(1)}, u32[]{:S(2)}, u32[]{:S(2)}) collective-permute-start(bf16[256,512]{1,0:T(8,128)(2,1)S(1)} %collective-permute-done.11.refs_1_), channel_id=1, source_target_pairs={{0,4},{1,5},{2,6},{3,7},{4,8},{5,9},{6,10},{7,11},{8,12},{9,13},{1... | collective-permute-start | bytes 786440 | tf_op jit(solution)/shard_map/ppermute | solution.py:36
  32.9 15.4 %collective-permute-start.6 = (bf16[256,512]{1,0:T(8,128)(2,1)S(1)}, bf16[256,512]{1,0:T(8,128)(2,1)S(1)}, u32[]{:S(2)}, u32[]{:S(2)}) collective-permute-start(bf16[256,512]{1,0:T(8,128)(2,1)S(1)} %slice.72), channel_id=1, source_target_pairs={{0,16},{16,0},{1,17},{17,1},{2,18},{18,2},{3,19},{19,3},{4,20},{20... | collective-permute-start | bytes 786440 | tf_op jit(solution)/shard_map/ppermute | solution.py:45
  34.5 13.8 %collective-permute-start.7 = (bf16[384,512]{1,0:T(8,128)(2,1)S(1)}, bf16[384,512]{1,0:T(8,128)(2,1)S(1)}, u32[]{:S(2)}, u32[]{:S(2)}) collective-permute-start(bf16[384,512]{1,0:T(8,128)(2,1)S(1)} %collective-permute-done.5.refs_3_), channel_id=1, source_target_pairs={{0,4},{1,5},{2,6},{3,7},{4,8},{5,9},{6,10},{7,11},{8,12},{9,13},{1... | collective-permute-start | bytes 1179656 | tf_op jit(solution)/shard_map/ppermute | solution.py:36
  34.6 21.9 %copy-start.1 = (bf16[512,1024]{1,0:T(8,128)(2,1)S(1)}, bf16[512,1024]{1,0:T(8,128)(2,1)}, u32[]{:S(2)}) copy-start(bf16[512,1024]{1,0:T(8,128)(2,1)} %refs_0_.3) | copy-start | bytes 3145732
  38.3 10.7 %collective-permute-start.14 = (bf16[256,512]{1,0:T(8,128)(2,1)S(1)}, bf16[256,512]{1,0:T(8,128)(2,1)S(1)}, u32[]{:S(2)}, u32[]{:S(2)}) collective-permute-start(bf16[256,512]{1,0:T(8,128)(2,1)S(1)} %collective-permute-done.13.refs_3_), channel_id=1, source_target_pairs={{0,16},{16,0},{1,17},{17,1},{2,18},{18,2},{3,19},{19,3},{4,20},{20... | collective-permute-start | bytes 786440 | tf_op jit(solution)/shard_map/ppermute | solution.py:45
  40.0 11.8 %collective-permute-start.15 = (bf16[256,512]{1,0:T(8,128)(2,1)S(1)}, bf16[256,512]{1,0:T(8,128)(2,1)S(1)}, u32[]{:S(2)}, u32[]{:S(2)}) collective-permute-start(bf16[256,512]{1,0:T(8,128)(2,1)S(1)} %collective-permute-done.13.refs_3_), channel_id=1, source_target_pairs={{0,4},{1,5},{2,6},{3,7},{4,8},{5,9},{6,10},{7,11},{8,12},{9,13},{1... | collective-permute-start | bytes 786440 | tf_op jit(solution)/shard_map/ppermute | solution.py:36
  44.4 12.0 %collective-permute-start.2 = (bf16[160,2048]{1,0:T(8,128)(2,1)S(1)}, bf16[160,2048]{1,0:T(8,128)(2,1)S(1)}, u32[]{:S(2)}, u32[]{:S(2)}) collective-permute-start(bf16[160,2048]{1,0:T(8,128)(2,1)S(1)} %slice.70), channel_id=1, source_target_pairs={{0,1},{1,0},{2,3},{3,2},{4,5},{5,4},{6,7},{7,6},{8,9},{9,8},{10,11... | collective-permute-start | bytes 1966088 | tf_op jit(solution)/shard_map/ppermute | solution.py:41
  48.4 8.0 %collective-permute-start.8 = (bf16[256,512]{1,0:T(8,128)(2,1)S(1)}, bf16[256,512]{1,0:T(8,128)(2,1)S(1)}, u32[]{:S(2)}, u32[]{:S(2)}) collective-permute-start(bf16[256,512]{1,0:T(8,128)(2,1)S(1)} %slice.73), channel_id=1, source_target_pairs={{0,16},{16,0},{1,17},{17,1},{2,18},{18,2},{3,19},{19,3},{4,20},{20... | collective-permute-start | bytes 786440 | tf_op jit(solution)/shard_map/ppermute | solution.py:45
  51.9 8.6 %collective-permute-start.16 = (bf16[256,512]{1,0:T(8,128)(2,1)S(1)}, bf16[256,512]{1,0:T(8,128)(2,1)S(1)}, u32[]{:S(2)}, u32[]{:S(2)}) collective-permute-start(bf16[256,512]{1,0:T(8,128)(2,1)S(1)} %collective-permute-done.15.refs_5_), channel_id=1, source_target_pairs={{0,16},{16,0},{1,17},{17,1},{2,18},{18,2},{3,19},{19,3},{4,20},{20... | collective-permute-start | bytes 786440 | tf_op jit(solution)/shard_map/ppermute | solution.py:45
  53.4 12.7 %collective-permute-start.19 = (bf16[512,512]{1,0:T(8,128)(2,1)S(1)}, bf16[512,512]{1,0:T(8,128)(2,1)}, u32[]{:S(2)}, u32[]{:S(2)}) collective-permute-start(bf16[512,512]{1,0:T(8,128)(2,1)S(1)} %slice_dynamic-update-slice_fusion.refs_0_), channel_id=1, source_target_pairs={{0,2},{1,3},{2,0},{3,1},{4,6},{5,7},{6,4},{7,5},{8,10},{9,11},{10,... | collective-permute-start | bytes 1572872 | tf_op jit(solution)/shard_map/ppermute | solution.py:41
  60.1 5.9 %collective-permute-start.9 = (bf16[320,512]{1,0:T(8,128)(2,1)}, bf16[320,512]{1,0:T(8,128)(2,1)}, u32[]{:S(2)}, u32[]{:S(2)}) collective-permute-start(bf16[320,512]{1,0:T(8,128)(2,1)} %get-tuple-element.34), channel_id=1, source_target_pairs={{0,1},{1,0},{2,3},{3,2},{4,5},{5,4},{6,7},{7,6},{8,9},{9,8},{10,11... | collective-permute-start | bytes 983048 | tf_op jit(solution)/shard_map/ppermute | solution.py:41
  60.2 5.1 %copy-start.10 = (s32[64,20]{0,1:T(8,128)S(1)}, s32[64,20]{0,1:T(8,128)}, u32[]{:S(2)}) copy-start(s32[64,20]{0,1:T(8,128)} %param.15) | copy-start | bytes 15364
  64.9 3.3 %copy-start.6 = (f32[320,512]{1,0:T(8,128)S(1)}, f32[320,512]{1,0:T(8,128)}, u32[]{:S(2)}) copy-start(f32[320,512]{1,0:T(8,128)} %copy-done.5) | copy-start | bytes 1966084
  64.9 3.3 %collective-permute-start.17 = (bf16[320,512]{1,0:T(8,128)(2,1)}, bf16[320,512]{1,0:T(8,128)(2,1)}, u32[]{:S(2)}, u32[]{:S(2)}) collective-permute-start(bf16[320,512]{1,0:T(8,128)(2,1)} %get-tuple-element.39), channel_id=1, source_target_pairs={{0,1},{1,0},{2,3},{3,2},{4,5},{5,4},{6,7},{7,6},{8,9},{9,8},{10,11... | collective-permute-start | bytes 983048 | tf_op jit(solution)/shard_map/ppermute | solution.py:41
  65.5 6.7 %collective-permute-start.20 = (bf16[512,512]{1,0:T(8,128)(2,1)S(1)}, bf16[512,512]{1,0:T(8,128)(2,1)S(1)}, u32[]{:S(2)}, u32[]{:S(2)}) collective-permute-start(bf16[512,512]{1,0:T(8,128)(2,1)S(1)} %slice_dynamic-update-slice_fusion.refs_0_), channel_id=1, source_target_pairs={{0,1},{1,0},{2,3},{3,2},{4,5},{5,4},{6,7},{7,6},{8,9},{9,8},{10,11... | collective-permute-start | bytes 1572872 | tf_op jit(solution)/shard_map/ppermute | solution.py:41
  66.1 6.1 %collective-permute-start.21 = (bf16[512,512]{1,0:T(8,128)(2,1)}, bf16[512,512]{1,0:T(8,128)(2,1)S(1)}, u32[]{:S(2)}, u32[]{:S(2)}) collective-permute-start(bf16[512,512]{1,0:T(8,128)(2,1)} %collective-permute-done.19.refs_1_), channel_id=1, source_target_pairs={{0,1},{1,0},{2,3},{3,2},{4,5},{5,4},{6,7},{7,6},{8,9},{9,8},{10,11... | collective-permute-start | bytes 1572872 | tf_op jit(solution)/shard_map/ppermute | solution.py:41
  67.1 5.1 %copy-start.2 = (bf16[4,40,4096]{2,1,0:T(8,128)(2,1)S(1)}, bf16[4,40,4096]{2,1,0:T(8,128)(2,1)}, u32[]{:S(2)}) copy-start(bf16[4,40,4096]{2,1,0:T(8,128)(2,1)} %q_ref.3) | copy-start | bytes 3932164
  67.1 5.1 %copy-start.8 = (s32[64]{0:T(128)S(1)}, s32[64]{0:T(128)}, u32[]{:S(2)}) copy-start(s32[64]{0:T(128)} %home_ref.1) | copy-start | bytes 772
  67.1 14.2 %collective-permute-start.10 = (bf16[160,512]{1,0:T(8,128)(2,1)S(1)}, bf16[160,512]{1,0:T(8,128)(2,1)S(1)}, u32[]{:S(2)}, u32[]{:S(2)}) collective-permute-start(bf16[160,512]{1,0:T(8,128)(2,1)S(1)} %get-tuple-element.47), channel_id=1, source_target_pairs={{0,2},{1,3},{2,0},{3,1},{4,6},{5,7},{6,4},{7,5},{8,10},{9,11},{10,... | collective-permute-start | bytes 491528 | tf_op jit(solution)/shard_map/ppermute | solution.py:41
  69.2 12.1 %collective-permute-start.18 = (bf16[160,512]{1,0:T(8,128)(2,1)S(1)}, bf16[160,512]{1,0:T(8,128)(2,1)S(1)}, u32[]{:S(2)}, u32[]{:S(2)}) collective-permute-start(bf16[160,512]{1,0:T(8,128)(2,1)S(1)} %get-tuple-element.45), channel_id=1, source_target_pairs={{0,2},{1,3},{2,0},{3,1},{4,6},{5,7},{6,4},{7,5},{8,10},{9,11},{10,... | collective-permute-start | bytes 491528 | tf_op jit(solution)/shard_map/ppermute | solution.py:41
  81.3 1.7 %copy-start.3 = (f32[4,4,320,128]{3,2,1,0:T(8,128)S(1)}, f32[4,4,320,128]{3,2,1,0:T(8,128)}, u32[]{:S(2)}) copy-start(f32[4,4,320,128]{3,2,1,0:T(8,128)} %get-tuple-element.41.part_ref) | copy-start | bytes 7864324
  (1 other events, 0.8 us)

commit v3 on v2

--- a/solution.py
+++ b/solution.py
@@ -14,8 +14,9 @@
 HEAD_GROUP = QUERY_HEADS // KEY_VALUE_HEADS
 GROUP = 4
 HIDDEN = -1e30
+NEVER = 1 << 30
 EXP2_SCALE = math.log2(math.e) / math.sqrt(HEAD_SIZE)
-VMEM_LIMIT = 48 * 2**20
+VMEM_LIMIT = 16 * 2**20
 
 
 def params(**more):
@@ -136,23 +137,23 @@
     )(*acts, own, *weights)
 
 
-def stacked_queries(q_ref, head):
-    parts = []
+def by_request(*shape):
+    return pl.BlockSpec((1, *shape), lambda r: (r,) + (0,) * len(shape))
+
+
+def against(a, b, dims):
+    return lax.dot_general(a, b, (dims, ((), ())), preferred_element_type=jnp.float32)
+
+def stacked_queries(q_ref, group):
+    heads = []
     for i in range(HEAD_GROUP):
-        at = (head * HEAD_GROUP + i) * HEAD_SIZE
-        parts.append(q_ref[0, :, at : at + HEAD_SIZE].astype(jnp.float32))
-    return jnp.concatenate(parts, axis=0).astype(jnp.bfloat16)
-
-
-def scores_of(q, keys, bias):
-    s = lax.dot_general(q, keys, (((1,), (1,)), ((), ())), preferred_element_type=jnp.float32)
-    rows, cols = bias.shape
-    s = (s * EXP2_SCALE).reshape(HEAD_GROUP, rows, cols) + bias[None]
-    return s.reshape(HEAD_GROUP * rows, cols)
-
-
-def cached_kernel(per_dev, place_ref, home_ref, ids_ref, q_ref, *refs):
-    sources, (bias_ref, out_ref, stat_ref, pages, context, sems) = refs[:-6], refs[-6:]
+        at = (group * HEAD_GROUP + i) * HEAD_SIZE
+        heads.append(q_ref[0, :, at : at + HEAD_SIZE].astype(jnp.float32))
+    return jnp.concatenate(heads, axis=0).astype(jnp.bfloat16)
+
+
+def cached_kernel(per_dev, place_ref, home_ref, ids_ref, rows_ref, count_ref, q_ref, *refs):
+    sources, (query_pos_ref, out_ref, stat_ref, stacked_ref, pages, context, bias, sems) = refs[:-8], refs[-8:]
     r = pl.program_id(0)
     maxp = ids_ref.shape[1]
     plen = context.shape[1] // maxp
@@ -176,140 +177,148 @@
         for c in range(2):
             at = pl.multiple_of((block + c * per_dev) * plen, plen)
             context[c, m * plen : (m + 1) * plen, :] = pages[pl.ds(at, plen), :]
-    bias = bias_ref[0]
-    lane = lax.broadcasted_iota(jnp.int32, (HEAD_GROUP * bias.shape[0], HEAD_SIZE), 1)
+    per_pass = rows_ref.shape[1] // maxp
+    row = lax.broadcasted_iota(jnp.int32, (plen, bias.shape[1]), 0)
+    for m in range(maxp):
+        hidden = m >= count_ref[r]
+        for i in range(per_pass):
+            hidden = hidden | (row == rows_ref[r, m * per_pass + i])
+        key_pos = jnp.where(hidden, NEVER, row + m * plen)
+        bias[m * plen : (m + 1) * plen, :] = jnp.where(key_pos <= query_pos_ref[0], 0.0, HIDDEN)
     for g in range(KEY_VALUE_HEADS):
-        q = stacked_queries(q_ref, g)
         keys = context[0, :, g * HEAD_SIZE : (g + 1) * HEAD_SIZE]
         values = context[1, :, g * HEAD_SIZE : (g + 1) * HEAD_SIZE]
-        s = scores_of(q, keys, bias)
-        top = jnp.max(s, axis=-1, keepdims=True)
+        q = stacked_queries(q_ref, g)
+        stacked_ref[0, g] = q
+        s = against(keys, q, ((1,), (1,))) * EXP2_SCALE + bias[...]
+        top = jnp.max(s, axis=0, keepdims=True)
         e = jnp.exp2(s - top)
-        total = jnp.sum(e, axis=-1, keepdims=True)
-        out_ref[0, g] = dot(e.astype(jnp.bfloat16), values)
-        stat_ref[0, g] = jnp.where(lane < HEAD_SIZE // 2, top, total)
-
-
-def cached_attention(per_dev, place, home, ids, sources, queries, bias):
-    owned, rows, width = queries.shape
-    context = bias.shape[2]
+        stat_ref[0, g, 0:1] = top
+        stat_ref[0, g, 1:2] = jnp.sum(e, axis=0, keepdims=True)
+        out_ref[0, g] = against(values, e.astype(jnp.bfloat16), ((0,), (0,)))
+
+
+def cached_attention(per_dev, plen, place, home, ids, sources, rows, count, queries, query_pos):
+    owned, selected, width = queries.shape
+    stacked = HEAD_GROUP * selected
+    context = ids.shape[1] * plen
     features = sources[0].shape[1]
-    stacked = HEAD_GROUP * rows
-    state = jax.ShapeDtypeStruct((owned, KEY_VALUE_HEADS, stacked, HEAD_SIZE), jnp.float32)
-    state_spec = pl.BlockSpec((1, KEY_VALUE_HEADS, stacked, HEAD_SIZE), lambda r: (r, 0, 0, 0))
+    heads = KEY_VALUE_HEADS
     return pl.pallas_call(
         functools.partial(cached_kernel, per_dev),
-        out_shape=[state, state],
+        out_shape=[
+            jax.ShapeDtypeStruct((owned, heads, HEAD_SIZE, stacked), jnp.float32),
+            jax.ShapeDtypeStruct((owned, heads, 2, stacked), jnp.float32),
+            jax.ShapeDtypeStruct((owned, heads, stacked, HEAD_SIZE), jnp.bfloat16),
+        ],
         grid=(owned,),
         in_specs=[
-            smem(),
-            smem(),
-            smem(),
-            pl.BlockSpec((1, rows, width), lambda r: (r, 0, 0)),
+            *[smem()] * 5,
+            by_request(selected, width),
             *[pl.BlockSpec(memory_space=pl.ANY)] * len(sources),
-            pl.BlockSpec((1, rows, context), lambda r: (r, 0, 0)),
-        ],
-        out_specs=[state_spec, state_spec],
+            by_request(1, stacked),
+        ],
+        out_specs=[
+            by_request(heads, HEAD_SIZE, stacked),
+            by_request(heads, 2, stacked),
+            by_request(heads, stacked, HEAD_SIZE),
+        ],
         scratch_shapes=[
             pltpu.VMEM((sum(x.shape[0] for x in sources), features), jnp.bfloat16),
             pltpu.VMEM((2, context, features), jnp.bfloat16),
+            pltpu.VMEM((context, stacked), jnp.float32),
             pltpu.SemaphoreType.DMA((len(sources),)),
         ],
         compiler_params=params(),
         cost_estimate=pl.CostEstimate(
-            flops=4 * owned * rows * width * context,
-            bytes_accessed=8 * sources[0].size + 2 * queries.size + 8 * owned * stacked * 4 * HEAD_SIZE,
-            transcendentals=owned * rows * QUERY_HEADS * context,
+            flops=4 * queries.size * context,
+            bytes_accessed=4 * queries.size + 8 * sources[0].size,
+            transcendentals=owned * heads * stacked * context,
         ),
         name="cached_attention",
-    )(place, home, ids, queries, *sources, bias)
-
-
-def added(own_ref, core_ref, y_ref):
-    total = own_ref[0] + core_ref[0].astype(jnp.float32) + y_ref[0].astype(jnp.float32)
+    )(place, home, ids, rows, count, queries, *sources, query_pos)
+
+
+def added(own_ref, *others):
+    total = own_ref[0]
+    for other in others:
+        total = total + other[0].astype(jnp.float32)
     return total.astype(jnp.bfloat16)
 
 
 def fresh_kernel(
-    maxp, count_ref, q_ref, ko_ref, kc_ref, ky_ref, vo_ref, vc_ref, vy_ref, bias_ref, part_ref,
-    stat_ref, out_ref,
+    maxp, count_ref, q_ref, k0, k1, k2, v0, v1, v2, query_pos_ref, part_ref, stat_ref, out_ref,
 ):
     r = pl.program_id(0)
-    fresh_keys = added(ko_ref, kc_ref, ky_ref)
-    fresh_values = added(vo_ref, vc_ref, vy_ref)
-    bias = bias_ref[0]
-    rows = bias.shape[0]
+    fresh_keys = added(k0, k1, k2)
+    fresh_values = added(v0, v1, v2)
+    rows = fresh_keys.shape[0]
     per_pass = rows // maxp
     slot = lax.broadcasted_iota(jnp.int32, (rows, HEAD_SIZE), 0) // per_pass
     live = slot < count_ref[r]
+    across = jnp.broadcast_to(query_pos_ref[0, :, :HEAD_SIZE], (HEAD_SIZE, HEAD_SIZE))
+    key_pos = jnp.where(live, across.T[:rows], NEVER)[:, :1]
+    bias = jnp.where(key_pos <= query_pos_ref[0], 0.0, HIDDEN)
     for g in range(KEY_VALUE_HEADS):
-        q = stacked_queries(q_ref, g)
         keys = fresh_keys[:, g * HEAD_SIZE : (g + 1) * HEAD_SIZE]
         values = fresh_values[:, g * HEAD_SIZE : (g + 1) * HEAD_SIZE]
-        s = scores_of(q, keys, bias)
-        top1 = stat_ref[0, g, :, 0:1]
-        sum1 = stat_ref[0, g, :, HEAD_SIZE // 2 : HEAD_SIZE // 2 + 1]
-        top = jnp.maximum(top1, jnp.max(s, axis=-1, keepdims=True))
+        s = against(keys, q_ref[0, g], ((1,), (1,))) * EXP2_SCALE + bias
+        top1 = stat_ref[0, g, 0:1]
+        top = jnp.maximum(top1, jnp.max(s, axis=0, keepdims=True))
         e = jnp.exp2(s - top)
         keep = jnp.exp2(top1 - top)
-        inv = 1.0 / (sum1 * keep + jnp.sum(e, axis=-1, keepdims=True))
-        result = (part_ref[0, g] * keep + dot(e.astype(jnp.bfloat16), values)) * inv
+        inv = 1.0 / (stat_ref[0, g, 1:2] * keep + jnp.sum(e, axis=0, keepdims=True))
+        term = against(values, e.astype(jnp.bfloat16), ((0,), (0,)))
+        result = ((part_ref[0, g] * keep + term) * inv).T
         for i in range(HEAD_GROUP):
             at = (g * HEAD_GROUP + i) * HEAD_SIZE
             one = result[i * rows : (i + 1) * rows]
             out_ref[0, :, at : at + HEAD_SIZE] = jnp.where(live, one, 0.0).astype(jnp.bfloat16)
 
 
-def fresh_attention(maxp, count, queries, terms, bias, part, stat):
-    owned, rows, width = queries.shape
-    features = terms[0].shape[-1]
-    stacked = HEAD_GROUP * rows
-    state_spec = pl.BlockSpec((1, KEY_VALUE_HEADS, stacked, HEAD_SIZE), lambda r: (r, 0, 0, 0))
-    row_spec = pl.BlockSpec((1, rows, features), lambda r: (r, 0, 0))
-    query_spec = pl.BlockSpec((1, rows, width), lambda r: (r, 0, 0))
+def fresh_attention(maxp, count, queries, terms, query_pos, part, stat):
+    owned, heads, stacked, _ = queries.shape
+    rows, features = terms[0].shape[1:]
+    width = QUERY_HEADS * HEAD_SIZE
     return pl.pallas_call(
         functools.partial(fresh_kernel, maxp),
-        out_shape=jax.ShapeDtypeStruct(queries.shape, jnp.bfloat16),
+        out_shape=jax.ShapeDtypeStruct((owned, rows, width), jnp.bfloat16),
         grid=(owned,),
         in_specs=[
             smem(),
-            query_spec,
-            *[row_spec] * 6,
-            pl.BlockSpec((1, rows, rows), lambda r: (r, 0, 0)),
-            state_spec,
-            state_spec,
-        ],
-        out_specs=query_spec,
+            by_request(heads, stacked, HEAD_SIZE),
+            *[by_request(rows, features)] * 6,
+            by_request(1, stacked),
+            by_request(heads, HEAD_SIZE, stacked),
+            by_request(heads, 2, stacked),
+        ],
+        out_specs=by_request(rows, width),
         compiler_params=params(),
         cost_estimate=pl.CostEstimate(
-            flops=4 * owned * rows * width * rows,
-            bytes_accessed=4 * queries.size + 8 * part.size,
-            transcendentals=owned * rows * QUERY_HEADS * rows,
+            flops=4 * queries.size * rows,
+            bytes_accessed=8 * queries.size,
+            transcendentals=owned * heads * stacked * rows,
         ),
         name="fresh_attention",
-    )(count, queries, *terms, bias, part, stat)
-
-
-def masks(rows, count, plen):
+    )(count, queries, *terms, query_pos, part, stat)
+
+
+def query_positions(rows, plen):
     owned, maxp, per_pass = rows.shape
-    selected = maxp * per_pass
-    touched = jnp.any(rows[..., None] == jnp.arange(plen, dtype=jnp.int32), axis=2)
-    touched = touched.reshape(owned, 1, maxp * plen)
-    key_pos = jnp.arange(maxp * plen, dtype=jnp.int32)
-    slot = jnp.arange(selected, dtype=jnp.int32) // per_pass
-    query_pos = slot * plen + rows.reshape(owned, selected)
-    seen = (key_pos // plen < count[:, None, None]) & (key_pos <= query_pos[:, :, None])
-    cached_bias = jnp.where(seen & ~touched, 0.0, HIDDEN).astype(jnp.float32)
-    seen = (slot < count[:, None, None]) & (query_pos[:, None, :] <= query_pos[:, :, None])
-    fresh_bias = jnp.where(seen, 0.0, HIDDEN).astype(jnp.float32)
-    return cached_bias, fresh_bias
+    slot = jnp.arange(maxp * per_pass, dtype=jnp.int32) // per_pass
+    at = slot * plen + rows.reshape(owned, maxp * per_pass)
+    return jnp.tile(at, (1, HEAD_GROUP))[:, None, :]
+
+
+def together(*arrays):
+    return lax.optimization_barrier(arrays)
 
 
 def after(x, *earlier):
     return lax.optimization_barrier((x, *earlier))[0]
 
 
-def ring_plan(rows_in, norm_gain, kv_weight, store_pages):
+def ring_plan(rows_in, norm_gain, kv_weight, store_pages, small):
     shards = lax.axis_size("store")
     me = lax.axis_index("store")
     side = lax.axis_index("parts")
@@ -320,6 +329,7 @@
     local, plen, _, kvw = store_pages.shape
     half = depth // 2
     columns = features // 2
+    count = owned * selected
 
     pages = store_pages.reshape(local * plen, 2, kvw)
     mine = [
@@ -327,8 +337,8 @@
     ]
     own = jnp.concatenate([pages[:, 0], pages[:, 1]], axis=0)
     a0 = jnp.concatenate([mine[0], own], axis=0)
-    a1, b1 = send(a0, 1), send(mine[1], 1)
-    gate = a0
+    a1 = send(a0, 1)
+    b1 = send(mine[1], 1)
 
     steps = jnp.arange(2 * ring, dtype=jnp.int32) // 2
     blocks = (z - steps) % ring
@@ -337,12 +347,16 @@
     targets = member ^ jnp.arange(GROUP, dtype=jnp.int32)
     offs = (blocks[None] * GROUP + targets[:, None]) * depth + halves[None] * half
     offs = (offs // 128).reshape(-1)
-    flat = rows_in.reshape(owned * selected, width)
-    acts = norm_rows(flat, norm_gain, after(offs, gate), half)
-    y_acts = flip(acts[1], 2)
+
+    device = jnp.arange(shards, dtype=jnp.int32)
+    rank = (z - device // GROUP) % ring
+    rel = (device % GROUP) ^ member
+    place = ((rel % 2) * 2 + rel // 2) * ring + rank
+    acts = norm_rows(rows_in.reshape(count, width), norm_gain, after(offs, a0), half)
+    y_acts = flip(after(acts[1], b1), 2)
     near_act = flip(acts[2], 1)
-
-    a2 = send(after(a1, near_act), 1)
+    a1, near_act, place, *small = together(a1, near_act, place, *small)
+    a2 = send(after(a1, b1), 1)
     xa1 = swap(after(a1[:half], near_act))
     b2 = send(after(b1, near_act), 1)
     xb1 = swap(b1)
@@ -350,30 +364,23 @@
     xa2 = swap(after(a2[:half], xa1))
     b3 = send(after(b2, xb1), 1)
     xb2 = swap(after(b2, xb1))
+    y_far = flip(y_acts[count:], 1)
     xa3 = swap(after(a3[:half], xa2))
+    xb3 = swap(after(b3, xb2))
     column = jnp.concatenate([own, a1[half:], a2[half:], a3[half:]], axis=0)
-    column = after(column, y_acts)
-    y_column = flip(column, 2)
-    y_far = flip(y_acts[acts[0].shape[0] :], 1)
-    xb3 = swap(after(b3, xb2))
-    far = flip(column, 1)
+    y_column = flip(after(column, y_acts), 2)
+    far = flip(after(column, b3), 1)
     y_column_far = flip(y_column, 1)
     acts = [acts[0], near_act, y_acts, y_far]
+
     chunks = [[a1, xa1, a2, xa2, a3, xa3], [b1, xb1, b2, xb2, b3, xb3]]
-
-    count = owned * selected
     terms = []
     for n in range(2):
         keep, out = project(acts, kv_weight, n, chunks[n], half)
         back = flip(out, 1)
         y_out = (keep[count:] + back[count:].astype(jnp.float32)).astype(jnp.bfloat16)
-        terms.append((keep[:count], back[:count], flip(y_out, 2)))
-
-    device = jnp.arange(shards, dtype=jnp.int32)
-    rank = (z - device // GROUP) % ring
-    rel = (device % GROUP) ^ member
-    place = ((rel % 2) * 2 + rel // 2) * ring + rank
-    return (place, [column, y_column, far, y_column_far]), terms
+        terms += [keep[:count], back[:count], flip(y_out, 2)]
+    return small, (place, [column, y_column, far, y_column_far]), terms
 
 
 def gathered_projection(rows_in, norm_gain, kv_weight):
@@ -383,7 +390,8 @@
     normed = (wide * inv * norm_gain.astype(jnp.float32)).astype(jnp.bfloat16)
     fresh = dot(normed, lax.all_gather(kv_weight, "store", axis=0, tiled=True))
     none = jnp.zeros((fresh.shape[0], fresh.shape[1] // 2), jnp.bfloat16)
-    return [(part, none, none) for part in jnp.split(fresh, 2, axis=1)]
+    keys, values = jnp.split(fresh, 2, axis=1)
+    return [keys, none, none, values, none, none]
 
 
 def sent_pages(store_pages, passage_home, passage_ids):
@@ -429,20 +437,27 @@
     owned, selected, _ = rows_in.shape
     local, plen = store_pages.shape[:2]
     ringed = shards == 4 * GROUP and lax.axis_size("parts") == 2 and kv_weight.shape[0] % 512 == 0
+    rows = lax.dynamic_slice_in_dim(recompute_rows, me * owned, owned, 0)
+    query_pos = query_positions(rows, plen)
+    flat_rows = rows.reshape(owned, selected)
     if ringed:
-        (place, sources), terms = ring_plan(rows_in, norm_gain, kv_weight, store_pages)
         ids = lax.dynamic_slice_in_dim(passage_ids, me * owned, owned, 0)
+        small, (place, sources), terms = ring_plan(
+            rows_in, norm_gain, kv_weight, store_pages, [ids, flat_rows, query_pos]
+        )
+        ids, flat_rows, query_pos = small
         pages = (place, passage_home, ids, sources)
         per_dev = local
     else:
         terms = gathered_projection(rows_in, norm_gain, kv_weight)
         pages = sent_pages(store_pages, passage_home, passage_ids)
         per_dev = 1
-    rows = lax.dynamic_slice_in_dim(recompute_rows, me * owned, owned, 0)
-    cached_bias, fresh_bias = masks(rows, passage_count, plen)
-    part, stat = cached_attention(per_dev, *pages, queries, cached_bias)
-    terms = [t.reshape(owned, selected, t.shape[1]) for chunk in terms for t in chunk]
-    return fresh_attention(passage_ids.shape[1], passage_count, queries, terms, fresh_bias, part, stat)
+    part, stat, stacked = cached_attention(
+        per_dev, plen, *pages, flat_rows, passage_count, queries, query_pos
+    )
+    terms = [t.reshape(owned, selected, t.shape[1]) for t in terms]
+    maxp = passage_ids.shape[1]
+    return fresh_attention(maxp, passage_count, stacked, terms, query_pos, part, stat)
 
 
 def solution(mesh):

time: 92.6 us -> 88.5 us (0.956)
  Pallas kernels: 29.5 us -> 22 us
  waiting for transfers between devices: 30.6 us -> 34.4 us
  starting transfers between devices: 18.2 us -> 19.5 us
  local copies, waits for them, and re-layouts: 10.9 us -> 9.62 us
    ppermute x6, waiting for transfers between devices: 24.2 us -> 29.3 us  [send(): return lax.ppermute(x, 'store', pairs)]
    ppermute x10, waiting for transfers between devices: 3.76 us -> 0.03 us  [flip(): return lax.ppermute(x, 'store', pairs)]
    pallas_call x1, Pallas kernels: 9.04 us -> 5.59 us  [fresh_attention(): pl.pallas_call(functools.partial(fresh_kernel, maxp), out_shape=jax.Shape...]
    pallas_call x2, Pallas kernels: 7.37 us -> 4.11 us  [project(): pl.pallas_call(project_kernel, out_shape=[jax.ShapeDtypeStruct((2 * rows,...]
    ppermute x6, waiting for transfers between devices: 2.68 us -> 5.09 us  [swap(): return lax.ppermute(x, 'parts', [(0, 1), (1, 0)])]
    slice x3, local copies, waits for them, and re-layouts: 2.98 us -> 1.92 us  [the longest x2 1.86 us: ring_plan(): terms += [keep[:count], back[:count], flip(y_out, 2)]]
    unnamed x28 -> x25, local copies, waits for them, and re-layouts: 5.4 us -> 5.29 us
  transfers between devices with their start and end apart: 22 -> 22, of which waited for: 10 -> 8; matrix products, arithmetic and copies ran while one was open for 7% -> 11% of each run, Pallas kernels for 22% -> 19%
where the time goes in v3:
time: 88.5 us; the launch traced here: 88.2 us
  waiting for transfers between devices  34.4 us (39%)
  Pallas kernels  22 us (25%)
  starting transfers between devices  19.5 us (22%)
  local copies, waits for them, and re-layouts  9.62 us (11%)
  other arithmetic  2.54 us (3%)
    ppermute x6, waiting for transfers between devices, send(): return lax.ppermute(x, 'store', pairs)  29.3 us
    ppermute x6, starting transfers between devices, swap(): return lax.ppermute(x, 'parts', [(0, 1), (1, 0)])  8.72 us
    pallas_call x1, Pallas kernels, cached_attention(): pl.pallas_call(functools.partial(cached_kernel, per_dev), out_shape=[jax....  8.2 us
    pallas_call x1, Pallas kernels, fresh_attention(): pl.pallas_call(functools.partial(fresh_kernel, maxp), out_shape=jax.Shape...  5.59 us
    ppermute x6, starting transfers between devices, send(): return lax.ppermute(x, 'store', pairs)  5.44 us
    ppermute x10, starting transfers between devices, flip(): return lax.ppermute(x, 'store', pairs)  5.34 us
    unnamed x25, local copies, waits for them, and re-layouts  5.29 us
    ppermute x6, waiting for transfers between devices, swap(): return lax.ppermute(x, 'parts', [(0, 1), (1, 0)])  5.09 us
  transfers between devices with their start and end apart: 22, of which 8 were waited for; matrix products, arithmetic and copies ran while one was open for 11% of the time, Pallas kernels for 19%

profile of v3, /device:TPU:0, one launch (start us, length us, event | category | flops | bytes accessed | tf_op | source)
XLA Modules:
  0.0 88.2 jit_solution(11653316847878230267)
XLA Ops:
  0.0 1.1 %constant_dynamic-slice_fusion.3 = (bf16[256,512]{1,0:T(8,128)(2,1)S(1)}, bf16[256,512]{1,0:T(8,128)(2,1)S(1)}) fusion(bf16[512,1024]{1,0:T(8,128)(2,1)} %refs_0_.3, s32[]{:T(128)S(6)} %select_n.97), kind=kLoop, calls=%fused_computation.55 | loop fusion | bytes 1048580 | tf_op jit(solution)/shard_map/dynamic_slice | solution.py:336
  1.1 3.1 %collective-permute-start.2 = (bf16[256,512]{1,0:T(8,128)(2,1)S(1)}, bf16[256,512]{1,0:T(8,128)(2,1)S(1)}, u32[]{:S(2)}, u32[]{:S(2)}) collective-permute-start(bf16[256,512]{1,0:T(8,128)(2,1)S(1)} %get-tuple-element.61), channel_id=1, source_target_pairs={{0,4},{1,5},{2,6},{3,7},{4,8},{5,9},{6,10},{7,11},{8,12},{9,13},{1... | collective-permute-start | bytes 786440 | tf_op jit(solution)/shard_map/ppermute | solution.py:37
  4.2 0.9 %copy.13 = bf16[4,16,2,512]{3,1,0,2:T(8,128)(2,1)S(1)} copy(bf16[4,16,2,512]{3,2,1,0:T(2,128)(2,1)} %param.13) | data formatting | bytes 262144 | tf_op args[4]
  5.2 0.8 pad_maximum_fusion
  6.1 1.7 %copy-done.2 = bf16[4,40,8192]{2,1,0:T(8,128)(2,1)S(1)} copy-done((bf16[4,40,8192]{2,1,0:T(8,128)(2,1)S(1)}, bf16[4,40,8192]{2,1,0:T(8,128)(2,1)}, u32[]{:S(2)}) %copy-start.2) | copy-done | bytes 2621464
  7.9 4.1 %norm.1 = (bf16[160,2048]{1,0:T(8,128)(2,1)S(1)}, bf16[2,160,2048]{2,1,0:T(8,128)(2,1)}, bf16[160,2048]{1,0:T(8,128)(2,1)}) custom-call(s32[32]{0:T(128)S(1)} %and_select_fusion.6.offs_ref, bf16[160,8192]{1,0:T(8,128)(2,1)S(1)} %bitcast.18, bf16[1,8192]{1,0:T(2,128)(2,1)S(1)} %reshape.129.gain_ref), custom_call_target="tpu_custom_call" | custom-call | flops 7864320 | bytes 5242880 | tf_op jit(solution)/shard_map/norm/pallas_call | solution.py:72
  12.5 1.5 %collective-permute-start.6 = (bf16[320,2048]{1,0:T(8,128)(2,1)}, bf16[320,2048]{1,0:T(8,128)(2,1)S(1)}, u32[]{:S(2)}, u32[]{:S(2)}) collective-permute-start(bf16[320,2048]{1,0:T(8,128)(2,1)} %bitcast.5), channel_id=1, source_target_pairs={{0,2},{1,3},{2,0},{3,1},{4,6},{5,7},{6,4},{7,5},{8,10},{9,11},{10,... | collective-permute-start | bytes 3932168 | tf_op jit(solution)/shard_map/ppermute | solution.py:42
  14.0 1.0 %collective-permute-start = (bf16[384,512]{1,0:T(8,128)(2,1)}, bf16[384,512]{1,0:T(8,128)(2,1)S(1)}, u32[]{:S(2)}, u32[]{:S(2)}) collective-permute-start(bf16[384,512]{1,0:T(8,128)(2,1)} %pad_maximum_fusion), channel_id=1, source_target_pairs={{0,4},{1,5},{2,6},{3,7},{4,8},{5,9},{6,10},{7,11},{8,12},{9,13},{1... | collective-permute-start | bytes 1179656 | tf_op jit(solution)/shard_map/ppermute | solution.py:37
  15.6 1.6 %collective-permute-start.9 = (bf16[256,512]{1,0:T(8,128)(2,1)S(1)}, bf16[256,512]{1,0:T(8,128)(2,1)S(1)}, u32[]{:S(2)}, u32[]{:S(2)}) collective-permute-start(bf16[256,512]{1,0:T(8,128)(2,1)S(1)} %collective-permute-done.2.refs_1_), channel_id=1, source_target_pairs={{0,16},{16,0},{1,17},{17,1},{2,18},{18,2},{3,19},{19,3},{4,20},{20... | collective-permute-start | bytes 786440 | tf_op jit(solution)/shard_map/ppermute | solution.py:46
  17.2 8.6 %collective-permute-done.refs_1_ = bf16[384,512]{1,0:T(8,128)(2,1)S(1)} collective-permute-done((bf16[384,512]{1,0:T(8,128)(2,1)}, bf16[384,512]{1,0:T(8,128)(2,1)S(1)}, u32[]{:S(2)}, u32[]{:S(2)}) %collective-permute-start) | collective-permute-done | bytes 393248 | tf_op jit(solution)/shard_map/ppermute | solution.py:37
  25.8 1.6 %collective-permute-start.4 = (bf16[256,512]{1,0:T(8,128)(2,1)S(1)}, bf16[256,512]{1,0:T(8,128)(2,1)S(1)}, u32[]{:S(2)}, u32[]{:S(2)}) collective-permute-start(bf16[256,512]{1,0:T(8,128)(2,1)S(1)} %slice.55), channel_id=1, source_target_pairs={{0,16},{16,0},{1,17},{17,1},{2,18},{18,2},{3,19},{19,3},{4,20},{20... | collective-permute-start | bytes 786440 | tf_op jit(solution)/shard_map/ppermute | solution.py:46
  27.4 1.3 %collective-permute-start.3 = (bf16[384,512]{1,0:T(8,128)(2,1)S(1)}, bf16[384,512]{1,0:T(8,128)(2,1)S(1)}, u32[]{:S(2)}, u32[]{:S(2)}) collective-permute-start(bf16[384,512]{1,0:T(8,128)(2,1)S(1)} %collective-permute-done.refs_1_), channel_id=1, source_target_pairs={{0,4},{1,5},{2,6},{3,7},{4,8},{5,9},{6,10},{7,11},{8,12},{9,13},{1... | collective-permute-start | bytes 1179656 | tf_op jit(solution)/shard_map/ppermute | solution.py:37
  30.0 6.9 %collective-permute-done.8.refs_3_ = bf16[256,512]{1,0:T(8,128)(2,1)S(1)} collective-permute-done((bf16[256,512]{1,0:T(8,128)(2,1)S(1)}, bf16[256,512]{1,0:T(8,128)(2,1)S(1)}, u32[]{:S(2)}, u32[]{:S(2)}) %collective-permute-start.8) | collective-permute-done | bytes 262176 | tf_op jit(solution)/shard_map/ppermute | solution.py:37
  36.9 1.5 %collective-permute-start.18 = (bf16[256,512]{1,0:T(8,128)(2,1)S(1)}, bf16[256,512]{1,0:T(8,128)(2,1)S(1)}, u32[]{:S(2)}, u32[]{:S(2)}) collective-permute-start(bf16[256,512]{1,0:T(8,128)(2,1)S(1)} %collective-permute-done.8.refs_3_), channel_id=1, source_target_pairs={{0,16},{16,0},{1,17},{17,1},{2,18},{18,2},{3,19},{19,3},{4,20},{20... | collective-permute-start | bytes 786440 | tf_op jit(solution)/shard_map/ppermute | solution.py:46
  38.3 6.9 %collective-permute-done.3.refs_3_ = bf16[384,512]{1,0:T(8,128)(2,1)S(1)} collective-permute-done((bf16[384,512]{1,0:T(8,128)(2,1)S(1)}, bf16[384,512]{1,0:T(8,128)(2,1)S(1)}, u32[]{:S(2)}, u32[]{:S(2)}) %collective-permute-start.3) | collective-permute-done | bytes 393248 | tf_op jit(solution)/shard_map/ppermute | solution.py:37
  46.1 1.6 %collective-permute-start.14 = (bf16[256,512]{1,0:T(8,128)(2,1)S(1)}, bf16[256,512]{1,0:T(8,128)(2,1)S(1)}, u32[]{:S(2)}, u32[]{:S(2)}) collective-permute-start(bf16[256,512]{1,0:T(8,128)(2,1)S(1)} %slice.73), channel_id=1, source_target_pairs={{0,16},{16,0},{1,17},{17,1},{2,18},{18,2},{3,19},{19,3},{4,20},{20... | collective-permute-start | bytes 786440 | tf_op jit(solution)/shard_map/ppermute | solution.py:46
  48.3 2.5 %collective-permute-done.10.refs_5_ = bf16[256,512]{1,0:T(8,128)(2,1)S(1)} collective-permute-done((bf16[256,512]{1,0:T(8,128)(2,1)S(1)}, bf16[256,512]{1,0:T(8,128)(2,1)S(1)}, u32[]{:S(2)}, u32[]{:S(2)}) %collective-permute-start.10) | collective-permute-done | bytes 262176 | tf_op jit(solution)/shard_map/ppermute | solution.py:37
  50.9 1.5 %collective-permute-start.19 = (bf16[256,512]{1,0:T(8,128)(2,1)S(1)}, bf16[256,512]{1,0:T(8,128)(2,1)S(1)}, u32[]{:S(2)}, u32[]{:S(2)}) collective-permute-start(bf16[256,512]{1,0:T(8,128)(2,1)S(1)} %collective-permute-done.10.refs_5_), channel_id=1, source_target_pairs={{0,16},{16,0},{1,17},{17,1},{2,18},{18,2},{3,19},{19,3},{4,20},{20... | collective-permute-start | bytes 786440 | tf_op jit(solution)/shard_map/ppermute | solution.py:46
  52.4 3.7 %collective-permute-done.5.refs_5_ = bf16[384,512]{1,0:T(8,128)(2,1)S(1)} collective-permute-done((bf16[384,512]{1,0:T(8,128)(2,1)S(1)}, bf16[384,512]{1,0:T(8,128)(2,1)S(1)}, u32[]{:S(2)}, u32[]{:S(2)}) %collective-permute-start.5) | collective-permute-done | bytes 393248 | tf_op jit(solution)/shard_map/ppermute | solution.py:37
  56.8 1.0 %collective-permute-start.7 = (bf16[512,512]{1,0:T(8,128)(2,1)}, bf16[512,512]{1,0:T(8,128)(2,1)}, u32[]{:S(2)}, u32[]{:S(2)}) collective-permute-start(bf16[512,512]{1,0:T(8,128)(2,1)} %slice_dynamic-update-slice_fusion.refs_0_), channel_id=1, source_target_pairs={{0,2},{1,3},{2,0},{3,1},{4,6},{5,7},{6,4},{7,5},{8,10},{9,11},{10,... | collective-permute-start | bytes 1572872 | tf_op jit(solution)/shard_map/ppermute | solution.py:42
  57.8 1.1 %collective-permute-start.15 = (bf16[256,512]{1,0:T(8,128)(2,1)S(1)}, bf16[256,512]{1,0:T(8,128)(2,1)S(1)}, u32[]{:S(2)}, u32[]{:S(2)}) collective-permute-start(bf16[256,512]{1,0:T(8,128)(2,1)S(1)} %slice.74), channel_id=1, source_target_pairs={{0,16},{16,0},{1,17},{17,1},{2,18},{18,2},{3,19},{19,3},{4,20},{20... | collective-permute-start | bytes 786440 | tf_op jit(solution)/shard_map/ppermute | solution.py:46
  58.9 2.0 %collective-permute-done.19.refs_6_ = bf16[256,512]{1,0:T(8,128)(2,1)S(1)} collective-permute-done((bf16[256,512]{1,0:T(8,128)(2,1)S(1)}, bf16[256,512]{1,0:T(8,128)(2,1)S(1)}, u32[]{:S(2)}, u32[]{:S(2)}) %collective-permute-start.19) | collective-permute-done | bytes 262176 | tf_op jit(solution)/shard_map/ppermute | solution.py:46
  60.9 2.1 %project.3 = (f32[320,512]{1,0:T(8,128)S(1)}, bf16[320,512]{1,0:T(8,128)(2,1)S(1)}) custom-call(bf16[160,2048]{1,0:T(8,128)(2,1)S(1)} %get-tuple-element.51.a0, bf16[160,2048]{1,0:T(8,128)(2,1)S(1)} %collective-permute-done.1.a1, bf16[320,2048]{1,0:T(8,128)(2,1)S(1)} %collective-permute-done.6.a2, bf16[160,2048]{1,0:T(8,128)(2,1)S(1)} %collective-permute-done.13.a3, ...), custom_call_target="tpu_custom_call" | custom-call | flops 1342177280 | bytes 6684672 | tf_op jit(solution)/shard_map/project/pallas_call | solution.py:119
  63.1 3.1 %collective-permute-done.15.refs_6_ = bf16[256,512]{1,0:T(8,128)(2,1)S(1)} collective-permute-done((bf16[256,512]{1,0:T(8,128)(2,1)S(1)}, bf16[256,512]{1,0:T(8,128)(2,1)S(1)}, u32[]{:S(2)}, u32[]{:S(2)}) %collective-permute-start.15) | collective-permute-done | bytes 262176 | tf_op jit(solution)/shard_map/ppermute | solution.py:46
  66.1 2.0 %project.2 = (f32[320,512]{1,0:T(8,128)S(1)}, bf16[320,512]{1,0:T(8,128)(2,1)S(1)}) custom-call(bf16[160,2048]{1,0:T(8,128)(2,1)S(1)} %get-tuple-element.51.a0, bf16[160,2048]{1,0:T(8,128)(2,1)S(1)} %collective-permute-done.1.a1, bf16[320,2048]{1,0:T(8,128)(2,1)S(1)} %collective-permute-done.6.a2, bf16[160,2048]{1,0:T(8,128)(2,1)S(1)} %collective-permute-done.13.a3, ...), custom_call_target="tpu_custom_call" | custom-call | flops 1342177280 | bytes 6684672 | tf_op jit(solution)/shard_map/project/pallas_call | solution.py:119
  68.8 0.8 add_convert_fusion
  70.3 0.8 add_convert_fusion.1
  71.1 1.3 %collective-permute-start.17 = (bf16[160,512]{1,0:T(8,128)(2,1)}, bf16[160,512]{1,0:T(8,128)(2,1)S(1)}, u32[]{:S(2)}, u32[]{:S(2)}) collective-permute-start(bf16[160,512]{1,0:T(8,128)(2,1)} %get-tuple-element.65), channel_id=1, source_target_pairs={{0,2},{1,3},{2,0},{3,1},{4,6},{5,7},{6,4},{7,5},{8,10},{9,11},{10,... | collective-permute-start | bytes 491528 | tf_op jit(solution)/shard_map/ppermute | solution.py:42
  72.5 0.9 %slice.77 = bf16[160,512]{1,0:T(8,128)(2,1)S(1)} slice(bf16[320,512]{1,0:T(8,128)(2,1)} %copy-done.6), slice={[0:160], [0:512]} | slice | bytes 327680 | tf_op jit(solution)/shard_map/slice | solution.py:382
  73.4 0.9 %slice.75 = bf16[160,512]{1,0:T(8,128)(2,1)S(1)} slice(bf16[320,512]{1,0:T(8,128)(2,1)} %copy-done.7), slice={[0:160], [0:512]} | slice | bytes 327680 | tf_op jit(solution)/shard_map/slice | solution.py:382
  74.4 8.2 %cached_attention.1 = (f32[4,4,128,320]{3,2,1,0:T(8,128)S(1)}, f32[4,4,2,320]{3,2,1,0:T(2,128)S(1)}, bf16[4,4,320,128]{3,2,1,0:T(8,128)(2,1)S(1)}) custom-call(s32[16]{0:T(128)S(1)} %fusion.place_ref, s32[64]{0:T(128)S(1)} %copy-done.5, s32[4,20]{1,0:T(4,128)S(1)} %copy.17.ids_ref, s32[4,40]{1,0:T(4,128)S(1)} %copy.16.rows_ref, s32[4]{0:T(128)S(1)} %copy-done.4, ...), custom_call_target="tpu_custom_call" | custom-call | flops 838860800 | bytes 4718592 | tf_op jit(solution)/shard_map/cached_attention/pallas_call | solution.py:207
  82.6 5.6 %fresh_attention.1 = bf16[4,40,4096]{2,1,0:T(8,128)(2,1)} custom-call(s32[4]{0:T(128)S(1)} %copy-done.4, bf16[4,4,320,128]{3,2,1,0:T(8,128)(2,1)S(1)} %get-tuple-element.50.q_ref, f32[4,40,512]{2,1,0:T(8,128)S(1)} %bitcast.20, bf16[4,40,512]{2,1,0:T(8,128)(2,1)S(1)} %bitcast.22, bf16[4,40,512]{2,1,0:T(8,128)(2,1)S(1)} %bitcast.24, ...), custom_call_target="tpu_custom_call" | custom-call | flops 104857600 | bytes 5242880 | tf_op jit(solution)/shard_map/fresh_attention/pallas_call | solution.py:283
  (70 shorter events, 6.3 us)
Async XLA Ops:
  0.0 15.1 %copy-start = (s32[64,20,2]{0,2,1:T(2,128)S(1)}, s32[64,20,2]{0,2,1:T(2,128)}, u32[]{:S(2)}) copy-start(s32[64,20,2]{0,2,1:T(2,128)} %param.17) | copy-start | bytes 30724
  0.0 6.1 %copy-start.8 = (bf16[8192]{0:T(1024)(128)(2,1)S(1)}, bf16[8192]{0:T(1024)(128)(2,1)}, u32[]{:S(2)}) copy-start(bf16[8192]{0:T(1024)(128)(2,1)} %param.10) | copy-start | bytes 49156
  1.1 11.4 %collective-permute-start.2 = (bf16[256,512]{1,0:T(8,128)(2,1)S(1)}, bf16[256,512]{1,0:T(8,128)(2,1)S(1)}, u32[]{:S(2)}, u32[]{:S(2)}) collective-permute-start(bf16[256,512]{1,0:T(8,128)(2,1)S(1)} %get-tuple-element.61), channel_id=1, source_target_pairs={{0,4},{1,5},{2,6},{3,7},{4,8},{5,9},{6,10},{7,11},{8,12},{9,13},{1... | collective-permute-start | bytes 786440 | tf_op jit(solution)/shard_map/ppermute | solution.py:37
  6.1 1.7 %copy-start.2 = (bf16[4,40,8192]{2,1,0:T(8,128)(2,1)S(1)}, bf16[4,40,8192]{2,1,0:T(8,128)(2,1)}, u32[]{:S(2)}) copy-start(bf16[4,40,8192]{2,1,0:T(8,128)(2,1)} %param.9) | copy-start | bytes 7864324
  7.9 7.6 %copy-start.9 = (s32[64,20]{0,1:T(8,128)S(1)}, s32[64,20]{0,1:T(8,128)}, u32[]{:S(2)}) copy-start(s32[64,20]{0,1:T(8,128)} %param.15) | copy-start | bytes 15364
  12.5 32.8 %collective-permute-start.6 = (bf16[320,2048]{1,0:T(8,128)(2,1)}, bf16[320,2048]{1,0:T(8,128)(2,1)S(1)}, u32[]{:S(2)}, u32[]{:S(2)}) collective-permute-start(bf16[320,2048]{1,0:T(8,128)(2,1)} %bitcast.5), channel_id=1, source_target_pairs={{0,2},{1,3},{2,0},{3,1},{4,6},{5,7},{6,4},{7,5},{8,10},{9,11},{10,... | collective-permute-start | bytes 3932168 | tf_op jit(solution)/shard_map/ppermute | solution.py:42
  14.0 11.8 %collective-permute-start = (bf16[384,512]{1,0:T(8,128)(2,1)}, bf16[384,512]{1,0:T(8,128)(2,1)S(1)}, u32[]{:S(2)}, u32[]{:S(2)}) collective-permute-start(bf16[384,512]{1,0:T(8,128)(2,1)} %pad_maximum_fusion), channel_id=1, source_target_pairs={{0,4},{1,5},{2,6},{3,7},{4,8},{5,9},{6,10},{7,11},{8,12},{9,13},{1... | collective-permute-start | bytes 1179656 | tf_op jit(solution)/shard_map/ppermute | solution.py:37
  15.0 10.8 %collective-permute-start.1 = (bf16[160,2048]{1,0:T(8,128)(2,1)}, bf16[160,2048]{1,0:T(8,128)(2,1)S(1)}, u32[]{:S(2)}, u32[]{:S(2)}) collective-permute-start(bf16[160,2048]{1,0:T(8,128)(2,1)} %get-tuple-element.34), channel_id=1, source_target_pairs={{0,1},{1,0},{2,3},{3,2},{4,5},{5,4},{6,7},{7,6},{8,9},{9,8},{10,11... | collective-permute-start | bytes 1966088 | tf_op jit(solution)/shard_map/ppermute | solution.py:42
  15.6 14.4 %collective-permute-start.9 = (bf16[256,512]{1,0:T(8,128)(2,1)S(1)}, bf16[256,512]{1,0:T(8,128)(2,1)S(1)}, u32[]{:S(2)}, u32[]{:S(2)}) collective-permute-start(bf16[256,512]{1,0:T(8,128)(2,1)S(1)} %collective-permute-done.2.refs_1_), channel_id=1, source_target_pairs={{0,16},{16,0},{1,17},{17,1},{2,18},{18,2},{3,19},{19,3},{4,20},{20... | collective-permute-start | bytes 786440 | tf_op jit(solution)/shard_map/ppermute | solution.py:46
  25.8 11.0 %collective-permute-start.8 = (bf16[256,512]{1,0:T(8,128)(2,1)S(1)}, bf16[256,512]{1,0:T(8,128)(2,1)S(1)}, u32[]{:S(2)}, u32[]{:S(2)}) collective-permute-start(bf16[256,512]{1,0:T(8,128)(2,1)S(1)} %collective-permute-done.2.refs_1_), channel_id=1, source_target_pairs={{0,4},{1,5},{2,6},{3,7},{4,8},{5,9},{6,10},{7,11},{8,12},{9,13},{1... | collective-permute-start | bytes 786440 | tf_op jit(solution)/shard_map/ppermute | solution.py:37
  25.8 12.5 %collective-permute-start.4 = (bf16[256,512]{1,0:T(8,128)(2,1)S(1)}, bf16[256,512]{1,0:T(8,128)(2,1)S(1)}, u32[]{:S(2)}, u32[]{:S(2)}) collective-permute-start(bf16[256,512]{1,0:T(8,128)(2,1)S(1)} %slice.55), channel_id=1, source_target_pairs={{0,16},{16,0},{1,17},{17,1},{2,18},{18,2},{3,19},{19,3},{4,20},{20... | collective-permute-start | bytes 786440 | tf_op jit(solution)/shard_map/ppermute | solution.py:46
  27.4 17.9 %collective-permute-start.3 = (bf16[384,512]{1,0:T(8,128)(2,1)S(1)}, bf16[384,512]{1,0:T(8,128)(2,1)S(1)}, u32[]{:S(2)}, u32[]{:S(2)}) collective-permute-start(bf16[384,512]{1,0:T(8,128)(2,1)S(1)} %collective-permute-done.refs_1_), channel_id=1, source_target_pairs={{0,4},{1,5},{2,6},{3,7},{4,8},{5,9},{6,10},{7,11},{8,12},{9,13},{1... | collective-permute-start | bytes 1179656 | tf_op jit(solution)/shard_map/ppermute | solution.py:37
  30.0 30.9 %copy-start.1 = (bf16[512,1024]{1,0:T(8,128)(2,1)S(1)}, bf16[512,1024]{1,0:T(8,128)(2,1)}, u32[]{:S(2)}) copy-start(bf16[512,1024]{1,0:T(8,128)(2,1)} %refs_0_.3) | copy-start | bytes 3145732
  36.8 14.0 %collective-permute-start.10 = (bf16[256,512]{1,0:T(8,128)(2,1)S(1)}, bf16[256,512]{1,0:T(8,128)(2,1)S(1)}, u32[]{:S(2)}, u32[]{:S(2)}) collective-permute-start(bf16[256,512]{1,0:T(8,128)(2,1)S(1)} %collective-permute-done.8.refs_3_), channel_id=1, source_target_pairs={{0,4},{1,5},{2,6},{3,7},{4,8},{5,9},{6,10},{7,11},{8,12},{9,13},{1... | collective-permute-start | bytes 786440 | tf_op jit(solution)/shard_map/ppermute | solution.py:37
  36.9 14.0 %collective-permute-start.18 = (bf16[256,512]{1,0:T(8,128)(2,1)S(1)}, bf16[256,512]{1,0:T(8,128)(2,1)S(1)}, u32[]{:S(2)}, u32[]{:S(2)}) collective-permute-start(bf16[256,512]{1,0:T(8,128)(2,1)S(1)} %collective-permute-done.8.refs_3_), channel_id=1, source_target_pairs={{0,16},{16,0},{1,17},{17,1},{2,18},{18,2},{3,19},{19,3},{4,20},{20... | collective-permute-start | bytes 786440 | tf_op jit(solution)/shard_map/ppermute | solution.py:46
  45.3 10.8 %collective-permute-start.5 = (bf16[384,512]{1,0:T(8,128)(2,1)S(1)}, bf16[384,512]{1,0:T(8,128)(2,1)S(1)}, u32[]{:S(2)}, u32[]{:S(2)}) collective-permute-start(bf16[384,512]{1,0:T(8,128)(2,1)S(1)} %collective-permute-done.3.refs_3_), channel_id=1, source_target_pairs={{0,4},{1,5},{2,6},{3,7},{4,8},{5,9},{6,10},{7,11},{8,12},{9,13},{1... | collective-permute-start | bytes 1179656 | tf_op jit(solution)/shard_map/ppermute | solution.py:37
  45.3 15.6 %collective-permute-start.13 = (bf16[160,2048]{1,0:T(8,128)(2,1)S(1)}, bf16[160,2048]{1,0:T(8,128)(2,1)S(1)}, u32[]{:S(2)}, u32[]{:S(2)}) collective-permute-start(bf16[160,2048]{1,0:T(8,128)(2,1)S(1)} %slice.72), channel_id=1, source_target_pairs={{0,1},{1,0},{2,3},{3,2},{4,5},{5,4},{6,7},{7,6},{8,9},{9,8},{10,11... | collective-permute-start | bytes 1966088 | tf_op jit(solution)/shard_map/ppermute | solution.py:42
  46.1 11.7 %collective-permute-start.14 = (bf16[256,512]{1,0:T(8,128)(2,1)S(1)}, bf16[256,512]{1,0:T(8,128)(2,1)S(1)}, u32[]{:S(2)}, u32[]{:S(2)}) collective-permute-start(bf16[256,512]{1,0:T(8,128)(2,1)S(1)} %slice.73), channel_id=1, source_target_pairs={{0,16},{16,0},{1,17},{17,1},{2,18},{18,2},{3,19},{19,3},{4,20},{20... | collective-permute-start | bytes 786440 | tf_op jit(solution)/shard_map/ppermute | solution.py:46
  50.9 10.0 %collective-permute-start.19 = (bf16[256,512]{1,0:T(8,128)(2,1)S(1)}, bf16[256,512]{1,0:T(8,128)(2,1)S(1)}, u32[]{:S(2)}, u32[]{:S(2)}) collective-permute-start(bf16[256,512]{1,0:T(8,128)(2,1)S(1)} %collective-permute-done.10.refs_5_), channel_id=1, source_target_pairs={{0,16},{16,0},{1,17},{17,1},{2,18},{18,2},{3,19},{19,3},{4,20},{20... | collective-permute-start | bytes 786440 | tf_op jit(solution)/shard_map/ppermute | solution.py:46
  56.8 12.0 %collective-permute-start.7 = (bf16[512,512]{1,0:T(8,128)(2,1)}, bf16[512,512]{1,0:T(8,128)(2,1)}, u32[]{:S(2)}, u32[]{:S(2)}) collective-permute-start(bf16[512,512]{1,0:T(8,128)(2,1)} %slice_dynamic-update-slice_fusion.refs_0_), channel_id=1, source_target_pairs={{0,2},{1,3},{2,0},{3,1},{4,6},{5,7},{6,4},{7,5},{8,10},{9,11},{10,... | collective-permute-start | bytes 1572872 | tf_op jit(solution)/shard_map/ppermute | solution.py:42
  57.8 8.3 %collective-permute-start.15 = (bf16[256,512]{1,0:T(8,128)(2,1)S(1)}, bf16[256,512]{1,0:T(8,128)(2,1)S(1)}, u32[]{:S(2)}, u32[]{:S(2)}) collective-permute-start(bf16[256,512]{1,0:T(8,128)(2,1)S(1)} %slice.74), channel_id=1, source_target_pairs={{0,16},{16,0},{1,17},{17,1},{2,18},{18,2},{3,19},{19,3},{4,20},{20... | collective-permute-start | bytes 786440 | tf_op jit(solution)/shard_map/ppermute | solution.py:46
  63.0 5.8 %collective-permute-start.20 = (bf16[320,512]{1,0:T(8,128)(2,1)S(1)}, bf16[320,512]{1,0:T(8,128)(2,1)S(1)}, u32[]{:S(2)}, u32[]{:S(2)}) collective-permute-start(bf16[320,512]{1,0:T(8,128)(2,1)S(1)} %get-tuple-element.58), channel_id=1, source_target_pairs={{0,1},{1,0},{2,3},{3,2},{4,5},{5,4},{6,7},{7,6},{8,9},{9,8},{10,11... | collective-permute-start | bytes 983048 | tf_op jit(solution)/shard_map/ppermute | solution.py:42
  68.2 2.2 %collective-permute-start.16 = (bf16[320,512]{1,0:T(8,128)(2,1)S(1)}, bf16[320,512]{1,0:T(8,128)(2,1)S(1)}, u32[]{:S(2)}, u32[]{:S(2)}) collective-permute-start(bf16[320,512]{1,0:T(8,128)(2,1)S(1)} %get-tuple-element.55), channel_id=1, source_target_pairs={{0,1},{1,0},{2,3},{3,2},{4,5},{5,4},{6,7},{7,6},{8,9},{9,8},{10,11... | collective-permute-start | bytes 983048 | tf_op jit(solution)/shard_map/ppermute | solution.py:42
  68.2 6.1 %collective-permute-start.11 = (bf16[512,512]{1,0:T(8,128)(2,1)}, bf16[512,512]{1,0:T(8,128)(2,1)S(1)}, u32[]{:S(2)}, u32[]{:S(2)}) collective-permute-start(bf16[512,512]{1,0:T(8,128)(2,1)} %slice_dynamic-update-slice_fusion.refs_0_), channel_id=1, source_target_pairs={{0,1},{1,0},{2,3},{3,2},{4,5},{5,4},{6,7},{7,6},{8,9},{9,8},{10,11... | collective-permute-start | bytes 1572872 | tf_op jit(solution)/shard_map/ppermute | solution.py:42
  68.7 5.6 %collective-permute-start.12 = (bf16[512,512]{1,0:T(8,128)(2,1)}, bf16[512,512]{1,0:T(8,128)(2,1)S(1)}, u32[]{:S(2)}, u32[]{:S(2)}) collective-permute-start(bf16[512,512]{1,0:T(8,128)(2,1)} %collective-permute-done.7.refs_1_), channel_id=1, source_target_pairs={{0,1},{1,0},{2,3},{3,2},{4,5},{5,4},{6,7},{7,6},{8,9},{9,8},{10,11... | collective-permute-start | bytes 1572872 | tf_op jit(solution)/shard_map/ppermute | solution.py:42
  68.8 2.3 %copy-start.6 = (bf16[320,512]{1,0:T(8,128)(2,1)}, bf16[320,512]{1,0:T(8,128)(2,1)S(1)}, u32[]{:S(2)}) copy-start(bf16[320,512]{1,0:T(8,128)(2,1)S(1)} %collective-permute-done.20) | copy-start | bytes 983044
  69.6 4.8 %copy-start.3 = (bf16[4,40,4096]{2,1,0:T(8,128)(2,1)S(1)}, bf16[4,40,4096]{2,1,0:T(8,128)(2,1)}, u32[]{:S(2)}) copy-start(bf16[4,40,4096]{2,1,0:T(8,128)(2,1)} %q_ref.1) | copy-start | bytes 3932164
  69.6 4.8 %copy-start.4 = (s32[4]{0:T(128)S(1)}, s32[4]{0:T(128)}, u32[]{:S(2)}) copy-start(s32[4]{0:T(128)} %count_ref.3) | copy-start | bytes 52
  69.6 4.8 %copy-start.5 = (s32[64]{0:T(128)S(1)}, s32[64]{0:T(128)}, u32[]{:S(2)}) copy-start(s32[64]{0:T(128)} %home_ref.1) | copy-start | bytes 772
  69.6 13.0 %collective-permute-start.21 = (bf16[160,512]{1,0:T(8,128)(2,1)}, bf16[160,512]{1,0:T(8,128)(2,1)S(1)}, u32[]{:S(2)}, u32[]{:S(2)}) collective-permute-start(bf16[160,512]{1,0:T(8,128)(2,1)} %get-tuple-element.63), channel_id=1, source_target_pairs={{0,2},{1,3},{2,0},{3,1},{4,6},{5,7},{6,4},{7,5},{8,10},{9,11},{10,... | collective-permute-start | bytes 491528 | tf_op jit(solution)/shard_map/ppermute | solution.py:42
  70.3 0.8 copy-start.7
  71.1 11.5 %collective-permute-start.17 = (bf16[160,512]{1,0:T(8,128)(2,1)}, bf16[160,512]{1,0:T(8,128)(2,1)S(1)}, u32[]{:S(2)}, u32[]{:S(2)}) collective-permute-start(bf16[160,512]{1,0:T(8,128)(2,1)} %get-tuple-element.65), channel_id=1, source_target_pairs={{0,2},{1,3},{2,0},{3,1},{4,6},{5,7},{6,4},{7,5},{8,10},{9,11},{10,... | collective-permute-start | bytes 491528 | tf_op jit(solution)/shard_map/ppermute | solution.py:42

commit v4 on v3

--- a/solution.py
+++ b/solution.py
@@ -93,48 +93,47 @@
     return jnp.dot(a, b, preferred_element_type=jnp.float32)
 
 
-def project_kernel(a0, a1, a2, a3, *refs):
-    weights, (keep, send) = refs[:-2], refs[-2:]
-    rows = a0.shape[0]
-    for j, a in enumerate((a0, a1, a2, a3)):
-        total = None
-        at = 0
-        for w in weights:
-            depth = w.shape[0]
-            term = dot(a[:, at : at + depth], w[...])
-            total = term if total is None else total + term
-            at += depth
-        place = slice((j // 2) * rows, (j // 2 + 1) * rows)
-        if j % 2:
-            send[place, :] = total.astype(jnp.bfloat16)
-        else:
-            keep[place, :] = total
-
-
-def project(acts, own, first, weights, half):
-    rows, depth = acts[0].shape
-    features = weights[0].shape[1]
-    block = 256
-    shift = first * features // block
+def project_kernel(skip, shift, depths, begins, *refs):
+    acts, refs = refs[:GROUP], refs[GROUP:]
+    start, weights, outs = refs[:begins], refs[begins : begins + len(depths)], refs[begins + len(depths) :]
+    rows = acts[0].shape[0]
+    width = 256 if outs[0].shape[1] % 256 == 0 else 128
+    for column in range(0, outs[0].shape[1], width):
+        columns = slice(column, column + width)
+        for j, a in enumerate(acts):
+            total = start[0][j * rows : (j + 1) * rows, columns] if start else None
+            at = skip
+            for n, (w, depth) in enumerate(zip(weights, depths)):
+                first = column + (0 if n or start else shift)
+                term = dot(a[:rows, at : at + depth], w[:depth, first : first + width])
+                total = term if total is None else total + term
+                at += depth
+            if len(outs) == 1:
+                outs[0][j * rows : (j + 1) * rows, columns] = total
+            else:
+                place = slice((j // 2) * rows, (j // 2 + 1) * rows)
+                outs[j % 2][place, columns] = total.astype(outs[j % 2].dtype)
+
+
+def project(acts, skip, shift, weights, depths, columns, start=(), last=True):
+    rows = acts[0].shape[0]
+    if last:
+        out = [(2 * rows, jnp.float32), (2 * rows, jnp.bfloat16)]
+    else:
+        out = [(GROUP * rows, jnp.float32)]
     return pl.pallas_call(
-        project_kernel,
-        out_shape=[
-            jax.ShapeDtypeStruct((2 * rows, features), jnp.float32),
-            jax.ShapeDtypeStruct((2 * rows, features), jnp.bfloat16),
-        ],
-        grid=(features // block,),
-        in_specs=[pl.BlockSpec((rows, depth), lambda i: (0, 0))] * GROUP
-        + [pl.BlockSpec((own.shape[0], block), lambda i: (0, i + shift))]
-        + [pl.BlockSpec((half, block), lambda i: (0, i)) for w in weights],
-        out_specs=[pl.BlockSpec((2 * rows, block), lambda i: (0, i))] * 2,
+        functools.partial(project_kernel, skip, shift, depths, len(start)),
+        out_shape=[jax.ShapeDtypeStruct((n, columns), t) for n, t in out],
+        in_specs=[whole()] * (len(acts) + len(start) + len(weights)),
+        out_specs=[whole()] * len(out),
         compiler_params=params(),
         cost_estimate=pl.CostEstimate(
-            flops=2 * GROUP * rows * depth * features,
-            bytes_accessed=2 * depth * (GROUP * rows + features) + 6 * GROUP * rows * features,
+            flops=2 * GROUP * rows * sum(depths) * columns,
+            bytes_accessed=2 * sum(depths) * (GROUP * rows + columns) + 6 * GROUP * rows * columns,
             transcendentals=0,
         ),
         name="project",
-    )(*acts, own, *weights)
+    )(*acts, *start, *weights)
 
 
 def by_request(*shape):
@@ -152,11 +151,11 @@
     return jnp.concatenate(heads, axis=0).astype(jnp.bfloat16)
 
 
-def cached_kernel(per_dev, place_ref, home_ref, ids_ref, rows_ref, count_ref, q_ref, *refs):
+def cached_kernel(per_dev, maxp, place_ref, home_ref, ids_ref, rows_ref, count_ref, q_ref, *refs):
     sources, (query_pos_ref, out_ref, stat_ref, stacked_ref, pages, context, bias, sems) = refs[:-8], refs[-8:]
     r = pl.program_id(0)
-    maxp = ids_ref.shape[1]
     plen = context.shape[1] // maxp
+    per_pass = q_ref.shape[1] // maxp
 
     @pl.when(r == 0)
     def _():
@@ -172,40 +171,44 @@
             copy.wait()
 
     for m in range(maxp):
-        slot = home_ref[ids_ref[r, m]]
+        slot = home_ref[ids_ref[r * maxp + m]]
         block = place_ref[slot // per_dev] * (2 * per_dev) + slot % per_dev
         for c in range(2):
             at = pl.multiple_of((block + c * per_dev) * plen, plen)
             context[c, m * plen : (m + 1) * plen, :] = pages[pl.ds(at, plen), :]
-    per_pass = rows_ref.shape[1] // maxp
     row = lax.broadcasted_iota(jnp.int32, (plen, bias.shape[1]), 0)
     for m in range(maxp):
         hidden = m >= count_ref[r]
         for i in range(per_pass):
-            hidden = hidden | (row == rows_ref[r, m * per_pass + i])
+            hidden = hidden | (row == rows_ref[(r * maxp + m) * per_pass + i])
         key_pos = jnp.where(hidden, NEVER, row + m * plen)
         bias[m * plen : (m + 1) * plen, :] = jnp.where(key_pos <= query_pos_ref[0], 0.0, HIDDEN)
-    for g in range(KEY_VALUE_HEADS):
-        keys = context[0, :, g * HEAD_SIZE : (g + 1) * HEAD_SIZE]
-        values = context[1, :, g * HEAD_SIZE : (g + 1) * HEAD_SIZE]
+    heads = [slice(g * HEAD_SIZE, (g + 1) * HEAD_SIZE) for g in range(KEY_VALUE_HEADS)]
+    scores = []
+    for g, head in enumerate(heads):
         q = stacked_queries(q_ref, g)
         stacked_ref[0, g] = q
-        s = against(keys, q, ((1,), (1,))) * EXP2_SCALE + bias[...]
+        scores.append(against(context[0, :, head], q, ((1,), (1,))))
+    weights = []
+    for g, s in enumerate(scores):
+        s = s * EXP2_SCALE + bias[...]
         top = jnp.max(s, axis=0, keepdims=True)
         e = jnp.exp2(s - top)
         stat_ref[0, g, 0:1] = top
         stat_ref[0, g, 1:2] = jnp.sum(e, axis=0, keepdims=True)
-        out_ref[0, g] = against(values, e.astype(jnp.bfloat16), ((0,), (0,)))
-
-
-def cached_attention(per_dev, plen, place, home, ids, sources, rows, count, queries, query_pos):
+        weights.append(e.astype(jnp.bfloat16))
+    for g, head in enumerate(heads):
+        out_ref[0, g] = against(context[1, :, head], weights[g], ((0,), (0,)))
+
+
+def cached_attention(per_dev, maxp, plen, place, home, ids, sources, rows, count, queries, query_pos):
     owned, selected, width = queries.shape
     stacked = HEAD_GROUP * selected
-    context = ids.shape[1] * plen
+    context = maxp * plen
     features = sources[0].shape[1]
     heads = KEY_VALUE_HEADS
     return pl.pallas_call(
-        functools.partial(cached_kernel, per_dev),
+        functools.partial(cached_kernel, per_dev, maxp),
         out_shape=[
             jax.ShapeDtypeStruct((owned, heads, HEAD_SIZE, stacked), jnp.float32),
             jax.ShapeDtypeStruct((owned, heads, 2, stacked), jnp.float32),
@@ -246,12 +249,12 @@
     return total.astype(jnp.bfloat16)
 
 
-def fresh_kernel(
-    maxp, count_ref, q_ref, k0, k1, k2, v0, v1, v2, query_pos_ref, part_ref, stat_ref, out_ref,
-):
+def fresh_kernel(maxp, count_ref, q_ref, *refs):
+    terms, (query_pos_ref, part_ref, stat_ref, out_ref) = refs[:-4], refs[-4:]
     r = pl.program_id(0)
-    fresh_keys = added(k0, k1, k2)
-    fresh_values = added(v0, v1, v2)
+    half = len(terms) // 2
+    fresh = jnp.concatenate([added(*terms[:half]), added(*terms[half:])], axis=1)
+    fresh_keys, fresh_values = fresh[:, : fresh.shape[1] // 2], fresh[:, fresh.shape[1] // 2 :]
     rows = fresh_keys.shape[0]
     per_pass = rows // maxp
     slot = lax.broadcasted_iota(jnp.int32, (rows, HEAD_SIZE), 0) // per_pass
@@ -259,17 +262,21 @@
     across = jnp.broadcast_to(query_pos_ref[0, :, :HEAD_SIZE], (HEAD_SIZE, HEAD_SIZE))
     key_pos = jnp.where(live, across.T[:rows], NEVER)[:, :1]
     bias = jnp.where(key_pos <= query_pos_ref[0], 0.0, HIDDEN)
-    for g in range(KEY_VALUE_HEADS):
-        keys = fresh_keys[:, g * HEAD_SIZE : (g + 1) * HEAD_SIZE]
-        values = fresh_values[:, g * HEAD_SIZE : (g + 1) * HEAD_SIZE]
-        s = against(keys, q_ref[0, g], ((1,), (1,))) * EXP2_SCALE + bias
+    heads = [slice(g * HEAD_SIZE, (g + 1) * HEAD_SIZE) for g in range(KEY_VALUE_HEADS)]
+    scores = [against(fresh_keys[:, head], q_ref[0, g], ((1,), (1,))) for g, head in enumerate(heads)]
+    weights, factors = [], []
+    for g, s in enumerate(scores):
+        s = s * EXP2_SCALE + bias
         top1 = stat_ref[0, g, 0:1]
         top = jnp.maximum(top1, jnp.max(s, axis=0, keepdims=True))
         e = jnp.exp2(s - top)
         keep = jnp.exp2(top1 - top)
-        inv = 1.0 / (stat_ref[0, g, 1:2] * keep + jnp.sum(e, axis=0, keepdims=True))
-        term = against(values, e.astype(jnp.bfloat16), ((0,), (0,)))
-        result = ((part_ref[0, g] * keep + term) * inv).T
+        total = stat_ref[0, g, 1:2] * keep + jnp.sum(e, axis=0, keepdims=True)
+        weights.append(e.astype(jnp.bfloat16))
+        factors.append((keep, 1.0 / total))
+    terms = [against(fresh_values[:, head], weights[g], ((0,), (0,))) for g, head in enumerate(heads)]
+    for g, (keep, inv) in enumerate(factors):
+        result = ((part_ref[0, g] * keep + terms[g]) * inv).T
         for i in range(HEAD_GROUP):
             at = (g * HEAD_GROUP + i) * HEAD_SIZE
             one = result[i * rows : (i + 1) * rows]
@@ -278,7 +285,7 @@
 
 def fresh_attention(maxp, count, queries, terms, query_pos, part, stat):
     owned, heads, stacked, _ = queries.shape
-    rows, features = terms[0].shape[1:]
+    rows = terms[0].shape[1]
     width = QUERY_HEADS * HEAD_SIZE
     return pl.pallas_call(
         functools.partial(fresh_kernel, maxp),
@@ -287,7 +294,7 @@
         in_specs=[
             smem(),
             by_request(heads, stacked, HEAD_SIZE),
-            *[by_request(rows, features)] * 6,
+            *[by_request(*t.shape[1:]) for t in terms],
             by_request(1, stacked),
             by_request(heads, HEAD_SIZE, stacked),
             by_request(heads, 2, stacked),
@@ -328,12 +335,13 @@
     depth, features = kv_weight.shape
     local, plen, _, kvw = store_pages.shape
     half = depth // 2
-    columns = features // 2
+    split = features // 2
     count = owned * selected
 
     pages = store_pages.reshape(local * plen, 2, kvw)
     mine = [
-        lax.dynamic_slice(kv_weight, (side * half, n * columns), (half, columns)) for n in range(2)
+        lax.dynamic_slice(kv_weight, (side * half, first), (half, columns))
+        for first, columns in ((0, split), (split, features - split))
     ]
     own = jnp.concatenate([pages[:, 0], pages[:, 1]], axis=0)
     a0 = jnp.concatenate([mine[0], own], axis=0)
@@ -373,13 +381,17 @@
     y_column_far = flip(y_column, 1)
     acts = [acts[0], near_act, y_acts, y_far]
 
-    chunks = [[a1, xa1, a2, xa2, a3, xa3], [b1, xb1, b2, xb2, b3, xb3]]
+    depths = (depth,) + (half,) * (2 * ring - 2)
     terms = []
-    for n in range(2):
-        keep, out = project(acts, kv_weight, n, chunks[n], half)
-        back = flip(out, 1)
-        y_out = (keep[count:] + back[count:].astype(jnp.float32)).astype(jnp.bfloat16)
-        terms += [keep[:count], back[:count], flip(y_out, 2)]
+    begun = project(acts, 0, 0, [kv_weight, a1, xa1, a2, xa2, a3], depths[:-1], split, (), False)
+    keep, out = project(acts, width // GROUP - half, 0, [xa3], depths[-1:], split, begun)
+    back = flip(out, 1)
+    y_out = (keep[count:] + back[count:].astype(jnp.float32)).astype(jnp.bfloat16)
+    terms += [keep, back, flip(y_out, 2)]
+    keep, out = project(acts, 0, split, [kv_weight, b1, xb1, b2, xb2, b3, xb3], depths, features - split)
+    back = flip(out, 1)
+    y_out = (keep[count:] + back[count:].astype(jnp.float32)).astype(jnp.bfloat16)
+    terms += [keep, back, flip(y_out, 2)]
     return small, (place, [column, y_column, far, y_column_far]), terms
 
 
@@ -417,7 +429,7 @@
     arrived = arrived.transpose(0, 2, 1, 3).reshape(shards * cap * 2 * plen, kvw)
     place = jnp.arange(shards * cap, dtype=jnp.int32)
     home = (my_shard * cap + my_rank).astype(jnp.int32)
-    ids = jnp.arange(positions, dtype=jnp.int32).reshape(owned, passage_ids.shape[1])
+    ids = jnp.arange(positions, dtype=jnp.int32)
     return place, home, ids, [arrived]
 
 
@@ -439,9 +451,10 @@
     ringed = shards == 4 * GROUP and lax.axis_size("parts") == 2 and kv_weight.shape[0] % 512 == 0
     rows = lax.dynamic_slice_in_dim(recompute_rows, me * owned, owned, 0)
     query_pos = query_positions(rows, plen)
-    flat_rows = rows.reshape(owned, selected)
+    flat_rows = rows.reshape(-1)
+    maxp = passage_ids.shape[1]
     if ringed:
-        ids = lax.dynamic_slice_in_dim(passage_ids, me * owned, owned, 0)
+        ids = lax.dynamic_slice_in_dim(passage_ids, me * owned, owned, 0).reshape(-1)
         small, (place, sources), terms = ring_plan(
             rows_in, norm_gain, kv_weight, store_pages, [ids, flat_rows, query_pos]
         )
@@ -453,10 +466,9 @@
         pages = sent_pages(store_pages, passage_home, passage_ids)
         per_dev = 1
     part, stat, stacked = cached_attention(
-        per_dev, plen, *pages, flat_rows, passage_count, queries, query_pos
+        per_dev, maxp, plen, *pages, flat_rows, passage_count, queries, query_pos
     )
-    terms = [t.reshape(owned, selected, t.shape[1]) for t in terms]
-    maxp = passage_ids.shape[1]
+    terms = [t.reshape(-1, selected, t.shape[1]) for t in terms]
     return fresh_attention(maxp, passage_count, stacked, terms, query_pos, part, stat)
 
 

time: 88.5 us -> 81.1 us (0.916)
  Pallas kernels: 22 us -> 16.5 us
  local copies, waits for them, and re-layouts: 9.62 us -> 4.95 us
  waiting for transfers between devices: 34.4 us -> 38.5 us
  other arithmetic: 2.54 us -> 1.07 us
    pallas_call x3 -> x4, Pallas kernels: 12.3 us -> 8.79 us  [the longest x1 5.48 us: cached_attention(): pl.pallas_call(functools.partial(cached_kernel, per_dev, maxp), out_shape...]
    ppermute x10, waiting for transfers between devices: 0.03 us -> 2.97 us  [flip(): return lax.ppermute(x, 'store', pairs)]
    unnamed x25 -> x21, local copies, waits for them, and re-layouts: 5.29 us -> 2.72 us
    ppermute x6, waiting for transfers between devices: 29.3 us -> 31.4 us  [send(): return lax.ppermute(x, 'store', pairs)]
    pallas_call x1, Pallas kernels: 5.59 us -> 3.7 us  [fresh_attention(): pl.pallas_call(functools.partial(fresh_kernel, maxp), out_shape=jax.Shape...]
    slice x2 -> x0, local copies, waits for them, and re-layouts: 1.86 us -> none  [ring_plan(): terms += [keep[:count], back[:count], flip(y_out, 2)]]
    convert_element_type x2, other arithmetic: 1.55 us -> 0.08 us  [ring_plan(): (keep[count:] + back[count:].astype(jnp.float32)).astype(jnp.bfloat16)]
    ppermute x6, waiting for transfers between devices: 5.09 us -> 4.14 us  [swap(): return lax.ppermute(x, 'parts', [(0, 1), (1, 0)])]
  transfers between devices with their start and end apart: 22 -> 22, of which waited for: 8 -> 10; matrix products, arithmetic and copies ran while one was open for 11% -> 4% of each run, Pallas kernels for 19% -> 16%
where the time goes in v4:
time: 81.1 us; the launch traced here: 80.9 us
  waiting for transfers between devices  38.5 us (47%)
  starting transfers between devices  19.6 us (24%)
  Pallas kernels  16.5 us (20%)
  local copies, waits for them, and re-layouts  4.95 us (6%)
  other arithmetic  1.07 us (1%)
    ppermute x6, waiting for transfers between devices, send(): return lax.ppermute(x, 'store', pairs)  31.4 us
    ppermute x6, starting transfers between devices, swap(): return lax.ppermute(x, 'parts', [(0, 1), (1, 0)])  8.72 us
    pallas_call x1, Pallas kernels, cached_attention(): pl.pallas_call(functools.partial(cached_kernel, per_dev, maxp), out_shape...  5.48 us
    ppermute x10, starting transfers between devices, flip(): return lax.ppermute(x, 'store', pairs)  5.46 us
    ppermute x6, starting transfers between devices, send(): return lax.ppermute(x, 'store', pairs)  5.4 us
    ppermute x6, waiting for transfers between devices, swap(): return lax.ppermute(x, 'parts', [(0, 1), (1, 0)])  4.14 us
    pallas_call x1, Pallas kernels, norm_rows(): pl.pallas_call(functools.partial(norm_kernel, chunk, chunks), out_shape=[...  4.06 us
    pallas_call x1, Pallas kernels, fresh_attention(): pl.pallas_call(functools.partial(fresh_kernel, maxp), out_shape=jax.Shape...  3.7 us
  transfers between devices with their start and end apart: 22, of which 10 were waited for; matrix products, arithmetic and copies ran while one was open for 4% of the time, Pallas kernels for 16%

profile of v4, /device:TPU:0, one launch (start us, length us, event | category | flops | bytes accessed | tf_op | source)
XLA Modules:
  0.0 80.9 jit_solution(14636207212842075159)
XLA Ops:
  0.0 1.1 %constant_dynamic-slice_fusion.3 = (bf16[256,512]{1,0:T(8,128)(2,1)S(1)}, bf16[256,512]{1,0:T(8,128)(2,1)S(1)}) fusion(bf16[512,1024]{1,0:T(8,128)(2,1)} %refs_4_.3, s32[]{:T(128)S(6)} %select_n.97), kind=kLoop, calls=%fused_computation.55 | loop fusion | bytes 1048580 | tf_op jit(solution)/shard_map/dynamic_slice | solution.py:343
  1.1 3.1 %collective-permute-start.2 = (bf16[256,512]{1,0:T(8,128)(2,1)S(1)}, bf16[256,512]{1,0:T(8,128)(2,1)S(1)}, u32[]{:S(2)}, u32[]{:S(2)}) collective-permute-start(bf16[256,512]{1,0:T(8,128)(2,1)S(1)} %get-tuple-element.61), channel_id=1, source_target_pairs={{0,4},{1,5},{2,6},{3,7},{4,8},{5,9},{6,10},{7,11},{8,12},{9,13},{1... | collective-permute-start | bytes 786440 | tf_op jit(solution)/shard_map/ppermute | solution.py:37
  4.2 0.9 %copy.12 = bf16[4,16,2,512]{3,1,0,2:T(8,128)(2,1)S(1)} copy(bf16[4,16,2,512]{3,2,1,0:T(2,128)(2,1)} %param.13) | data formatting | bytes 262144 | tf_op args[4]
  5.2 0.8 pad_maximum_fusion
  6.1 1.7 %copy-done.2 = bf16[4,40,8192]{2,1,0:T(8,128)(2,1)S(1)} copy-done((bf16[4,40,8192]{2,1,0:T(8,128)(2,1)S(1)}, bf16[4,40,8192]{2,1,0:T(8,128)(2,1)}, u32[]{:S(2)}) %copy-start.2) | copy-done | bytes 2621464
  7.9 4.1 %norm.1 = (bf16[160,2048]{1,0:T(8,128)(2,1)S(1)}, bf16[2,160,2048]{2,1,0:T(8,128)(2,1)}, bf16[160,2048]{1,0:T(8,128)(2,1)}) custom-call(s32[32]{0:T(128)S(1)} %and_select_fusion.6.offs_ref, bf16[160,8192]{1,0:T(8,128)(2,1)S(1)} %bitcast.18, bf16[1,8192]{1,0:T(2,128)(2,1)S(1)} %reshape.134.gain_ref), custom_call_target="tpu_custom_call" | custom-call | flops 7864320 | bytes 5242880 | tf_op jit(solution)/shard_map/norm/pallas_call | solution.py:72
  11.9 0.6 collective-permute-done.2.refs_5_
  12.5 1.5 %collective-permute-start.6 = (bf16[320,2048]{1,0:T(8,128)(2,1)}, bf16[320,2048]{1,0:T(8,128)(2,1)S(1)}, u32[]{:S(2)}, u32[]{:S(2)}) collective-permute-start(bf16[320,2048]{1,0:T(8,128)(2,1)} %bitcast.5), channel_id=1, source_target_pairs={{0,2},{1,3},{2,0},{3,1},{4,6},{5,7},{6,4},{7,5},{8,10},{9,11},{10,... | collective-permute-start | bytes 3932168 | tf_op jit(solution)/shard_map/ppermute | solution.py:42
  14.0 1.0 %collective-permute-start = (bf16[384,512]{1,0:T(8,128)(2,1)}, bf16[384,512]{1,0:T(8,128)(2,1)S(1)}, u32[]{:S(2)}, u32[]{:S(2)}) collective-permute-start(bf16[384,512]{1,0:T(8,128)(2,1)} %pad_maximum_fusion), channel_id=1, source_target_pairs={{0,4},{1,5},{2,6},{3,7},{4,8},{5,9},{6,10},{7,11},{8,12},{9,13},{1... | collective-permute-start | bytes 1179656 | tf_op jit(solution)/shard_map/ppermute | solution.py:37
  16.1 1.6 %collective-permute-start.9 = (bf16[256,512]{1,0:T(8,128)(2,1)S(1)}, bf16[256,512]{1,0:T(8,128)(2,1)S(1)}, u32[]{:S(2)}, u32[]{:S(2)}) collective-permute-start(bf16[256,512]{1,0:T(8,128)(2,1)S(1)} %collective-permute-done.2.refs_5_), channel_id=1, source_target_pairs={{0,16},{16,0},{1,17},{17,1},{2,18},{18,2},{3,19},{19,3},{4,20},{20... | collective-permute-start | bytes 786440 | tf_op jit(solution)/shard_map/ppermute | solution.py:46
  17.6 8.2 %collective-permute-done.refs_5_ = bf16[384,512]{1,0:T(8,128)(2,1)S(1)} collective-permute-done((bf16[384,512]{1,0:T(8,128)(2,1)}, bf16[384,512]{1,0:T(8,128)(2,1)S(1)}, u32[]{:S(2)}, u32[]{:S(2)}) %collective-permute-start) | collective-permute-done | bytes 393248 | tf_op jit(solution)/shard_map/ppermute | solution.py:37
  25.8 1.6 %collective-permute-start.4 = (bf16[256,512]{1,0:T(8,128)(2,1)S(1)}, bf16[256,512]{1,0:T(8,128)(2,1)S(1)}, u32[]{:S(2)}, u32[]{:S(2)}) collective-permute-start(bf16[256,512]{1,0:T(8,128)(2,1)S(1)} %slice.43), channel_id=1, source_target_pairs={{0,16},{16,0},{1,17},{17,1},{2,18},{18,2},{3,19},{19,3},{4,20},{20... | collective-permute-start | bytes 786440 | tf_op jit(solution)/shard_map/ppermute | solution.py:46
  27.4 1.3 %collective-permute-start.3 = (bf16[384,512]{1,0:T(8,128)(2,1)S(1)}, bf16[384,512]{1,0:T(8,128)(2,1)S(1)}, u32[]{:S(2)}, u32[]{:S(2)}) collective-permute-start(bf16[384,512]{1,0:T(8,128)(2,1)S(1)} %collective-permute-done.refs_5_), channel_id=1, source_target_pairs={{0,4},{1,5},{2,6},{3,7},{4,8},{5,9},{6,10},{7,11},{8,12},{9,13},{1... | collective-permute-start | bytes 1179656 | tf_op jit(solution)/shard_map/ppermute | solution.py:37
  28.7 8.1 %collective-permute-done.8.refs_7_ = bf16[256,512]{1,0:T(8,128)(2,1)S(1)} collective-permute-done((bf16[256,512]{1,0:T(8,128)(2,1)S(1)}, bf16[256,512]{1,0:T(8,128)(2,1)S(1)}, u32[]{:S(2)}, u32[]{:S(2)}) %collective-permute-start.8) | collective-permute-done | bytes 262176 | tf_op jit(solution)/shard_map/ppermute | solution.py:37
  36.9 1.5 %collective-permute-start.18 = (bf16[256,512]{1,0:T(8,128)(2,1)S(1)}, bf16[256,512]{1,0:T(8,128)(2,1)S(1)}, u32[]{:S(2)}, u32[]{:S(2)}) collective-permute-start(bf16[256,512]{1,0:T(8,128)(2,1)S(1)} %collective-permute-done.8.refs_7_), channel_id=1, source_target_pairs={{0,16},{16,0},{1,17},{17,1},{2,18},{18,2},{3,19},{19,3},{4,20},{20... | collective-permute-start | bytes 786440 | tf_op jit(solution)/shard_map/ppermute | solution.py:46
  38.3 6.9 %collective-permute-done.3.refs_7_ = bf16[384,512]{1,0:T(8,128)(2,1)S(1)} collective-permute-done((bf16[384,512]{1,0:T(8,128)(2,1)S(1)}, bf16[384,512]{1,0:T(8,128)(2,1)S(1)}, u32[]{:S(2)}, u32[]{:S(2)}) %collective-permute-start.3) | collective-permute-done | bytes 393248 | tf_op jit(solution)/shard_map/ppermute | solution.py:37
  45.5 1.6 %collective-permute-start.14 = (bf16[256,512]{1,0:T(8,128)(2,1)S(1)}, bf16[256,512]{1,0:T(8,128)(2,1)S(1)}, u32[]{:S(2)}, u32[]{:S(2)}) collective-permute-start(bf16[256,512]{1,0:T(8,128)(2,1)S(1)} %slice.57), channel_id=1, source_target_pairs={{0,16},{16,0},{1,17},{17,1},{2,18},{18,2},{3,19},{19,3},{4,20},{20... | collective-permute-start | bytes 786440 | tf_op jit(solution)/shard_map/ppermute | solution.py:46
  47.0 3.9 %collective-permute-done.10.refs_9_ = bf16[256,512]{1,0:T(8,128)(2,1)S(1)} collective-permute-done((bf16[256,512]{1,0:T(8,128)(2,1)S(1)}, bf16[256,512]{1,0:T(8,128)(2,1)S(1)}, u32[]{:S(2)}, u32[]{:S(2)}) %collective-permute-start.10) | collective-permute-done | bytes 262176 | tf_op jit(solution)/shard_map/ppermute | solution.py:37
  50.9 1.5 %collective-permute-start.19 = (bf16[256,512]{1,0:T(8,128)(2,1)S(1)}, bf16[256,512]{1,0:T(8,128)(2,1)S(1)}, u32[]{:S(2)}, u32[]{:S(2)}) collective-permute-start(bf16[256,512]{1,0:T(8,128)(2,1)S(1)} %collective-permute-done.10.refs_9_), channel_id=1, source_target_pairs={{0,16},{16,0},{1,17},{17,1},{2,18},{18,2},{3,19},{19,3},{4,20},{20... | collective-permute-start | bytes 786440 | tf_op jit(solution)/shard_map/ppermute | solution.py:46
  52.4 3.7 %collective-permute-done.5.refs_9_ = bf16[384,512]{1,0:T(8,128)(2,1)S(1)} collective-permute-done((bf16[384,512]{1,0:T(8,128)(2,1)S(1)}, bf16[384,512]{1,0:T(8,128)(2,1)S(1)}, u32[]{:S(2)}, u32[]{:S(2)}) %collective-permute-start.5) | collective-permute-done | bytes 393248 | tf_op jit(solution)/shard_map/ppermute | solution.py:37
  56.1 1.1 %collective-permute-start.7 = (bf16[512,512]{1,0:T(8,128)(2,1)S(1)}, bf16[512,512]{1,0:T(8,128)(2,1)S(1)}, u32[]{:S(2)}, u32[]{:S(2)}) collective-permute-start(bf16[512,512]{1,0:T(8,128)(2,1)S(1)} %slice_dynamic-update-slice_fusion.refs_0_), channel_id=1, source_target_pairs={{0,2},{1,3},{2,0},{3,1},{4,6},{5,7},{6,4},{7,5},{8,10},{9,11},{10,... | collective-permute-start | bytes 1572872 | tf_op jit(solution)/shard_map/ppermute | solution.py:42
  57.2 1.1 %collective-permute-start.15 = (bf16[256,512]{1,0:T(8,128)(2,1)S(1)}, bf16[256,512]{1,0:T(8,128)(2,1)S(1)}, u32[]{:S(2)}, u32[]{:S(2)}) collective-permute-start(bf16[256,512]{1,0:T(8,128)(2,1)S(1)} %slice.58), channel_id=1, source_target_pairs={{0,16},{16,0},{1,17},{17,1},{2,18},{18,2},{3,19},{19,3},{4,20},{20... | collective-permute-start | bytes 786440 | tf_op jit(solution)/shard_map/ppermute | solution.py:46
  58.3 2.0 %collective-permute-done.19.refs_10_ = bf16[256,512]{1,0:T(8,128)(2,1)S(1)} collective-permute-done((bf16[256,512]{1,0:T(8,128)(2,1)S(1)}, bf16[256,512]{1,0:T(8,128)(2,1)S(1)}, u32[]{:S(2)}, u32[]{:S(2)}) %collective-permute-start.19) | collective-permute-done | bytes 262176 | tf_op jit(solution)/shard_map/ppermute | solution.py:46
  60.3 1.6 %project.5 = (f32[320,512]{1,0:T(8,128)S(1)}, bf16[320,512]{1,0:T(8,128)(2,1)S(1)}) custom-call(bf16[160,2048]{1,0:T(8,128)(2,1)S(1)} %get-tuple-element.51.refs_0_, bf16[160,2048]{1,0:T(8,128)(2,1)S(1)} %collective-permute-done.1.refs_1_, bf16[320,2048]{1,0:T(8,128)(2,1)S(1)} %collective-permute-done.6.refs_2_, ...), custom_call_target="tpu_custom_call" | custom-call | flops 1342177280 | bytes 6684672 | tf_op jit(solution)/shard_map/project/pallas_call | solution.py:124
  61.9 1.4 %project.3.refs_4_ = f32[640,512]{1,0:T(8,128)S(1)} custom-call(bf16[160,2048]{1,0:T(8,128)(2,1)S(1)} %get-tuple-element.51.refs_0_, bf16[160,2048]{1,0:T(8,128)(2,1)S(1)} %collective-permute-done.1.refs_1_, bf16[320,2048]{1,0:T(8,128)(2,1)S(1)} %collective-permute-done.6.refs_2_, bf16[160,2048]{1,0:T(8,128)(2,1)S(1)} %collective-permute-done.13.refs_3_, ...), custom_call_target="tpu_custom_call" | custom-call | flops 1174405120 | bytes 6094848 | tf_op jit(solution)/shard_map/project/pallas_call | solution.py:124
  63.3 2.2 %collective-permute-done.15.refs_5_ = bf16[256,512]{1,0:T(8,128)(2,1)S(1)} collective-permute-done((bf16[256,512]{1,0:T(8,128)(2,1)S(1)}, bf16[256,512]{1,0:T(8,128)(2,1)S(1)}, u32[]{:S(2)}, u32[]{:S(2)}) %collective-permute-start.15) | collective-permute-done | bytes 262176 | tf_op jit(solution)/shard_map/ppermute | solution.py:46
  65.9 0.5 collective-permute-start.11
  67.0 1.3 %collective-permute-start.21 = (bf16[160,512]{1,0:T(8,128)(2,1)S(1)}, bf16[160,512]{1,0:T(8,128)(2,1)S(1)}, u32[]{:S(2)}, u32[]{:S(2)}) collective-permute-start(bf16[160,512]{1,0:T(8,128)(2,1)S(1)} %add_convert_fusion), channel_id=1, source_target_pairs={{0,2},{1,3},{2,0},{3,1},{4,6},{5,7},{6,4},{7,5},{8,10},{9,11},{10,... | collective-permute-start | bytes 491528 | tf_op jit(solution)/shard_map/ppermute | solution.py:42
  68.4 0.8 %collective-permute-start.17 = (bf16[160,512]{1,0:T(8,128)(2,1)S(1)}, bf16[160,512]{1,0:T(8,128)(2,1)S(1)}, u32[]{:S(2)}, u32[]{:S(2)}) collective-permute-start(bf16[160,512]{1,0:T(8,128)(2,1)S(1)} %add_convert_fusion.1), channel_id=1, source_target_pairs={{0,2},{1,3},{2,0},{3,1},{4,6},{5,7},{6,4},{7,5},{8,10},{9,11},{10,... | collective-permute-start | bytes 491528 | tf_op jit(solution)/shard_map/ppermute | solution.py:42
  69.2 5.5 %cached_attention.1 = (f32[4,4,128,320]{3,2,1,0:T(8,128)S(1)}, f32[4,4,2,320]{3,2,1,0:T(2,128)S(1)}, bf16[4,4,320,128]{3,2,1,0:T(8,128)(2,1)S(1)}) custom-call(s32[16]{0:T(128)S(1)} %fusion.place_ref, s32[64]{0:T(128)S(1)} %copy-done.5, s32[80]{0:T(128)S(1)} %reshape.135.ids_ref, s32[160]{0:T(256)S(1)} %reshape.136.rows_ref, s32[4]{0:T(128)S(1)} %copy-done.4, ...), custom_call_target="tpu_custom_call" | custom-call | flops 838860800 | bytes 4718592 | tf_op jit(solution)/shard_map/cached_attention/pallas_call | solution.py:210
  74.7 2.4 %collective-permute-done.17 = bf16[160,512]{1,0:T(8,128)(2,1)S(1)} collective-permute-done((bf16[160,512]{1,0:T(8,128)(2,1)S(1)}, bf16[160,512]{1,0:T(8,128)(2,1)S(1)}, u32[]{:S(2)}, u32[]{:S(2)}) %collective-permute-start.17) | collective-permute-done | bytes 163872 | tf_op jit(solution)/shard_map/ppermute | solution.py:42
  77.2 3.7 %fresh_attention.1 = bf16[4,40,4096]{2,1,0:T(8,128)(2,1)} custom-call(s32[4]{0:T(128)S(1)} %copy-done.4, bf16[4,4,320,128]{3,2,1,0:T(8,128)(2,1)S(1)} %get-tuple-element.50.q_ref, f32[8,40,512]{2,1,0:T(8,128)S(1)} %bitcast.20, bf16[8,40,512]{2,1,0:T(8,128)(2,1)S(1)} %bitcast.22, bf16[4,40,512]{2,1,0:T(8,128)(2,1)S(1)} %bitcast.24, ...), custom_call_target="tpu_custom_call" | custom-call | flops 104857600 | bytes 5242880 | tf_op jit(solution)/shard_map/fresh_attention/pallas_call | solution.py:290
  (67 shorter events, 2.6 us)
Async XLA Ops:
  0.0 15.0 %copy-start = (s32[64,20,2]{0,2,1:T(2,128)S(1)}, s32[64,20,2]{0,2,1:T(2,128)}, u32[]{:S(2)}) copy-start(s32[64,20,2]{0,2,1:T(2,128)} %param.17) | copy-start | bytes 30724
  0.0 6.1 %copy-start.6 = (bf16[8192]{0:T(1024)(128)(2,1)S(1)}, bf16[8192]{0:T(1024)(128)(2,1)}, u32[]{:S(2)}) copy-start(bf16[8192]{0:T(1024)(128)(2,1)} %param.10) | copy-start | bytes 49156
  1.1 11.4 %collective-permute-start.2 = (bf16[256,512]{1,0:T(8,128)(2,1)S(1)}, bf16[256,512]{1,0:T(8,128)(2,1)S(1)}, u32[]{:S(2)}, u32[]{:S(2)}) collective-permute-start(bf16[256,512]{1,0:T(8,128)(2,1)S(1)} %get-tuple-element.61), channel_id=1, source_target_pairs={{0,4},{1,5},{2,6},{3,7},{4,8},{5,9},{6,10},{7,11},{8,12},{9,13},{1... | collective-permute-start | bytes 786440 | tf_op jit(solution)/shard_map/ppermute | solution.py:37
  6.1 1.7 %copy-start.2 = (bf16[4,40,8192]{2,1,0:T(8,128)(2,1)S(1)}, bf16[4,40,8192]{2,1,0:T(8,128)(2,1)}, u32[]{:S(2)}) copy-start(bf16[4,40,8192]{2,1,0:T(8,128)(2,1)} %param.9) | copy-start | bytes 7864324
  7.9 7.9 %copy-start.7 = (s32[64,20]{0,1:T(8,128)S(1)}, s32[64,20]{0,1:T(8,128)}, u32[]{:S(2)}) copy-start(s32[64,20]{0,1:T(8,128)} %param.15) | copy-start | bytes 15364
  12.5 32.8 %collective-permute-start.6 = (bf16[320,2048]{1,0:T(8,128)(2,1)}, bf16[320,2048]{1,0:T(8,128)(2,1)S(1)}, u32[]{:S(2)}, u32[]{:S(2)}) collective-permute-start(bf16[320,2048]{1,0:T(8,128)(2,1)} %bitcast.5), channel_id=1, source_target_pairs={{0,2},{1,3},{2,0},{3,1},{4,6},{5,7},{6,4},{7,5},{8,10},{9,11},{10,... | collective-permute-start | bytes 3932168 | tf_op jit(solution)/shard_map/ppermute | solution.py:42
  14.0 11.8 %collective-permute-start = (bf16[384,512]{1,0:T(8,128)(2,1)}, bf16[384,512]{1,0:T(8,128)(2,1)S(1)}, u32[]{:S(2)}, u32[]{:S(2)}) collective-permute-start(bf16[384,512]{1,0:T(8,128)(2,1)} %pad_maximum_fusion), channel_id=1, source_target_pairs={{0,4},{1,5},{2,6},{3,7},{4,8},{5,9},{6,10},{7,11},{8,12},{9,13},{1... | collective-permute-start | bytes 1179656 | tf_op jit(solution)/shard_map/ppermute | solution.py:37
  15.0 10.8 %collective-permute-start.1 = (bf16[160,2048]{1,0:T(8,128)(2,1)}, bf16[160,2048]{1,0:T(8,128)(2,1)S(1)}, u32[]{:S(2)}, u32[]{:S(2)}) collective-permute-start(bf16[160,2048]{1,0:T(8,128)(2,1)} %get-tuple-element.34), channel_id=1, source_target_pairs={{0,1},{1,0},{2,3},{3,2},{4,5},{5,4},{6,7},{7,6},{8,9},{9,8},{10,11... | collective-permute-start | bytes 1966088 | tf_op jit(solution)/shard_map/ppermute | solution.py:42
  16.1 12.6 %collective-permute-start.9 = (bf16[256,512]{1,0:T(8,128)(2,1)S(1)}, bf16[256,512]{1,0:T(8,128)(2,1)S(1)}, u32[]{:S(2)}, u32[]{:S(2)}) collective-permute-start(bf16[256,512]{1,0:T(8,128)(2,1)S(1)} %collective-permute-done.2.refs_5_), channel_id=1, source_target_pairs={{0,16},{16,0},{1,17},{17,1},{2,18},{18,2},{3,19},{19,3},{4,20},{20... | collective-permute-start | bytes 786440 | tf_op jit(solution)/shard_map/ppermute | solution.py:46
  25.8 11.0 %collective-permute-start.8 = (bf16[256,512]{1,0:T(8,128)(2,1)S(1)}, bf16[256,512]{1,0:T(8,128)(2,1)S(1)}, u32[]{:S(2)}, u32[]{:S(2)}) collective-permute-start(bf16[256,512]{1,0:T(8,128)(2,1)S(1)} %collective-permute-done.2.refs_5_), channel_id=1, source_target_pairs={{0,4},{1,5},{2,6},{3,7},{4,8},{5,9},{6,10},{7,11},{8,12},{9,13},{1... | collective-permute-start | bytes 786440 | tf_op jit(solution)/shard_map/ppermute | solution.py:37
  25.8 12.5 %collective-permute-start.4 = (bf16[256,512]{1,0:T(8,128)(2,1)S(1)}, bf16[256,512]{1,0:T(8,128)(2,1)S(1)}, u32[]{:S(2)}, u32[]{:S(2)}) collective-permute-start(bf16[256,512]{1,0:T(8,128)(2,1)S(1)} %slice.43), channel_id=1, source_target_pairs={{0,16},{16,0},{1,17},{17,1},{2,18},{18,2},{3,19},{19,3},{4,20},{20... | collective-permute-start | bytes 786440 | tf_op jit(solution)/shard_map/ppermute | solution.py:46
  27.4 17.9 %collective-permute-start.3 = (bf16[384,512]{1,0:T(8,128)(2,1)S(1)}, bf16[384,512]{1,0:T(8,128)(2,1)S(1)}, u32[]{:S(2)}, u32[]{:S(2)}) collective-permute-start(bf16[384,512]{1,0:T(8,128)(2,1)S(1)} %collective-permute-done.refs_5_), channel_id=1, source_target_pairs={{0,4},{1,5},{2,6},{3,7},{4,8},{5,9},{6,10},{7,11},{8,12},{9,13},{1... | collective-permute-start | bytes 1179656 | tf_op jit(solution)/shard_map/ppermute | solution.py:37
  28.7 31.5 %copy-start.1 = (bf16[512,1024]{1,0:T(8,128)(2,1)S(1)}, bf16[512,1024]{1,0:T(8,128)(2,1)}, u32[]{:S(2)}) copy-start(bf16[512,1024]{1,0:T(8,128)(2,1)} %refs_4_.3) | copy-start | bytes 3145732
  36.8 14.0 %collective-permute-start.10 = (bf16[256,512]{1,0:T(8,128)(2,1)S(1)}, bf16[256,512]{1,0:T(8,128)(2,1)S(1)}, u32[]{:S(2)}, u32[]{:S(2)}) collective-permute-start(bf16[256,512]{1,0:T(8,128)(2,1)S(1)} %collective-permute-done.8.refs_7_), channel_id=1, source_target_pairs={{0,4},{1,5},{2,6},{3,7},{4,8},{5,9},{6,10},{7,11},{8,12},{9,13},{1... | collective-permute-start | bytes 786440 | tf_op jit(solution)/shard_map/ppermute | solution.py:37
  36.9 14.0 %collective-permute-start.18 = (bf16[256,512]{1,0:T(8,128)(2,1)S(1)}, bf16[256,512]{1,0:T(8,128)(2,1)S(1)}, u32[]{:S(2)}, u32[]{:S(2)}) collective-permute-start(bf16[256,512]{1,0:T(8,128)(2,1)S(1)} %collective-permute-done.8.refs_7_), channel_id=1, source_target_pairs={{0,16},{16,0},{1,17},{17,1},{2,18},{18,2},{3,19},{19,3},{4,20},{20... | collective-permute-start | bytes 786440 | tf_op jit(solution)/shard_map/ppermute | solution.py:46
  45.3 10.8 %collective-permute-start.5 = (bf16[384,512]{1,0:T(8,128)(2,1)S(1)}, bf16[384,512]{1,0:T(8,128)(2,1)S(1)}, u32[]{:S(2)}, u32[]{:S(2)}) collective-permute-start(bf16[384,512]{1,0:T(8,128)(2,1)S(1)} %collective-permute-done.3.refs_7_), channel_id=1, source_target_pairs={{0,4},{1,5},{2,6},{3,7},{4,8},{5,9},{6,10},{7,11},{8,12},{9,13},{1... | collective-permute-start | bytes 1179656 | tf_op jit(solution)/shard_map/ppermute | solution.py:37
  45.3 14.9 %collective-permute-start.13 = (bf16[160,2048]{1,0:T(8,128)(2,1)S(1)}, bf16[160,2048]{1,0:T(8,128)(2,1)S(1)}, u32[]{:S(2)}, u32[]{:S(2)}) collective-permute-start(bf16[160,2048]{1,0:T(8,128)(2,1)S(1)} %slice.56), channel_id=1, source_target_pairs={{0,1},{1,0},{2,3},{3,2},{4,5},{5,4},{6,7},{7,6},{8,9},{9,8},{10,11... | collective-permute-start | bytes 1966088 | tf_op jit(solution)/shard_map/ppermute | solution.py:42
  45.5 11.8 %collective-permute-start.14 = (bf16[256,512]{1,0:T(8,128)(2,1)S(1)}, bf16[256,512]{1,0:T(8,128)(2,1)S(1)}, u32[]{:S(2)}, u32[]{:S(2)}) collective-permute-start(bf16[256,512]{1,0:T(8,128)(2,1)S(1)} %slice.57), channel_id=1, source_target_pairs={{0,16},{16,0},{1,17},{17,1},{2,18},{18,2},{3,19},{19,3},{4,20},{20... | collective-permute-start | bytes 786440 | tf_op jit(solution)/shard_map/ppermute | solution.py:46
  50.9 9.4 %collective-permute-start.19 = (bf16[256,512]{1,0:T(8,128)(2,1)S(1)}, bf16[256,512]{1,0:T(8,128)(2,1)S(1)}, u32[]{:S(2)}, u32[]{:S(2)}) collective-permute-start(bf16[256,512]{1,0:T(8,128)(2,1)S(1)} %collective-permute-done.10.refs_9_), channel_id=1, source_target_pairs={{0,16},{16,0},{1,17},{17,1},{2,18},{18,2},{3,19},{19,3},{4,20},{20... | collective-permute-start | bytes 786440 | tf_op jit(solution)/shard_map/ppermute | solution.py:46
  56.1 10.8 %collective-permute-start.7 = (bf16[512,512]{1,0:T(8,128)(2,1)S(1)}, bf16[512,512]{1,0:T(8,128)(2,1)S(1)}, u32[]{:S(2)}, u32[]{:S(2)}) collective-permute-start(bf16[512,512]{1,0:T(8,128)(2,1)S(1)} %slice_dynamic-update-slice_fusion.refs_0_), channel_id=1, source_target_pairs={{0,2},{1,3},{2,0},{3,1},{4,6},{5,7},{6,4},{7,5},{8,10},{9,11},{10,... | collective-permute-start | bytes 1572872 | tf_op jit(solution)/shard_map/ppermute | solution.py:42
  57.2 8.2 %collective-permute-start.15 = (bf16[256,512]{1,0:T(8,128)(2,1)S(1)}, bf16[256,512]{1,0:T(8,128)(2,1)S(1)}, u32[]{:S(2)}, u32[]{:S(2)}) collective-permute-start(bf16[256,512]{1,0:T(8,128)(2,1)S(1)} %slice.58), channel_id=1, source_target_pairs={{0,16},{16,0},{1,17},{17,1},{2,18},{18,2},{3,19},{19,3},{4,20},{20... | collective-permute-start | bytes 786440 | tf_op jit(solution)/shard_map/ppermute | solution.py:46
  61.8 5.1 %collective-permute-start.20 = (bf16[320,512]{1,0:T(8,128)(2,1)S(1)}, bf16[320,512]{1,0:T(8,128)(2,1)S(1)}, u32[]{:S(2)}, u32[]{:S(2)}) collective-permute-start(bf16[320,512]{1,0:T(8,128)(2,1)S(1)} %get-tuple-element.58), channel_id=1, source_target_pairs={{0,1},{1,0},{2,3},{3,2},{4,5},{5,4},{6,7},{7,6},{8,9},{9,8},{10,11... | collective-permute-start | bytes 983048 | tf_op jit(solution)/shard_map/ppermute | solution.py:42
  65.8 3.4 %copy-start.3 = (bf16[4,40,4096]{2,1,0:T(8,128)(2,1)S(1)}, bf16[4,40,4096]{2,1,0:T(8,128)(2,1)}, u32[]{:S(2)}) copy-start(bf16[4,40,4096]{2,1,0:T(8,128)(2,1)} %q_ref.1) | copy-start | bytes 3932164
  65.8 3.4 %copy-start.4 = (s32[4]{0:T(128)S(1)}, s32[4]{0:T(128)}, u32[]{:S(2)}) copy-start(s32[4]{0:T(128)} %count_ref.3) | copy-start | bytes 52
  65.9 3.4 %copy-start.5 = (s32[64]{0:T(128)S(1)}, s32[64]{0:T(128)}, u32[]{:S(2)}) copy-start(s32[64]{0:T(128)} %home_ref.1) | copy-start | bytes 772
  65.9 2.4 %collective-permute-start.16 = (bf16[320,512]{1,0:T(8,128)(2,1)S(1)}, bf16[320,512]{1,0:T(8,128)(2,1)S(1)}, u32[]{:S(2)}, u32[]{:S(2)}) collective-permute-start(bf16[320,512]{1,0:T(8,128)(2,1)S(1)} %get-tuple-element.55), channel_id=1, source_target_pairs={{0,1},{1,0},{2,3},{3,2},{4,5},{5,4},{6,7},{7,6},{8,9},{9,8},{10,11... | collective-permute-start | bytes 983048 | tf_op jit(solution)/shard_map/ppermute | solution.py:42
  65.9 3.3 %collective-permute-start.11 = (bf16[512,512]{1,0:T(8,128)(2,1)S(1)}, bf16[512,512]{1,0:T(8,128)(2,1)S(1)}, u32[]{:S(2)}, u32[]{:S(2)}) collective-permute-start(bf16[512,512]{1,0:T(8,128)(2,1)S(1)} %slice_dynamic-update-slice_fusion.refs_0_), channel_id=1, source_target_pairs={{0,1},{1,0},{2,3},{3,2},{4,5},{5,4},{6,7},{7,6},{8,9},{9,8},{10,11... | collective-permute-start | bytes 1572872 | tf_op jit(solution)/shard_map/ppermute | solution.py:42
  66.9 2.3 %collective-permute-start.12 = (bf16[512,512]{1,0:T(8,128)(2,1)S(1)}, bf16[512,512]{1,0:T(8,128)(2,1)S(1)}, u32[]{:S(2)}, u32[]{:S(2)}) collective-permute-start(bf16[512,512]{1,0:T(8,128)(2,1)S(1)} %collective-permute-done.7.refs_1_), channel_id=1, source_target_pairs={{0,1},{1,0},{2,3},{3,2},{4,5},{5,4},{6,7},{7,6},{8,9},{9,8},{10,11... | collective-permute-start | bytes 1572872 | tf_op jit(solution)/shard_map/ppermute | solution.py:42
  67.0 7.7 %collective-permute-start.21 = (bf16[160,512]{1,0:T(8,128)(2,1)S(1)}, bf16[160,512]{1,0:T(8,128)(2,1)S(1)}, u32[]{:S(2)}, u32[]{:S(2)}) collective-permute-start(bf16[160,512]{1,0:T(8,128)(2,1)S(1)} %add_convert_fusion), channel_id=1, source_target_pairs={{0,2},{1,3},{2,0},{3,1},{4,6},{5,7},{6,4},{7,5},{8,10},{9,11},{10,... | collective-permute-start | bytes 491528 | tf_op jit(solution)/shard_map/ppermute | solution.py:42
  68.4 8.8 %collective-permute-start.17 = (bf16[160,512]{1,0:T(8,128)(2,1)S(1)}, bf16[160,512]{1,0:T(8,128)(2,1)S(1)}, u32[]{:S(2)}, u32[]{:S(2)}) collective-permute-start(bf16[160,512]{1,0:T(8,128)(2,1)S(1)} %add_convert_fusion.1), channel_id=1, source_target_pairs={{0,2},{1,3},{2,0},{3,1},{4,6},{5,7},{6,4},{7,5},{8,10},{9,11},{10,... | collective-permute-start | bytes 491528 | tf_op jit(solution)/shard_map/ppermute | solution.py:42

commit v5 on v4

--- a/solution.py
+++ b/solution.py
@@ -249,65 +249,95 @@
     return total.astype(jnp.bfloat16)
 
 
-def fresh_kernel(maxp, count_ref, q_ref, *refs):
-    terms, (query_pos_ref, part_ref, stat_ref, out_ref) = refs[:-4], refs[-4:]
-    r = pl.program_id(0)
-    half = len(terms) // 2
-    fresh = jnp.concatenate([added(*terms[:half]), added(*terms[half:])], axis=1)
-    fresh_keys, fresh_values = fresh[:, : fresh.shape[1] // 2], fresh[:, fresh.shape[1] // 2 :]
+def scores_kernel(maxp, count_ref, q_ref, *refs):
+    terms, (query_pos_ref, stat_ref, part_ref, weight_ref, base_ref) = refs[:-5], refs[-5:]
+    count = count_ref[pl.program_id(0)]
+    fresh_keys = added(*terms)
     rows = fresh_keys.shape[0]
     per_pass = rows // maxp
     slot = lax.broadcasted_iota(jnp.int32, (rows, HEAD_SIZE), 0) // per_pass
-    live = slot < count_ref[r]
     across = jnp.broadcast_to(query_pos_ref[0, :, :HEAD_SIZE], (HEAD_SIZE, HEAD_SIZE))
-    key_pos = jnp.where(live, across.T[:rows], NEVER)[:, :1]
+    key_pos = jnp.where(slot < count, across.T[:rows], NEVER)[:, :1]
     bias = jnp.where(key_pos <= query_pos_ref[0], 0.0, HIDDEN)
+    query = lax.broadcasted_iota(jnp.int32, query_pos_ref.shape[1:], 1)
+    live = query % rows // per_pass < count
     heads = [slice(g * HEAD_SIZE, (g + 1) * HEAD_SIZE) for g in range(KEY_VALUE_HEADS)]
     scores = [against(fresh_keys[:, head], q_ref[0, g], ((1,), (1,))) for g, head in enumerate(heads)]
-    weights, factors = [], []
     for g, s in enumerate(scores):
         s = s * EXP2_SCALE + bias
         top1 = stat_ref[0, g, 0:1]
         top = jnp.maximum(top1, jnp.max(s, axis=0, keepdims=True))
         e = jnp.exp2(s - top)
         keep = jnp.exp2(top1 - top)
-        total = stat_ref[0, g, 1:2] * keep + jnp.sum(e, axis=0, keepdims=True)
-        weights.append(e.astype(jnp.bfloat16))
-        factors.append((keep, 1.0 / total))
-    terms = [against(fresh_values[:, head], weights[g], ((0,), (0,))) for g, head in enumerate(heads)]
-    for g, (keep, inv) in enumerate(factors):
-        result = ((part_ref[0, g] * keep + terms[g]) * inv).T
-        for i in range(HEAD_GROUP):
-            at = (g * HEAD_GROUP + i) * HEAD_SIZE
-            one = result[i * rows : (i + 1) * rows]
-            out_ref[0, :, at : at + HEAD_SIZE] = jnp.where(live, one, 0.0).astype(jnp.bfloat16)
-
-
-def fresh_attention(maxp, count, queries, terms, query_pos, part, stat):
+        inv = 1.0 / (stat_ref[0, g, 1:2] * keep + jnp.sum(e, axis=0, keepdims=True))
+        inv = jnp.where(live, inv, 0.0)
+        weight_ref[0, g] = (e * inv).astype(jnp.bfloat16)
+        base_ref[0, g] = (part_ref[0, g] * (keep * inv)).T
+
+
+def fresh_scores(maxp, count, queries, terms, query_pos, part, stat):
     owned, heads, stacked, _ = queries.shape
     rows = terms[0].shape[1]
-    width = QUERY_HEADS * HEAD_SIZE
     return pl.pallas_call(
-        functools.partial(fresh_kernel, maxp),
-        out_shape=jax.ShapeDtypeStruct((owned, rows, width), jnp.bfloat16),
+        functools.partial(scores_kernel, maxp),
+        out_shape=[
+            jax.ShapeDtypeStruct((owned, heads, rows, stacked), jnp.bfloat16),
+            jax.ShapeDtypeStruct((owned, heads, stacked, HEAD_SIZE), jnp.float32),
+        ],
         grid=(owned,),
         in_specs=[
             smem(),
             by_request(heads, stacked, HEAD_SIZE),
             *[by_request(*t.shape[1:]) for t in terms],
             by_request(1, stacked),
+            by_request(heads, 2, stacked),
             by_request(heads, HEAD_SIZE, stacked),
-            by_request(heads, 2, stacked),
+        ],
+        out_specs=[by_request(heads, rows, stacked), by_request(heads, stacked, HEAD_SIZE)],
+        compiler_params=params(),
+        cost_estimate=pl.CostEstimate(
+            flops=2 * queries.size * rows,
+            bytes_accessed=8 * part.size,
+            transcendentals=owned * heads * stacked * rows,
+        ),
+        name="fresh_scores",
+    )(count, queries, *terms, query_pos, stat, part)
+
+
+def values_kernel(*refs):
+    terms, (weight_ref, base_ref, out_ref) = refs[:-3], refs[-3:]
+    fresh_values = added(*terms)
+    rows = fresh_values.shape[0]
+    heads = [slice(g * HEAD_SIZE, (g + 1) * HEAD_SIZE) for g in range(KEY_VALUE_HEADS)]
+    sums = [against(weight_ref[0, g], fresh_values[:, head], ((0,), (0,))) for g, head in enumerate(heads)]
+    for g, fresh in enumerate(sums):
+        result = base_ref[0, g] + fresh
+        for i in range(HEAD_GROUP):
+            at = (g * HEAD_GROUP + i) * HEAD_SIZE
+            out_ref[0, :, at : at + HEAD_SIZE] = result[i * rows : (i + 1) * rows].astype(jnp.bfloat16)
+
+
+def fresh_attention(weights, terms, base):
+    owned, heads, rows, stacked = weights.shape
+    width = QUERY_HEADS * HEAD_SIZE
+    return pl.pallas_call(
+        values_kernel,
+        out_shape=jax.ShapeDtypeStruct((owned, rows, width), jnp.bfloat16),
+        grid=(owned,),
+        in_specs=[
+            *[by_request(*t.shape[1:]) for t in terms],
+            by_request(heads, rows, stacked),
+            by_request(heads, stacked, HEAD_SIZE),
         ],
         out_specs=by_request(rows, width),
         compiler_params=params(),
         cost_estimate=pl.CostEstimate(
-            flops=4 * queries.size * rows,
-            bytes_accessed=8 * queries.size,
-            transcendentals=owned * heads * stacked * rows,
+            flops=2 * owned * rows * width * rows,
+            bytes_accessed=4 * base.size + 2 * owned * rows * width,
+            transcendentals=0,
         ),
         name="fresh_attention",
-    )(count, queries, *terms, query_pos, part, stat)
+    )(*terms, weights, base)
 
 
 def query_positions(rows, plen):
@@ -341,14 +371,15 @@
     pages = store_pages.reshape(local * plen, 2, kvw)
     mine = [
         lax.dynamic_slice(kv_weight, (side * half, first), (half, columns))
-        for first, columns in ((0, split), (split, features - split))
+        for first, columns in ((split, features - split), (0, split))
     ]
     own = jnp.concatenate([pages[:, 0], pages[:, 1]], axis=0)
-    a0 = jnp.concatenate([mine[0], own], axis=0)
+    a0 = mine[0]
+    b0 = jnp.concatenate([mine[1], own], axis=0)
     a1 = send(a0, 1)
-    b1 = send(mine[1], 1)
-
-    steps = jnp.arange(2 * ring, dtype=jnp.int32) // 2
+    b1 = send(b0, 1)
+
+    steps = jnp.array([0, 0, 1, 1, 3, 3, 2, 2], jnp.int32)
     blocks = (z - steps) % ring
     halves = jnp.arange(2 * ring, dtype=jnp.int32) % 2
     halves = jnp.where(steps == 0, halves, halves ^ side)
@@ -360,35 +391,36 @@
     rank = (z - device // GROUP) % ring
     rel = (device % GROUP) ^ member
     place = ((rel % 2) * 2 + rel // 2) * ring + rank
-    acts = norm_rows(rows_in.reshape(count, width), norm_gain, after(offs, a0), half)
-    y_acts = flip(after(acts[1], b1), 2)
+    acts = norm_rows(rows_in.reshape(count, width), norm_gain, after(offs, b0), half)
+    y_acts = flip(after(acts[1], a1), 2)
     near_act = flip(acts[2], 1)
     a1, near_act, place, *small = together(a1, near_act, place, *small)
-    a2 = send(after(a1, b1), 1)
-    xa1 = swap(after(a1[:half], near_act))
-    b2 = send(after(b1, near_act), 1)
-    xb1 = swap(b1)
-    a3 = send(after(a2, xa1), 1)
-    xa2 = swap(after(a2[:half], xa1))
-    b3 = send(after(b2, xb1), 1)
-    xb2 = swap(after(b2, xb1))
+    b3 = send(after(b0, b1, a1), -1)
+    xb1 = swap(after(b1[:half], near_act))
+    a3 = send(after(a0, near_act, a1), -1)
+    xa1 = swap(a1)
+    b2 = send(after(b1, b3), 1)
+    xb3 = swap(after(b3[:half], xb1))
+    a2 = send(after(a1, xa1), 1)
+    xa3 = swap(after(a3, xa1))
     y_far = flip(y_acts[count:], 1)
-    xa3 = swap(after(a3[:half], xa2))
-    xb3 = swap(after(b3, xb2))
-    column = jnp.concatenate([own, a1[half:], a2[half:], a3[half:]], axis=0)
+    xb2 = swap(after(b2[:half], xb3))
+    xa2 = swap(after(a2, xa3))
+    column = jnp.concatenate([own, b1[half:], b2[half:], b3[half:]], axis=0)
     y_column = flip(after(column, y_acts), 2)
-    far = flip(after(column, b3), 1)
-    y_column_far = flip(y_column, 1)
+    far = flip(column, 1)
+    y_column_far = flip(after(y_column, xb2), 1)
     acts = [acts[0], near_act, y_acts, y_far]
 
     depths = (depth,) + (half,) * (2 * ring - 2)
     terms = []
-    begun = project(acts, 0, 0, [kv_weight, a1, xa1, a2, xa2, a3], depths[:-1], split, (), False)
-    keep, out = project(acts, width // GROUP - half, 0, [xa3], depths[-1:], split, begun)
+    begun = project(acts, 0, 0, [kv_weight, b1, xb1, b3, xb3, b2], depths[:-1], split, (), False)
+    keep, out = project(acts, width // GROUP - half, 0, [xb2], depths[-1:], split, begun)
     back = flip(out, 1)
     y_out = (keep[count:] + back[count:].astype(jnp.float32)).astype(jnp.bfloat16)
     terms += [keep, back, flip(y_out, 2)]
-    keep, out = project(acts, 0, split, [kv_weight, b1, xb1, b2, xb2, b3, xb3], depths, features - split)
+    begun = project(acts, 0, split, [kv_weight, a1, xa1, a3, xa3, a2], depths[:-1], features - split, (), False)
+    keep, out = project(acts, width // GROUP - half, 0, [xa2], depths[-1:], features - split, begun)
     back = flip(out, 1)
     y_out = (keep[count:] + back[count:].astype(jnp.float32)).astype(jnp.bfloat16)
     terms += [keep, back, flip(y_out, 2)]
@@ -469,7 +501,11 @@
         per_dev, maxp, plen, *pages, flat_rows, passage_count, queries, query_pos
     )
     terms = [t.reshape(-1, selected, t.shape[1]) for t in terms]
-    return fresh_attention(maxp, passage_count, stacked, terms, query_pos, part, stat)
+    half = len(terms) // 2
+    weights, base = fresh_scores(
+        maxp, passage_count, stacked, terms[:half], query_pos, part, stat
+    )
+    return fresh_attention(weights, terms[half:], base)
 
 
 def solution(mesh):

time: 81.1 us -> 77.2 us (0.952)
  waiting for transfers between devices: 38.5 us -> 30.9 us
  starting transfers between devices: 19.6 us -> 21.7 us
  Pallas kernels: 16.5 us -> 18 us
    ppermute x6, waiting for transfers between devices: 31.4 us -> 23.5 us  [send(): return lax.ppermute(x, 'store', pairs)]
    ppermute x6, starting transfers between devices: 5.4 us -> 8.12 us  [send(): return lax.ppermute(x, 'store', pairs)]
    ppermute x10, waiting for transfers between devices: 2.97 us -> 4.53 us  [flip(): return lax.ppermute(x, 'store', pairs)]
    ppermute x6, waiting for transfers between devices: 4.14 us -> 2.84 us  [swap(): return lax.ppermute(x, 'parts', [(0, 1), (1, 0)])]
    pallas_call x1 -> x2, Pallas kernels: 3.7 us -> 4.94 us  [the longest x1 2.59 us: fresh_scores(): pl.pallas_call(functools.partial(scores_kernel, maxp), out_shape=[jax.Sha...]
    pallas_call x3 -> x4, Pallas kernels: 3.3 us -> 3.45 us  [project(): pl.pallas_call(functools.partial(project_kernel, skip, shift, depths, len...]
    unnamed x21 -> x27, local copies, waits for them, and re-layouts: 2.72 us -> 2.73 us
  transfers between devices with their start and end apart: 22 -> 22, of which waited for: 10 -> 9; matrix products, arithmetic and copies ran while one was open for 4% -> 4% of each run, Pallas kernels for 16% -> 20%
where the time goes in v5:
time: 77.2 us; the launch traced here: 77 us
  waiting for transfers between devices  30.9 us (40%)
  starting transfers between devices  21.7 us (28%)
  Pallas kernels  18 us (23%)
  local copies, waits for them, and re-layouts  4.96 us (6%)
  other arithmetic  1.05 us (1%)
    ppermute x6, waiting for transfers between devices, send(): return lax.ppermute(x, 'store', pairs)  23.5 us
    ppermute x6, starting transfers between devices, swap(): return lax.ppermute(x, 'parts', [(0, 1), (1, 0)])  8.86 us
    ppermute x6, starting transfers between devices, send(): return lax.ppermute(x, 'store', pairs)  8.12 us
    pallas_call x1, Pallas kernels, cached_attention(): pl.pallas_call(functools.partial(cached_kernel, per_dev, maxp), out_shape...  5.55 us
    ppermute x10, starting transfers between devices, flip(): return lax.ppermute(x, 'store', pairs)  4.75 us
    ppermute x10, waiting for transfers between devices, flip(): return lax.ppermute(x, 'store', pairs)  4.53 us
    pallas_call x1, Pallas kernels, norm_rows(): pl.pallas_call(functools.partial(norm_kernel, chunk, chunks), out_shape=[...  4.08 us
    pallas_call x4, Pallas kernels, project(): pl.pallas_call(functools.partial(project_kernel, skip, shift, depths, len...  3.45 us
  transfers between devices with their start and end apart: 22, of which 9 were waited for; matrix products, arithmetic and copies ran while one was open for 4% of the time, Pallas kernels for 20%

profile of v5, /device:TPU:0, one launch (start us, length us, event | category | flops | bytes accessed | tf_op | source)
XLA Modules:
  0.0 77.0 jit_solution(9653848195862242789)
XLA Ops:
  0.0 1.1 %constant_dynamic-slice_fusion.3 = (bf16[256,512]{1,0:T(8,128)(2,1)S(1)}, bf16[256,512]{1,0:T(8,128)(2,1)S(1)}) fusion(bf16[512,1024]{1,0:T(8,128)(2,1)} %refs_4_.3, s32[]{:T(128)S(6)} %select_n.78), kind=kLoop, calls=%fused_computation.51 | loop fusion | bytes 1048580 | tf_op jit(solution)/shard_map/dynamic_slice | solution.py:373
  1.1 3.1 %collective-permute-start = (bf16[256,512]{1,0:T(8,128)(2,1)S(1)}, bf16[256,512]{1,0:T(8,128)(2,1)S(1)}, u32[]{:S(2)}, u32[]{:S(2)}) collective-permute-start(bf16[256,512]{1,0:T(8,128)(2,1)S(1)} %get-tuple-element.43), channel_id=1, source_target_pairs={{0,4},{1,5},{2,6},{3,7},{4,8},{5,9},{6,10},{7,11},{8,12},{9,13},{1... | collective-permute-start | bytes 786440 | tf_op jit(solution)/shard_map/ppermute | solution.py:37
  4.2 0.9 %copy.13 = bf16[4,16,2,512]{3,1,0,2:T(8,128)(2,1)S(1)} copy(bf16[4,16,2,512]{3,2,1,0:T(2,128)(2,1)} %param.14) | data formatting | bytes 262144 | tf_op args[4]
  5.3 0.8 %pad_maximum_fusion = bf16[384,512]{1,0:T(8,128)(2,1)} fusion(bf16[64,512]{1,0:T(8,128)(2,1)S(1)} %get-tuple-element.70, bf16[64,512]{1,0:T(8,128)(2,1)S(1)} %get-tuple-element.69, bf16[256,512]{1,0:T(8,128)(2,1)S(1)} %get-tuple-element.68), kind=kLoop, calls=%fused_computation | loop fusion | flops 1179648 | bytes 786432 | tf_op jit(solution)/shard_map/concatenate | solution.py:378
  6.2 1.7 %copy-done.2 = bf16[4,40,8192]{2,1,0:T(8,128)(2,1)S(1)} copy-done((bf16[4,40,8192]{2,1,0:T(8,128)(2,1)S(1)}, bf16[4,40,8192]{2,1,0:T(8,128)(2,1)}, u32[]{:S(2)}) %copy-start.2) | copy-done | bytes 2621464
  7.9 4.1 %norm.1 = (bf16[160,2048]{1,0:T(8,128)(2,1)S(1)}, bf16[2,160,2048]{2,1,0:T(8,128)(2,1)}, bf16[160,2048]{1,0:T(8,128)(2,1)}) custom-call(s32[32]{0:T(128)S(1)} %and_select_fusion.6.offs_ref, bf16[160,8192]{1,0:T(8,128)(2,1)S(1)} %bitcast.18, bf16[1,8192]{1,0:T(2,128)(2,1)S(1)} %reshape.95.gain_ref), custom_call_target="tpu_custom_call" | custom-call | flops 7864320 | bytes 5242880 | tf_op jit(solution)/shard_map/norm/pallas_call | solution.py:72
  12.0 0.5 collective-permute-done.refs_5_
  12.5 1.5 %collective-permute-start.2 = (bf16[320,2048]{1,0:T(8,128)(2,1)}, bf16[320,2048]{1,0:T(8,128)(2,1)S(1)}, u32[]{:S(2)}, u32[]{:S(2)}) collective-permute-start(bf16[320,2048]{1,0:T(8,128)(2,1)} %bitcast.5), channel_id=1, source_target_pairs={{0,2},{1,3},{2,0},{3,1},{4,6},{5,7},{6,4},{7,5},{8,10},{9,11},{10,... | collective-permute-start | bytes 3932168 | tf_op jit(solution)/shard_map/ppermute | solution.py:42
  14.1 1.1 %collective-permute-start.11 = (bf16[384,512]{1,0:T(8,128)(2,1)}, bf16[384,512]{1,0:T(8,128)(2,1)S(1)}, u32[]{:S(2)}, u32[]{:S(2)}) collective-permute-start(bf16[384,512]{1,0:T(8,128)(2,1)} %pad_maximum_fusion), channel_id=1, source_target_pairs={{0,4},{1,5},{2,6},{3,7},{4,8},{5,9},{6,10},{7,11},{8,12},{9,13},{1... | collective-permute-start | bytes 1179656 | tf_op jit(solution)/shard_map/ppermute | solution.py:37
  16.2 1.3 %collective-permute-done.1.refs_1_ = bf16[160,2048]{1,0:T(8,128)(2,1)S(1)} collective-permute-done((bf16[160,2048]{1,0:T(8,128)(2,1)}, bf16[160,2048]{1,0:T(8,128)(2,1)S(1)}, u32[]{:S(2)}, u32[]{:S(2)}) %collective-permute-start.1) | collective-permute-done | bytes 655392 | tf_op jit(solution)/shard_map/ppermute | solution.py:42
  17.5 8.4 %collective-permute-done.11.refs_5_ = bf16[384,512]{1,0:T(8,128)(2,1)S(1)} collective-permute-done((bf16[384,512]{1,0:T(8,128)(2,1)}, bf16[384,512]{1,0:T(8,128)(2,1)S(1)}, u32[]{:S(2)}, u32[]{:S(2)}) %collective-permute-start.11) | collective-permute-done | bytes 393248 | tf_op jit(solution)/shard_map/ppermute | solution.py:37
  25.9 0.6 collective-permute-start.12
  26.5 1.6 %collective-permute-start.16 = (bf16[256,512]{1,0:T(8,128)(2,1)S(1)}, bf16[256,512]{1,0:T(8,128)(2,1)S(1)}, u32[]{:S(2)}, u32[]{:S(2)}) collective-permute-start(bf16[256,512]{1,0:T(8,128)(2,1)S(1)} %slice.61), channel_id=1, source_target_pairs={{0,16},{16,0},{1,17},{17,1},{2,18},{18,2},{3,19},{19,3},{4,20},{20... | collective-permute-start | bytes 786440 | tf_op jit(solution)/shard_map/ppermute | solution.py:46
  28.1 0.5 collective-permute-start.4
  28.6 1.7 %collective-permute-start.5 = (bf16[256,512]{1,0:T(8,128)(2,1)}, bf16[256,512]{1,0:T(8,128)(2,1)S(1)}, u32[]{:S(2)}, u32[]{:S(2)}) collective-permute-start(bf16[256,512]{1,0:T(8,128)(2,1)} %copy-done.6), channel_id=1, source_target_pairs={{0,12},{1,13},{2,14},{3,15},{4,0},{5,1},{6,2},{7,3},{8,4},{9,5},{1... | collective-permute-start | bytes 786440 | tf_op jit(solution)/shard_map/ppermute | solution.py:37
  30.3 7.6 %collective-permute-done.12.refs_7_ = bf16[384,512]{1,0:T(8,128)(2,1)S(1)} collective-permute-done((bf16[384,512]{1,0:T(8,128)(2,1)}, bf16[384,512]{1,0:T(8,128)(2,1)S(1)}, u32[]{:S(2)}, u32[]{:S(2)}) %collective-permute-start.12) | collective-permute-done | bytes 393248 | tf_op jit(solution)/shard_map/ppermute | solution.py:37
  37.9 1.6 %collective-permute-start.17 = (bf16[256,512]{1,0:T(8,128)(2,1)S(1)}, bf16[256,512]{1,0:T(8,128)(2,1)S(1)}, u32[]{:S(2)}, u32[]{:S(2)}) collective-permute-start(bf16[256,512]{1,0:T(8,128)(2,1)S(1)} %slice.60), channel_id=1, source_target_pairs={{0,16},{16,0},{1,17},{17,1},{2,18},{18,2},{3,19},{19,3},{4,20},{20... | collective-permute-start | bytes 786440 | tf_op jit(solution)/shard_map/ppermute | solution.py:46
  39.5 3.2 %collective-permute-done.2.refs_2_ = bf16[320,2048]{1,0:T(8,128)(2,1)S(1)} collective-permute-done((bf16[320,2048]{1,0:T(8,128)(2,1)}, bf16[320,2048]{1,0:T(8,128)(2,1)S(1)}, u32[]{:S(2)}, u32[]{:S(2)}) %collective-permute-start.2) | collective-permute-done | bytes 1310752 | tf_op jit(solution)/shard_map/ppermute | solution.py:42
  42.9 1.4 %collective-permute-start.6 = (bf16[256,512]{1,0:T(8,128)(2,1)S(1)}, bf16[256,512]{1,0:T(8,128)(2,1)S(1)}, u32[]{:S(2)}, u32[]{:S(2)}) collective-permute-start(bf16[256,512]{1,0:T(8,128)(2,1)S(1)} %collective-permute-done.5.refs_7_), channel_id=1, source_target_pairs={{0,16},{16,0},{1,17},{17,1},{2,18},{18,2},{3,19},{19,3},{4,20},{20... | collective-permute-start | bytes 786440 | tf_op jit(solution)/shard_map/ppermute | solution.py:46
  44.3 1.6 %collective-permute-start.7 = (bf16[256,512]{1,0:T(8,128)(2,1)S(1)}, bf16[256,512]{1,0:T(8,128)(2,1)S(1)}, u32[]{:S(2)}, u32[]{:S(2)}) collective-permute-start(bf16[256,512]{1,0:T(8,128)(2,1)S(1)} %collective-permute-done.refs_5_), channel_id=1, source_target_pairs={{0,4},{1,5},{2,6},{3,7},{4,8},{5,9},{6,10},{7,11},{8,12},{9,13},{1... | collective-permute-start | bytes 786440 | tf_op jit(solution)/shard_map/ppermute | solution.py:37
  45.9 4.7 %collective-permute-done.13.refs_9_ = bf16[384,512]{1,0:T(8,128)(2,1)S(1)} collective-permute-done((bf16[384,512]{1,0:T(8,128)(2,1)S(1)}, bf16[384,512]{1,0:T(8,128)(2,1)S(1)}, u32[]{:S(2)}, u32[]{:S(2)}) %collective-permute-start.13) | collective-permute-done | bytes 393248 | tf_op jit(solution)/shard_map/ppermute | solution.py:37
  50.6 2.3 %collective-permute-start.18 = (bf16[256,512]{1,0:T(8,128)(2,1)S(1)}, bf16[256,512]{1,0:T(8,128)(2,1)S(1)}, u32[]{:S(2)}, u32[]{:S(2)}) collective-permute-start(bf16[256,512]{1,0:T(8,128)(2,1)S(1)} %slice.59), channel_id=1, source_target_pairs={{0,16},{16,0},{1,17},{17,1},{2,18},{18,2},{3,19},{19,3},{4,20},{20... | collective-permute-start | bytes 786440 | tf_op jit(solution)/shard_map/ppermute | solution.py:46
  53.1 2.3 %collective-permute-done.7.refs_9_ = bf16[256,512]{1,0:T(8,128)(2,1)S(1)} collective-permute-done((bf16[256,512]{1,0:T(8,128)(2,1)S(1)}, bf16[256,512]{1,0:T(8,128)(2,1)S(1)}, u32[]{:S(2)}, u32[]{:S(2)}) %collective-permute-start.7) | collective-permute-done | bytes 262176 | tf_op jit(solution)/shard_map/ppermute | solution.py:37
  55.4 1.5 %collective-permute-start.8 = (bf16[256,512]{1,0:T(8,128)(2,1)S(1)}, bf16[256,512]{1,0:T(8,128)(2,1)S(1)}, u32[]{:S(2)}, u32[]{:S(2)}) collective-permute-start(bf16[256,512]{1,0:T(8,128)(2,1)S(1)} %collective-permute-done.7.refs_9_), channel_id=1, source_target_pairs={{0,16},{16,0},{1,17},{17,1},{2,18},{18,2},{3,19},{19,3},{4,20},{20... | collective-permute-start | bytes 786440 | tf_op jit(solution)/shard_map/ppermute | solution.py:46
  56.9 1.4 %project.6.refs_4_ = f32[640,512]{1,0:T(8,128)S(1)} custom-call(bf16[160,2048]{1,0:T(8,128)(2,1)S(1)} %get-tuple-element.37.refs_0_, bf16[160,2048]{1,0:T(8,128)(2,1)S(1)} %collective-permute-done.1.refs_1_, bf16[320,2048]{1,0:T(8,128)(2,1)S(1)} %collective-permute-done.2.refs_2_, bf16[160,2048]{1,0:T(8,128)(2,1)S(1)} %collective-permute-done.3.refs_3_, ...), custom_call_target="tpu_custom_call" | custom-call | flops 1174405120 | bytes 6094848 | tf_op jit(solution)/shard_map/project/pallas_call | solution.py:124
  58.7 1.4 %project.4.refs_4_ = f32[640,512]{1,0:T(8,128)S(1)} custom-call(bf16[160,2048]{1,0:T(8,128)(2,1)S(1)} %get-tuple-element.37.refs_0_, bf16[160,2048]{1,0:T(8,128)(2,1)S(1)} %collective-permute-done.1.refs_1_, bf16[320,2048]{1,0:T(8,128)(2,1)S(1)} %collective-permute-done.2.refs_2_, bf16[160,2048]{1,0:T(8,128)(2,1)S(1)} %collective-permute-done.3.refs_3_, ...), custom_call_target="tpu_custom_call" | custom-call | flops 1174405120 | bytes 6094848 | tf_op jit(solution)/shard_map/project/pallas_call | solution.py:124
  60.1 2.8 %collective-permute-done.8.refs_5_ = bf16[256,512]{1,0:T(8,128)(2,1)S(1)} collective-permute-done((bf16[256,512]{1,0:T(8,128)(2,1)S(1)}, bf16[256,512]{1,0:T(8,128)(2,1)S(1)}, u32[]{:S(2)}, u32[]{:S(2)}) %collective-permute-start.8) | collective-permute-done | bytes 262176 | tf_op jit(solution)/shard_map/ppermute | solution.py:46
  64.0 1.4 %collective-permute-start.21 = (bf16[160,512]{1,0:T(8,128)(2,1)S(1)}, bf16[160,512]{1,0:T(8,128)(2,1)S(1)}, u32[]{:S(2)}, u32[]{:S(2)}) collective-permute-start(bf16[160,512]{1,0:T(8,128)(2,1)S(1)} %add_convert_fusion), channel_id=1, source_target_pairs={{0,2},{1,3},{2,0},{3,1},{4,6},{5,7},{6,4},{7,5},{8,10},{9,11},{10,... | collective-permute-start | bytes 491528 | tf_op jit(solution)/shard_map/ppermute | solution.py:42
  65.4 1.0 %collective-permute-start.10 = (bf16[160,512]{1,0:T(8,128)(2,1)S(1)}, bf16[160,512]{1,0:T(8,128)(2,1)S(1)}, u32[]{:S(2)}, u32[]{:S(2)}) collective-permute-start(bf16[160,512]{1,0:T(8,128)(2,1)S(1)} %add_convert_fusion.1), channel_id=1, source_target_pairs={{0,2},{1,3},{2,0},{3,1},{4,6},{5,7},{6,4},{7,5},{8,10},{9,11},{10,... | collective-permute-start | bytes 491528 | tf_op jit(solution)/shard_map/ppermute | solution.py:42
  66.5 5.5 %cached_attention.1 = (f32[4,4,128,320]{3,2,1,0:T(8,128)S(1)}, f32[4,4,2,320]{3,2,1,0:T(2,128)S(1)}, bf16[4,4,320,128]{3,2,1,0:T(8,128)(2,1)S(1)}) custom-call(s32[16]{0:T(128)S(1)} %fusion.place_ref, s32[64]{0:T(128)S(1)} %copy-done.5, s32[80]{0:T(128)S(1)} %reshape.96.ids_ref, s32[160]{0:T(256)S(1)} %reshape.97.rows_ref, s32[4]{0:T(128)S(1)} %copy-done.4, ...), custom_call_target="tpu_custom_call" | custom-call | flops 838860800 | bytes 4718592 | tf_op jit(solution)/shard_map/cached_attention/pallas_call | solution.py:210
  72.1 2.6 %fresh_scores.1 = (bf16[4,4,40,320]{3,2,1,0:T(8,128)(2,1)S(1)}, f32[4,4,320,128]{3,2,1,0:T(8,128)S(1)}) custom-call(s32[4]{0:T(128)S(1)} %copy-done.4, bf16[4,4,320,128]{3,2,1,0:T(8,128)(2,1)S(1)} %get-tuple-element.60.q_ref, f32[8,40,512]{2,1,0:T(8,128)S(1)} %bitcast.19, bf16[8,40,512]{2,1,0:T(8,128)(2,1)S(1)} %bitcast.21, ...), custom_call_target="tpu_custom_call" | custom-call | flops 52428800 | bytes 5242880 | tf_op jit(solution)/shard_map/fresh_scores/pallas_call | solution.py:281
  74.7 2.3 %fresh_attention.1 = bf16[4,40,4096]{2,1,0:T(8,128)(2,1)} custom-call(f32[8,40,512]{2,1,0:T(8,128)S(1)} %bitcast.20, bf16[8,40,512]{2,1,0:T(8,128)(2,1)S(1)} %bitcast.22, bf16[4,40,512]{2,1,0:T(8,128)(2,1)S(1)} %bitcast.23, bf16[4,4,40,320]{3,2,1,0:T(8,128)(2,1)S(1)} %get-tuple-element.65.refs_3_, f32[4,4,320,128]{3,2,1,0:T(8,128)S(1)} %get-tuple-element.66.refs_4_), custom_call_target="tpu_custom_call" | custom-call | flops 52428800 | bytes 3932160 | tf_op jit(solution)/shard_map/fresh_attention/pallas_call | solution.py:323
  (75 shorter events, 3.2 us)
Async XLA Ops:
  0.0 15.3 %copy-start = (s32[64,20,2]{0,2,1:T(2,128)S(1)}, s32[64,20,2]{0,2,1:T(2,128)}, u32[]{:S(2)}) copy-start(s32[64,20,2]{0,2,1:T(2,128)} %param.18) | copy-start | bytes 30724
  0.0 5.2 %copy-start.9 = (pred[8]{0:T(512)(128)(4,1)S(1)}, pred[8]{0:T(512)(128)(4,1)}, u32[]{:S(2)}) copy-start(pred[8]{0:T(512)(128)(4,1)} %constant.138) | copy-start | bytes 28
  0.0 5.2 %copy-start.10 = (s32[8]{0:T(128)S(1)}, s32[8]{0:T(128)}, u32[]{:S(2)}) copy-start(s32[8]{0:T(128)} %constant.137) | copy-start | bytes 100
  0.0 6.1 %copy-start.7 = (bf16[8192]{0:T(1024)(128)(2,1)S(1)}, bf16[8192]{0:T(1024)(128)(2,1)}, u32[]{:S(2)}) copy-start(bf16[8192]{0:T(1024)(128)(2,1)} %param.11) | copy-start | bytes 49156
  1.1 10.9 %copy-start.6 = (bf16[256,512]{1,0:T(8,128)(2,1)}, bf16[256,512]{1,0:T(8,128)(2,1)S(1)}, u32[]{:S(2)}) copy-start(bf16[256,512]{1,0:T(8,128)(2,1)S(1)} %get-tuple-element.43) | copy-start | bytes 786436
  1.1 11.4 %collective-permute-start = (bf16[256,512]{1,0:T(8,128)(2,1)S(1)}, bf16[256,512]{1,0:T(8,128)(2,1)S(1)}, u32[]{:S(2)}, u32[]{:S(2)}) collective-permute-start(bf16[256,512]{1,0:T(8,128)(2,1)S(1)} %get-tuple-element.43), channel_id=1, source_target_pairs={{0,4},{1,5},{2,6},{3,7},{4,8},{5,9},{6,10},{7,11},{8,12},{9,13},{1... | collective-permute-start | bytes 786440 | tf_op jit(solution)/shard_map/ppermute | solution.py:37
  7.9 7.3 %copy-start.8 = (s32[64,20]{0,1:T(8,128)S(1)}, s32[64,20]{0,1:T(8,128)}, u32[]{:S(2)}) copy-start(s32[64,20]{0,1:T(8,128)} %param.16) | copy-start | bytes 15364
  12.5 30.2 %collective-permute-start.2 = (bf16[320,2048]{1,0:T(8,128)(2,1)}, bf16[320,2048]{1,0:T(8,128)(2,1)S(1)}, u32[]{:S(2)}, u32[]{:S(2)}) collective-permute-start(bf16[320,2048]{1,0:T(8,128)(2,1)} %bitcast.5), channel_id=1, source_target_pairs={{0,2},{1,3},{2,0},{3,1},{4,6},{5,7},{6,4},{7,5},{8,10},{9,11},{10,... | collective-permute-start | bytes 3932168 | tf_op jit(solution)/shard_map/ppermute | solution.py:42
  14.1 11.8 %collective-permute-start.11 = (bf16[384,512]{1,0:T(8,128)(2,1)}, bf16[384,512]{1,0:T(8,128)(2,1)S(1)}, u32[]{:S(2)}, u32[]{:S(2)}) collective-permute-start(bf16[384,512]{1,0:T(8,128)(2,1)} %pad_maximum_fusion), channel_id=1, source_target_pairs={{0,4},{1,5},{2,6},{3,7},{4,8},{5,9},{6,10},{7,11},{8,12},{9,13},{1... | collective-permute-start | bytes 1179656 | tf_op jit(solution)/shard_map/ppermute | solution.py:37
  15.2 2.3 %collective-permute-start.1 = (bf16[160,2048]{1,0:T(8,128)(2,1)}, bf16[160,2048]{1,0:T(8,128)(2,1)S(1)}, u32[]{:S(2)}, u32[]{:S(2)}) collective-permute-start(bf16[160,2048]{1,0:T(8,128)(2,1)} %get-tuple-element.38), channel_id=1, source_target_pairs={{0,1},{1,0},{2,3},{3,2},{4,5},{5,4},{6,7},{7,6},{8,9},{9,8},{10,11... | collective-permute-start | bytes 1966088 | tf_op jit(solution)/shard_map/ppermute | solution.py:42
  25.9 11.9 %collective-permute-start.12 = (bf16[384,512]{1,0:T(8,128)(2,1)}, bf16[384,512]{1,0:T(8,128)(2,1)S(1)}, u32[]{:S(2)}, u32[]{:S(2)}) collective-permute-start(bf16[384,512]{1,0:T(8,128)(2,1)} %pad_maximum_fusion), channel_id=1, source_target_pairs={{0,12},{1,13},{2,14},{3,15},{4,0},{5,1},{6,2},{7,3},{8,4},{9,5},{1... | collective-permute-start | bytes 1179656 | tf_op jit(solution)/shard_map/ppermute | solution.py:37
  26.5 11.4 %collective-permute-start.16 = (bf16[256,512]{1,0:T(8,128)(2,1)S(1)}, bf16[256,512]{1,0:T(8,128)(2,1)S(1)}, u32[]{:S(2)}, u32[]{:S(2)}) collective-permute-start(bf16[256,512]{1,0:T(8,128)(2,1)S(1)} %slice.61), channel_id=1, source_target_pairs={{0,16},{16,0},{1,17},{17,1},{2,18},{18,2},{3,19},{19,3},{4,20},{20... | collective-permute-start | bytes 786440 | tf_op jit(solution)/shard_map/ppermute | solution.py:46
  28.1 14.8 %collective-permute-start.4 = (bf16[256,512]{1,0:T(8,128)(2,1)S(1)}, bf16[256,512]{1,0:T(8,128)(2,1)S(1)}, u32[]{:S(2)}, u32[]{:S(2)}) collective-permute-start(bf16[256,512]{1,0:T(8,128)(2,1)S(1)} %collective-permute-done.refs_5_), channel_id=1, source_target_pairs={{0,16},{16,0},{1,17},{17,1},{2,18},{18,2},{3,19},{19,3},{4,20},{20... | collective-permute-start | bytes 786440 | tf_op jit(solution)/shard_map/ppermute | solution.py:46
  28.6 14.3 %collective-permute-start.5 = (bf16[256,512]{1,0:T(8,128)(2,1)}, bf16[256,512]{1,0:T(8,128)(2,1)S(1)}, u32[]{:S(2)}, u32[]{:S(2)}) collective-permute-start(bf16[256,512]{1,0:T(8,128)(2,1)} %copy-done.6), channel_id=1, source_target_pairs={{0,12},{1,13},{2,14},{3,15},{4,0},{5,1},{6,2},{7,3},{8,4},{9,5},{1... | collective-permute-start | bytes 786440 | tf_op jit(solution)/shard_map/ppermute | solution.py:37
  37.9 12.7 %collective-permute-start.17 = (bf16[256,512]{1,0:T(8,128)(2,1)S(1)}, bf16[256,512]{1,0:T(8,128)(2,1)S(1)}, u32[]{:S(2)}, u32[]{:S(2)}) collective-permute-start(bf16[256,512]{1,0:T(8,128)(2,1)S(1)} %slice.60), channel_id=1, source_target_pairs={{0,16},{16,0},{1,17},{17,1},{2,18},{18,2},{3,19},{19,3},{4,20},{20... | collective-permute-start | bytes 786440 | tf_op jit(solution)/shard_map/ppermute | solution.py:46
  39.4 11.1 %collective-permute-start.13 = (bf16[384,512]{1,0:T(8,128)(2,1)S(1)}, bf16[384,512]{1,0:T(8,128)(2,1)S(1)}, u32[]{:S(2)}, u32[]{:S(2)}) collective-permute-start(bf16[384,512]{1,0:T(8,128)(2,1)S(1)} %collective-permute-done.11.refs_5_), channel_id=1, source_target_pairs={{0,4},{1,5},{2,6},{3,7},{4,8},{5,9},{6,10},{7,11},{8,12},{9,13},{1... | collective-permute-start | bytes 1179656 | tf_op jit(solution)/shard_map/ppermute | solution.py:37
  39.5 17.3 %copy-start.1 = (bf16[512,1024]{1,0:T(8,128)(2,1)S(1)}, bf16[512,1024]{1,0:T(8,128)(2,1)}, u32[]{:S(2)}) copy-start(bf16[512,1024]{1,0:T(8,128)(2,1)} %refs_4_.3) | copy-start | bytes 3145732
  42.8 14.1 %collective-permute-start.3 = (bf16[160,2048]{1,0:T(8,128)(2,1)S(1)}, bf16[160,2048]{1,0:T(8,128)(2,1)S(1)}, u32[]{:S(2)}, u32[]{:S(2)}) collective-permute-start(bf16[160,2048]{1,0:T(8,128)(2,1)S(1)} %slice.54), channel_id=1, source_target_pairs={{0,1},{1,0},{2,3},{3,2},{4,5},{5,4},{6,7},{7,6},{8,9},{9,8},{10,11... | collective-permute-start | bytes 1966088 | tf_op jit(solution)/shard_map/ppermute | solution.py:42
  42.9 10.2 %collective-permute-start.6 = (bf16[256,512]{1,0:T(8,128)(2,1)S(1)}, bf16[256,512]{1,0:T(8,128)(2,1)S(1)}, u32[]{:S(2)}, u32[]{:S(2)}) collective-permute-start(bf16[256,512]{1,0:T(8,128)(2,1)S(1)} %collective-permute-done.5.refs_7_), channel_id=1, source_target_pairs={{0,16},{16,0},{1,17},{17,1},{2,18},{18,2},{3,19},{19,3},{4,20},{20... | collective-permute-start | bytes 786440 | tf_op jit(solution)/shard_map/ppermute | solution.py:46
  44.3 11.1 %collective-permute-start.7 = (bf16[256,512]{1,0:T(8,128)(2,1)S(1)}, bf16[256,512]{1,0:T(8,128)(2,1)S(1)}, u32[]{:S(2)}, u32[]{:S(2)}) collective-permute-start(bf16[256,512]{1,0:T(8,128)(2,1)S(1)} %collective-permute-done.refs_5_), channel_id=1, source_target_pairs={{0,4},{1,5},{2,6},{3,7},{4,8},{5,9},{6,10},{7,11},{8,12},{9,13},{1... | collective-permute-start | bytes 786440 | tf_op jit(solution)/shard_map/ppermute | solution.py:37
  50.6 7.7 %collective-permute-start.18 = (bf16[256,512]{1,0:T(8,128)(2,1)S(1)}, bf16[256,512]{1,0:T(8,128)(2,1)S(1)}, u32[]{:S(2)}, u32[]{:S(2)}) collective-permute-start(bf16[256,512]{1,0:T(8,128)(2,1)S(1)} %slice.59), channel_id=1, source_target_pairs={{0,16},{16,0},{1,17},{17,1},{2,18},{18,2},{3,19},{19,3},{4,20},{20... | collective-permute-start | bytes 786440 | tf_op jit(solution)/shard_map/ppermute | solution.py:46
  53.0 10.9 %collective-permute-start.14 = (bf16[512,512]{1,0:T(8,128)(2,1)S(1)}, bf16[512,512]{1,0:T(8,128)(2,1)S(1)}, u32[]{:S(2)}, u32[]{:S(2)}) collective-permute-start(bf16[512,512]{1,0:T(8,128)(2,1)S(1)} %slice_dynamic-update-slice_fusion.refs_0_), channel_id=1, source_target_pairs={{0,2},{1,3},{2,0},{3,1},{4,6},{5,7},{6,4},{7,5},{8,10},{9,11},{10,... | collective-permute-start | bytes 1572872 | tf_op jit(solution)/shard_map/ppermute | solution.py:42
  55.4 7.5 %collective-permute-start.8 = (bf16[256,512]{1,0:T(8,128)(2,1)S(1)}, bf16[256,512]{1,0:T(8,128)(2,1)S(1)}, u32[]{:S(2)}, u32[]{:S(2)}) collective-permute-start(bf16[256,512]{1,0:T(8,128)(2,1)S(1)} %collective-permute-done.7.refs_9_), channel_id=1, source_target_pairs={{0,16},{16,0},{1,17},{17,1},{2,18},{18,2},{3,19},{19,3},{4,20},{20... | collective-permute-start | bytes 786440 | tf_op jit(solution)/shard_map/ppermute | solution.py:46
  58.6 5.3 %collective-permute-start.20 = (bf16[320,512]{1,0:T(8,128)(2,1)S(1)}, bf16[320,512]{1,0:T(8,128)(2,1)S(1)}, u32[]{:S(2)}, u32[]{:S(2)}) collective-permute-start(bf16[320,512]{1,0:T(8,128)(2,1)S(1)} %get-tuple-element.62), channel_id=1, source_target_pairs={{0,1},{1,0},{2,3},{3,2},{4,5},{5,4},{6,7},{7,6},{8,9},{9,8},{10,11... | collective-permute-start | bytes 983048 | tf_op jit(solution)/shard_map/ppermute | solution.py:42
  63.3 3.2 %copy-start.3 = (bf16[4,40,4096]{2,1,0:T(8,128)(2,1)S(1)}, bf16[4,40,4096]{2,1,0:T(8,128)(2,1)}, u32[]{:S(2)}) copy-start(bf16[4,40,4096]{2,1,0:T(8,128)(2,1)} %q_ref.1) | copy-start | bytes 3932164
  63.3 3.2 %copy-start.4 = (s32[4]{0:T(128)S(1)}, s32[4]{0:T(128)}, u32[]{:S(2)}) copy-start(s32[4]{0:T(128)} %count_ref.3) | copy-start | bytes 52
  63.3 3.2 %copy-start.5 = (s32[64]{0:T(128)S(1)}, s32[64]{0:T(128)}, u32[]{:S(2)}) copy-start(s32[64]{0:T(128)} %home_ref.1) | copy-start | bytes 772
  63.3 2.1 %collective-permute-start.9 = (bf16[320,512]{1,0:T(8,128)(2,1)S(1)}, bf16[320,512]{1,0:T(8,128)(2,1)S(1)}, u32[]{:S(2)}, u32[]{:S(2)}) collective-permute-start(bf16[320,512]{1,0:T(8,128)(2,1)S(1)} %get-tuple-element.48), channel_id=1, source_target_pairs={{0,1},{1,0},{2,3},{3,2},{4,5},{5,4},{6,7},{7,6},{8,9},{9,8},{10,11... | collective-permute-start | bytes 983048 | tf_op jit(solution)/shard_map/ppermute | solution.py:42
  63.4 3.0 %collective-permute-start.15 = (bf16[512,512]{1,0:T(8,128)(2,1)S(1)}, bf16[512,512]{1,0:T(8,128)(2,1)S(1)}, u32[]{:S(2)}, u32[]{:S(2)}) collective-permute-start(bf16[512,512]{1,0:T(8,128)(2,1)S(1)} %slice_dynamic-update-slice_fusion.refs_0_), channel_id=1, source_target_pairs={{0,1},{1,0},{2,3},{3,2},{4,5},{5,4},{6,7},{7,6},{8,9},{9,8},{10,11... | collective-permute-start | bytes 1572872 | tf_op jit(solution)/shard_map/ppermute | solution.py:42
  63.9 2.6 %collective-permute-start.19 = (bf16[512,512]{1,0:T(8,128)(2,1)S(1)}, bf16[512,512]{1,0:T(8,128)(2,1)S(1)}, u32[]{:S(2)}, u32[]{:S(2)}) collective-permute-start(bf16[512,512]{1,0:T(8,128)(2,1)S(1)} %collective-permute-done.14.refs_1_), channel_id=1, source_target_pairs={{0,1},{1,0},{2,3},{3,2},{4,5},{5,4},{6,7},{7,6},{8,9},{9,8},{10,11... | collective-permute-start | bytes 1572872 | tf_op jit(solution)/shard_map/ppermute | solution.py:42
  64.0 8.1 %collective-permute-start.21 = (bf16[160,512]{1,0:T(8,128)(2,1)S(1)}, bf16[160,512]{1,0:T(8,128)(2,1)S(1)}, u32[]{:S(2)}, u32[]{:S(2)}) collective-permute-start(bf16[160,512]{1,0:T(8,128)(2,1)S(1)} %add_convert_fusion), channel_id=1, source_target_pairs={{0,2},{1,3},{2,0},{3,1},{4,6},{5,7},{6,4},{7,5},{8,10},{9,11},{10,... | collective-permute-start | bytes 491528 | tf_op jit(solution)/shard_map/ppermute | solution.py:42
  65.4 9.2 %collective-permute-start.10 = (bf16[160,512]{1,0:T(8,128)(2,1)S(1)}, bf16[160,512]{1,0:T(8,128)(2,1)S(1)}, u32[]{:S(2)}, u32[]{:S(2)}) collective-permute-start(bf16[160,512]{1,0:T(8,128)(2,1)S(1)} %add_convert_fusion.1), channel_id=1, source_target_pairs={{0,2},{1,3},{2,0},{3,1},{4,6},{5,7},{6,4},{7,5},{8,10},{9,11},{10,... | collective-permute-start | bytes 491528 | tf_op jit(solution)/shard_map/ppermute | solution.py:42
  (1 other events, 1.7 us)
